TPU v7x, 256 devices: a whole 4x4x8 slice. The times are simulated.
256 devices in a mesh: row: 32 (over z_hi, x, core), feat: 8 (over z_lo, y).
Axes of the slice: x: 4, y: 4, z: 8 (z_hi: 4, z_lo: 2; z = z_hi * 2 + z_lo), core: 2. Of those that a mesh axis runs over, the one named last changes fastest.
Arguments:
- features: bfloat16 [131072, 8192], P('row', 'feat'), may hold values from -6 to 6
- coef: bfloat16 [8192], P('feat'), may hold values from -0.0625 to 0.0625
- labels: int32 [131072], P('row'), may hold values 0 or 1
- sign_bits: int32 [131072], P('row'), may hold values 0 or 1
- samples: int32 [32, 4096], P('row'), may hold values from 0 to 4095
Outputs:
- gradient: float32 [8192], P('feat')
- sketch: bfloat16 [4096, 8192], P('row', 'feat')
- gram: float32 [4096, 4096], P('row', 'feat')
Inputs may be any that keep to these rules, and one draw needn't show every extreme that they name: `samples`: row index inside the block.
All inputs are finite; a program needn't handle non-finite values. No bound on the sum of `labels` or of `sign_bits` on one device may be relied on, other than what follows from the above.
Results may differ from a plain program's by a relative error of at most 0.017.
Values may be sent and summed in bfloat16 or wider, within the bound.
No kernel may reach another device: no remote copies, remote signals or barrier semaphores. Data moves between devices by JAX's collectives and lax.ppermute only.
A program may use at most 128 MiB of HBM per device.

v0:
```python
import jax
import jax.numpy as jnp
from jax import lax
from jax.sharding import PartitionSpec as P


def sylvester(hadamard_order):
    positions = jnp.arange(hadamard_order, dtype=jnp.int32)
    bit_correlation = positions[:, None] & positions[None, :]
    parity_count = jnp.zeros_like(bit_correlation)
    for bit_pos in range(max(hadamard_order.bit_length() - 1, 0)):
        parity_count = parity_count + (bit_correlation >> bit_pos & 1)
    return (1 - 2 * (parity_count % 2)).astype(jnp.float32)


def per_device(features, coef, labels, sign_bits, samples):
    rows_here = features.shape[0]
    feat_here = features.shape[1]
    row_count = lax.axis_size("row")
    total_rows = rows_here * row_count
    all_features = feat_here * lax.axis_size("feat")
    root_total = jnp.sqrt(jnp.float32(total_rows))
    partial_value = jnp.dot(features, coef, preferred_element_type=jnp.float32)
    margins = lax.psum(partial_value, "feat")
    probability = jax.nn.sigmoid(margins)
    row_scale = jnp.sqrt(probability * (1.0 - probability))
    residual_full = probability - labels.astype(jnp.float32)
    residual = residual_full.astype(jnp.bfloat16)
    grad_term = jnp.dot(residual, features, preferred_element_type=jnp.float32)
    gradient = lax.psum(grad_term, "row") / root_total
    signs = 2.0 * sign_bits.astype(jnp.float32) - 1.0
    weighted = ((signs * row_scale)[:, None] * features).astype(jnp.bfloat16)
    sample_rows = samples[0]
    big_order = 32
    small_order = rows_here // big_order
    high_table = sylvester(big_order).astype(jnp.bfloat16)
    low_table = sylvester(small_order)
    shaped = weighted.reshape(big_order, small_order, feat_here)
    first_pass = jnp.einsum("ij,jkf->ikf", high_table, shaped, preferred_element_type=jnp.float32)
    second_pass = jnp.einsum("kl,ilf->ikf", low_table, first_pass, precision=lax.Precision.HIGHEST)
    transformed = second_pass.reshape(rows_here, feat_here)
    picked = jnp.take(transformed, sample_rows, axis=0).astype(jnp.bfloat16)
    summed = lax.psum_scatter(
        picked.astype(jnp.float32).astype(jnp.bfloat16), "row", scatter_dimension=0, tiled=True
    ).astype(jnp.float32)
    sketch = (summed / root_total).astype(jnp.bfloat16)
    gram_part = lax.dot_general(
        sketch,
        lax.all_gather(sketch, "row", axis=0, tiled=True),
        (((1,), (1,)), ((), ())),
        preferred_element_type=jnp.float32,
    )
    gram_block = (
        lax.psum_scatter(
            gram_part.astype(jnp.bfloat16), "feat", scatter_dimension=1, tiled=True
        ).astype(jnp.float32)
        / all_features
    )
    return (gradient, sketch, gram_block)


def solution(mesh):
    in_specs = (P("row", "feat"), P("feat"), P("row"), P("row"), P("row", None))
    out_specs = (P("feat"), P("row", "feat"), P("row", "feat"))
    return jax.shard_map(
        per_device, mesh=mesh, in_specs=in_specs, out_specs=out_specs, check_vma=False
    )
```

profile of v0, /device:TPU:8, one launch (start us, length us, event | category | flops | bytes accessed | tf_op | source)
XLA Modules:
  0.0 438.1 jit_solution(1388875084883146769)
XLA Ops:
  7.2 0.0 copy-start.1
  7.2 0.0 copy-start.2
  7.2 0.0 reduce-scatter.3.cloned.1.call-start
  7.2 0.7 reshape.57
  7.9 5.6 %fusion.46 = f32[1,4096]{1,0:T(1,128)S(1)} fusion(bf16[4096,1024]{1,0:T(8,128)(2,1)} %param.5, bf16[1024,1]{0,1:T(2,128)(2,1)S(1)} %reshape.57), kind=kOutput, calls=%fused_computation.64 | convolution fusion | flops 8388608 | bytes 8407040 | tf_op jit(solution)/shard_map/dot_general | solution.py:23
  13.6 30.9 %psum.14 = f32[4096]{0:T(1024)S(1)} all-reduce(f32[4096]{0:T(1024)S(1)} %bitcast.24), channel_id=1, replica_groups=mesh['row'=32,'feat'=8] {'feat'}, use_global_device_ids=true, to_apply=%region_0.0 | all-reduce | flops 4096 | bytes 32768 | tf_op jit(solution)/shard_map/psum | solution.py:24
  44.5 0.0 copy-done.1
  44.5 0.0 copy-done.2
  44.5 8.0 %multiply_convert_fusion = bf16[4096,1024]{1,0:T(8,128)(2,1)} fusion(bf16[4096,1024]{1,0:T(8,128)(2,1)} %param.5, f32[4096]{0:T(1024)S(1)} %get-tuple-element.3), kind=kLoop, calls=%fused_computation.4 | loop fusion | flops 12582912 | bytes 16793600 | tf_op jit(solution)/shard_map/convert_element_type | solution.py:32
  52.5 20.8 %fusion.2 = f32[32,128,1024]{2,0,1:T(8,128)} fusion(bf16[32,128,1024]{2,1,0:T(8,128)(2,1)} %bitcast.23), kind=kOutput, calls=%fused_computation.5 | convolution fusion | flops 268466176 | bytes 25165824 | tf_op jit(solution)/shard_map/ij,jkf->ikf/dot_general | solution.py:39
  73.3 0.0 copy-start
  73.3 32.0 %fusion = bf16[32,1024,128]{1,2,0:T(8,128)(2,1)} fusion(f32[32,128,1024]{2,0,1:T(8,128)} %fusion.2), kind=kOutput, calls=%fused_computation.1 | convolution fusion | flops 6443024384 | bytes 25165824 | tf_op jit(solution)/shard_map/kl,ilf->ikf/dot_general | solution.py:40
  105.3 0.0 copy-done
  105.3 25.3 %gather_fusion = bf16[4096,1024]{1,0:T(8,128)(2,1)} fusion(bf16[4096,1024]{1,0:T(8,128)(2,1)} %bitcast.22, s32[4096]{0:T(1024)S(1)} %broadcast_clamp_fusion), kind=kCustom, calls=%fused_computation | custom fusion | bytes 16793600 | tf_op jit(solution)/shard_map/jit(_take)/gather | solution.py:42
  130.7 7.6 %select_convert_fusion = bf16[4096,1024]{1,0:T(8,128)(2,1)} fusion(bf16[4096,1024]{1,0:T(8,128)(2,1)} %gather_fusion, pred[4096]{0:T(1024)(128)(4,1)S(1)} %compare_and_fusion), kind=kLoop, calls=%fused_computation.3 | loop fusion | flops 4194304 | bytes 16781312 | tf_op jit(solution)/shard_map/convert_element_type | solution.py:42
  138.2 0.0 reduce-scatter.3.cloned.1.call-update
  138.3 0.0 all-gather.2.cloned.1.call-start
  138.3 124.8 %reduce-scatter.3.cloned.1.call-done = bf16[128,1024]{1,0:T(8,128)(2,1)} async-done(((bf16[4096,1024]{1,0:T(8,128)(2,1)}), bf16[128,1024]{1,0:T(8,128)(2,1)}) %reduce-scatter.3.cloned.1.call-update) | async-done | bytes 262160 | tf_op jit(solution)/shard_map/reduce_scatter | solution.py:43
  263.1 1.7 multiply_convert_fusion.1
  264.8 0.0 all-gather.2.cloned.1.call-update
  264.8 0.0 reduce-scatter.5.cloned.1.call-start
  264.9 77.3 %all-gather.2.cloned.1.call-done = bf16[4096,1024]{1,0:T(8,128)(2,1)} async-done(((bf16[128,1024]{1,0:T(8,128)(2,1)}), bf16[4096,1024]{1,0:T(8,128)(2,1)}) %all-gather.2.cloned.1.call-update) | async-done | bytes 8388624 | tf_op jit(solution)/shard_map/all_gather | solution.py:49
  342.2 7.4 %convolution_convert_fusion = bf16[128,4096]{1,0:T(8,128)(2,1)} fusion(bf16[128,1024]{1,0:T(8,128)(2,1)} %multiply_convert_fusion.1, bf16[4096,1024]{1,0:T(8,128)(2,1)} %all-gather.2.cloned.1.call-done), kind=kOutput, calls=%fused_computation.7 | convolution fusion | flops 1074266112 | bytes 9699328 | tf_op jit(solution)/shard_map/dot_general | solution.py:47
  349.6 0.0 reduce-scatter.5.cloned.1.call-update
  349.6 4.6 %fusion.47 = f32[1,1024]{1,0:T(1,128)S(1)} fusion(bf16[4096,1]{0,1:T(2,128)(2,1)S(1)} %reshape.59, bf16[4096,1024]{1,0:T(8,128)(2,1)} %param.5), kind=kOutput, calls=%fused_computation.65 | convolution fusion | flops 8388608 | bytes 8400896 | tf_op jit(solution)/shard_map/dot_general | solution.py:29
  354.2 75.1 %psum.15 = f32[1024]{0:T(1024)S(1)} all-reduce(f32[1024]{0:T(1024)S(1)} %bitcast.27), channel_id=1, replica_groups=mesh['row'=32,'feat'=8] {'row'}, use_global_device_ids=true, to_apply=%region_1.0 | all-reduce | flops 1024 | bytes 8192 | tf_op jit(solution)/shard_map/psum | solution.py:30
  429.3 0.6 broadcast_multiply_fusion
  429.9 0.0 reduce-scatter.5.cloned.1.call-done
  429.9 1.6 convert_multiply_fusion
  (5 shorter events, 0.1 us)
Async XLA Ops:
  7.2 37.3 %copy-start.1 = (s32[4096]{0:T(1024)S(1)}, s32[4096]{0:T(1024)}, u32[]{:S(2)}) copy-start(s32[4096]{0:T(1024)} %param.8) | copy-start | bytes 49156
  7.2 37.3 %copy-start.2 = (s32[4096]{0:T(1024)S(1)}, s32[4096]{0:T(1024)}, u32[]{:S(2)}) copy-start(s32[4096]{0:T(1024)} %param.7) | copy-start | bytes 49156
  7.2 255.9 %reduce-scatter.3.cloned.1.call-start = ((), (), s32[]{:S(2)}) async-start(), calls=%async_computation.2 | async-start | bytes 8650752 | tf_op jit(solution)/shard_map/reduce_scatter | solution.py:43
  73.3 32.0 %copy-start = (s32[1,4096]{1,0:T(1,128)S(1)}, s32[1,4096]{1,0:T(1,128)}, u32[]{:S(2)}) copy-start(s32[1,4096]{1,0:T(1,128)} %param.9) | copy-start | bytes 49156
  138.3 203.9 %all-gather.2.cloned.1.call-start = ((), (), s32[]{:S(2)}) async-start(), calls=%async_computation.3 | async-start | bytes 8650752 | tf_op jit(solution)/shard_map/all_gather | solution.py:49
  264.8 165.1 %reduce-scatter.5.cloned.1.call-start = ((), (), s32[]{:S(2)}) async-start(), calls=%async_computation.4 | async-start | bytes 1179648 | tf_op jit(solution)/shard_map/reduce_scatter | solution.py:54
Sparse Core Ops, SparseCore 0:
  138.4 124.6 reduce-scatter.2
  266.6 75.5 all-gather.1
  349.7 37.7 reduce-scatter.4
where the time goes:
time: 439 us; the launch traced here: 438 us
  waiting for transfers between devices  202 us (46%)
  blocking collectives  106 us (24%)
  matrix products  70.4 us (16%)
  local copies, waits for them, and re-layouts  26.1 us (6%)
  other arithmetic  19.6 us (4%)
  between operations  13.8 us (3%)
    reduce_scatter x1, waiting for transfers between devices, per_device(): lax.psum_scatter(picked.astype(jnp.float32).astype(jnp.bfloat16), 'row',...  125 us
    all_gather x1, waiting for transfers between devices, per_device(): lax.all_gather(sketch, 'row', axis=0, tiled=True)  77.3 us
    psum x1, blocking collectives, per_device(): gradient = lax.psum(grad_term, 'row') / root_total  75.1 us
    dot_general x1, matrix products, per_device(): jnp.einsum('kl,ilf->ikf', low_table, first_pass, precision=lax.Precision....  32 us
    psum x1, blocking collectives, per_device(): margins = lax.psum(partial_value, 'feat')  30.9 us
    gather x1, local copies, waits for them, and re-layouts, per_device(): picked = jnp.take(transformed, sample_rows, axis=0).astype(jnp.bfloat16)  25.3 us
    dot_general x1, matrix products, per_device(): jnp.einsum('ij,jkf->ikf', high_table, shaped, preferred_element_type=jnp....  20.8 us
  transfers between devices with their start and end apart: 3, of which 2 were waited for; matrix products, arithmetic and copies ran while one was open for 1% of the time, Pallas kernels for 0%

commit v1 on v0

v1 whole, which is shorter than its diff:
```python
import functools

import jax
import jax.numpy as jnp
from jax import lax
from jax.experimental import pallas as pl
from jax.experimental.pallas import tpu as pltpu
from jax.sharding import Mesh, PartitionSpec as P

ROWS = 4096
COLS = 1024
LOW = 256
HIGH = ROWS // LOW
GROUP = 256
LANE_TILES = COLS // 128
HALF_PAIRS = 32
UNROLL = 16
EXTRA = 16


def ring(axis_name, value, shift):
    size = lax.axis_size(axis_name)
    return lax.ppermute(value, axis_name, [(i, (i + shift) % size) for i in range(size)])


def sketch_kernel(spots, own_ref, other_ref, factor_ref, residual_ref, *refs):
    outs, (gradient, table_rows, own_pass, other_pass, transformed) = refs[:8], refs[8:]
    step = pl.program_id(0)
    last = COLS // GROUP

    def multiply(block, high):
        source, target = ((own_ref, own_pass), (other_ref, other_pass))[block]
        product = jnp.dot(
            table_rows[block * HIGH + high],
            source[pl.ds(pl.multiple_of(high * LOW, LOW), LOW), :],
            preferred_element_type=jnp.float32,
        )
        target[high] = product[:LOW]
        gradient[step] += product[LOW : LOW + 8]

    def combine(block, group, tile_row):
        source = (own_pass, other_pass)[block]
        for lane_tile in range(GROUP // 128):
            rows = pl.ds(pl.multiple_of(tile_row * 8, 8), 8)
            values = [source[high, rows, lane_tile * 128 : (lane_tile + 1) * 128] for high in range(HIGH)]
            stride = 1
            while stride < HIGH:
                for high in range(HIGH):
                    if not high & stride:
                        a, b = values[high], values[high + stride]
                        values[high], values[high + stride] = a + b, a - b
                stride *= 2
            place = tile_row * 64 + (group * (GROUP // 128) + lane_tile) * 8
            for high in range(HIGH):
                transformed[block, pl.ds(pl.multiple_of(high * (LOW * 8) + place, 8), 8), :] = values[high]

    def run(multiplied, combined):
        def body(high, carry):
            if multiplied is not None:
                multiply(multiplied, high)
            if combined is not None:
                for tile in range(LOW // 8 // HIGH):
                    combine(*combined, high * (LOW // 8 // HIGH) + tile)
            return carry

        lax.fori_loop(0, HIGH, body, 0, unroll=UNROLL)

    @pl.when(step == 0)
    def _():
        both = lax.broadcasted_iota(jnp.int32, (LOW, LOW), 0) & lax.broadcasted_iota(jnp.int32, (LOW, LOW), 1)
        for bit in (4, 2, 1):
            both = both ^ (both >> bit)
        signs = (1 - 2 * (both & 1)).astype(jnp.float32)
        for part in range(2 * HIGH):
            table_rows[part, :LOW] = (signs * factor_ref[part : part + 1, :]).astype(jnp.bfloat16)
            table_rows[part, LOW:] = jnp.broadcast_to(residual_ref[part : part + 1, :], (EXTRA, LOW)).astype(
                jnp.bfloat16
            )
        gradient[...] = jnp.zeros_like(gradient)
        run(0, None)

    @pl.when((step > 0) & (step < last))
    def _():
        run(0, (1, step - 1))

    @pl.when(step < last)
    def _():
        run(1, (0, step))

    @pl.when(step == last)
    def _():
        run(None, (1, last - 1))
        start = 0
        for out in outs:
            pairs = out.shape[0]

            def pick(pair, carry, out=out, start=start):
                rows = []
                for member in range(2):
                    at = start + pair * 2 + member
                    rows.append(
                        transformed[0, pl.ds(spots[at], 8, 8), :]
                        + transformed[1, pl.ds(spots[2 * 1024 + at], 8, 8), :]
                    )
                out[pair] = jnp.concatenate(rows, axis=0).astype(jnp.bfloat16)
                return carry

            lax.fori_loop(0, pairs, pick, 0, unroll=16)
            start += 2 * pairs


def sketch_pieces(spots, own, other, factors, residuals):
    pairs = [4 * HALF_PAIRS] * 8
    last = COLS // GROUP - 1
    return pl.pallas_call(
        sketch_kernel,
        grid_spec=pltpu.PrefetchScalarGridSpec(
            num_scalar_prefetch=1,
            grid=(last + 2,),
            in_specs=[
                pl.BlockSpec((ROWS, GROUP), lambda i, s: (0, jnp.minimum(i, last))),
                pl.BlockSpec((ROWS, GROUP), lambda i, s: (0, jnp.minimum(i, last))),
                pl.BlockSpec((2 * HIGH, LOW), lambda i, s: (0, 0)),
                pl.BlockSpec((2 * HIGH, LOW), lambda i, s: (0, 0)),
            ],
            out_specs=[pl.BlockSpec((n, 16, 128), lambda i, s: (0, 0, 0)) for n in pairs]
            + [pl.BlockSpec((COLS // GROUP, 8, GROUP), lambda i, s: (0, 0, 0))],
            scratch_shapes=[
                pltpu.VMEM((2 * HIGH, LOW + EXTRA, LOW), jnp.bfloat16),
                pltpu.VMEM((HIGH, LOW, GROUP), jnp.float32),
                pltpu.VMEM((HIGH, LOW, GROUP), jnp.float32),
                pltpu.VMEM((2, ROWS * LANE_TILES + 64, 128), jnp.float32),
            ],
        ),
        out_shape=[jax.ShapeDtypeStruct((n, 16, 128), jnp.bfloat16) for n in pairs]
        + [jax.ShapeDtypeStruct((COLS // GROUP, 8, GROUP), jnp.float32)],
        compiler_params=pltpu.CompilerParams(vmem_limit_bytes=62 * 1024 * 1024),
        cost_estimate=pl.CostEstimate(flops=4_400_000_000, bytes_accessed=22_000_000, transcendentals=0),
        name="hadamard_pick",
    )(spots, own, other, factors, residuals)


def gram_kernel(place, left_ref, own_ref, other_ref, out, tile):
    my_zh, my_x, my_c = [place[i] for i in range(3)]
    for which, source in enumerate((own_ref, other_ref)):
        core = my_c if which == 0 else 1 - my_c
        for shift in range(4):
            product = lax.dot_general(
                left_ref[...],
                source[shift * 128 : (shift + 1) * 128, :],
                (((1,), (1,)), ((), ())),
                preferred_element_type=jnp.float32,
            )
            for row in range(4):
                tile[lax.rem(my_zh + shift, 4) * 2 + core, lax.rem(my_x + row, 4)] = product[
                    row * 128 : (row + 1) * 128
                ].astype(jnp.bfloat16)
    for target in range(8):
        zh, x_low = target // 2, target % 2
        for i in range(2):
            x_high = lax.rem(my_x + i, 2)
            for core in range(2):
                out[target, i, :, core * 128 : (core + 1) * 128] = tile[zh * 2 + core, x_high * 2 + x_low]


def gram_pieces(place, left, right):
    vmem = pl.BlockSpec(memory_space=pltpu.VMEM)
    return pl.pallas_call(
        gram_kernel,
        in_specs=[pl.BlockSpec(memory_space=pltpu.SMEM)] + [vmem] * 3,
        out_specs=vmem,
        out_shape=jax.ShapeDtypeStruct((8, 2, 128, 256), jnp.bfloat16),
        scratch_shapes=[pltpu.VMEM((8, 4, 128, 128), jnp.bfloat16)],
        compiler_params=pltpu.CompilerParams(vmem_limit_bytes=32 * 1024 * 1024),
        cost_estimate=pl.CostEstimate(flops=1_100_000_000, bytes_accessed=4_000_000, transcendentals=0),
        name="gram_tile",
    )(place, *left, *right)


def add_up(*terms):
    total = terms[0].astype(jnp.float32)
    for term in terms[1:]:
        total = total + term.astype(jnp.float32)
    return total


def narrow(*terms):
    return add_up(*terms).astype(jnp.bfloat16)


def per_device(features, coef, labels, sign_bits, samples):
    my_zh, my_x, my_c = lax.axis_index("zh"), lax.axis_index("x"), lax.axis_index("c")
    my_zl, my_y = lax.axis_index("zl"), lax.axis_index("y")
    root_total = jnp.sqrt(jnp.float32(ROWS * 32))

    other_features = ring("c", features, 1)
    integers = jnp.concatenate([samples, sign_bits[None], labels[None]], axis=0)
    other_integers = ring("c", integers, 1)

    partial_value = jnp.dot(features, coef, preferred_element_type=jnp.float32).reshape(32, 128)
    everyone = lax.all_to_all(jnp.broadcast_to(partial_value, (16, 32, 128)), ("c", "zl", "y"), 0, 0).reshape(2, 8, 32, 128)
    by_core = [sum(everyone[core, k] for k in range(8)) for core in range(2)]
    margins = jnp.where(my_c == 0, by_core[0], by_core[1])
    other_margins = jnp.where(my_c == 0, by_core[1], by_core[0])

    def row_terms(value, bits, targets):
        probability = jax.nn.sigmoid(value)
        scale = jnp.sqrt(probability * (1.0 - probability))
        factor = (2.0 * bits.reshape(32, 128).astype(jnp.float32) - 1.0) * scale
        return factor.reshape(HIGH, LOW), (probability - targets.reshape(32, 128).astype(jnp.float32)).reshape(HIGH, LOW)

    terms = [row_terms(margins, sign_bits, labels), row_terms(other_margins, other_integers[1], other_integers[2])]
    factors, residuals = (jnp.concatenate(pair, axis=0) for pair in zip(*terms))

    picks = jnp.stack([integers[0], other_integers[0]]).reshape(2, 4, 4, 2, 2, 64)
    picks = lax.dynamic_index_in_dim(picks, my_c, axis=3, keepdims=False)
    picks = jnp.roll(picks, (-my_zh, -my_x), axis=(1, 2))
    picks = picks.transpose(0, 2, 3, 1, 4).reshape(4096)
    spots = (picks >> 3) * 64 + (picks & 7)

    *pieces, gradient = sketch_pieces(spots, features, other_features, factors, residuals)
    gradient = gradient[:, 0, :].reshape(8, 128)
    piece = [[pieces[2 * b + h].reshape(4, HALF_PAIRS, 16, 128) for h in range(2)] for b in range(4)]

    def swap_add(axis_name, flip, value):
        return value + lax.ppermute(value, axis_name, [(i, i ^ flip) for i in range(4)])

    far_0, far_1 = ring("x", piece[2][0], 1), ring("x", piece[2][1], -1)
    after_1, before_0 = ring("x", piece[1][1], 1), ring("x", piece[3][0], -1)
    gradient = swap_add("zh", 1, gradient)
    far_0, far_1, gradient = lax.optimization_barrier((far_0, far_1, gradient))
    after_0 = ring("x", narrow(piece[1][0], far_0), 1)
    before_1 = ring("x", narrow(piece[3][1], far_1), -1)
    gradient = swap_add("zh", 2, gradient)
    after_1, before_0, gradient = lax.optimization_barrier((after_1, before_0, gradient))
    wide = [
        [add_up(piece[0][0][a], after_0[a], before_0[a]), add_up(piece[0][1][a], after_1[a], before_1[a])]
        for a in range(4)
    ]
    short = [[half.astype(jnp.bfloat16) for half in pair] for pair in wide]
    from_last = ring("zh", jnp.stack([short[2][0], short[1][1]]), 1)
    from_next = ring("zh", jnp.stack([short[2][1], short[3][0]]), -1)
    gradient = swap_add("x", 1, gradient)
    from_last, from_next, gradient = lax.optimization_barrier((from_last, from_next, gradient))
    end_0 = ring("zh", narrow(short[1][0], from_last[0]), 1)
    end_1 = ring("zh", narrow(short[3][1], from_next[0]), -1)
    gradient = swap_add("x", 2, gradient)
    end_0, end_1, gradient = lax.optimization_barrier((end_0, end_1, gradient))
    summed = [add_up(wide[0][0], from_next[1], end_0), add_up(wide[0][1], from_last[1], end_1)]
    summed = jnp.concatenate(summed, axis=0).reshape(128, COLS)
    sketch = (summed / root_total).astype(jnp.bfloat16)

    zh_last, zh_next = ring("zh", sketch, 1), ring("zh", sketch, -1)
    x_next, x_far, x_last = (ring("x", sketch, shift) for shift in (-1, 2, 1))
    zh_last, zh_next, x_last, x_next, x_far = lax.optimization_barrier((zh_last, zh_next, x_last, x_next, x_far))
    zh_far_0, zh_far_1 = ring("zh", zh_last[:64], 1), ring("zh", zh_next[64:], -1)
    left = [jnp.concatenate([sketch, x_next, x_far, x_last], axis=0)]
    own_rows = jnp.concatenate([sketch, zh_next, zh_far_0, zh_far_1, zh_last], axis=0)
    right = [own_rows, ring("c", own_rows, 1)]
    place = jnp.stack([my_zh, my_x, my_c]).astype(jnp.int32)
    tiles = gram_pieces(place, left, right)
    parts = lax.all_to_all(tiles, ("zl", "y"), 0, 0)
    over_feat = add_up(*(parts[k] for k in range(8))).astype(jnp.bfloat16)

    def deliver(i):
        moves = []
        for x in range(4):
            for y in range(4):
                to_x, to_y = ((x & 1) ^ i) * 2 + (y & 1), (y & 2) | (x >> 1)
                moves.append((x * 4 + y, to_x * 4 + to_y))
        return lax.ppermute(over_feat[i], ("x", "y"), moves).astype(jnp.float32)

    same, turned = deliver(0), deliver(1)
    upper = my_x >= 2
    gram = jnp.concatenate([jnp.where(upper, turned, same), jnp.where(upper, same, turned)], axis=1)
    gram = gram / jnp.float32(8 * COLS)
    gradient = gradient.reshape(COLS)
    return (gradient / root_total, sketch, gram)


def solution(mesh):
    fine = Mesh(mesh.devices.reshape(4, 4, 2, 2, 4), ("zh", "x", "c", "zl", "y"))
    row, feat = ("zh", "x", "c"), ("zl", "y")
    return jax.shard_map(
        per_device,
        mesh=fine,
        in_specs=(P(row, feat), P(feat), P(row), P(row), P(row, None)),
        out_specs=(P(feat), P(row, feat), P(row, feat)),
        check_vma=False,
    )
```

time: 439 us -> 179 us (0.41)
  waiting for transfers between devices: 202 us -> 72.9 us
  blocking collectives: 106 us -> 0 us
  matrix products: 70.4 us -> 5.68 us
  starting transfers between devices: 0.12 us -> 63.5 us
  Pallas kernels: 0 us -> 25.3 us
  local copies, waits for them, and re-layouts: 26.1 us -> 3.32 us
  other arithmetic: 19.6 us -> 6.46 us
  between operations: 13.8 us -> 1.1 us
    reduce_scatter x2 -> x0, waiting for transfers between devices: 125 us -> none  [the longest x1 125 us: per_device(): lax.psum_scatter(picked.astype(jnp.float32).astype(jnp.bfloat16), 'row',...]
    psum x2 -> x0, blocking collectives: 106 us -> none  [the longest x1 75.1 us: per_device(): gradient = lax.psum(grad_term, 'row') / root_total]
    all_gather x1 -> x0, waiting for transfers between devices: 77.3 us -> none  [per_device(): lax.all_gather(sketch, 'row', axis=0, tiled=True)]
    dot_general x5 -> x1, matrix products: 70.4 us -> 5.68 us  [per_device(): jnp.dot(features, coef, preferred_element_type=jnp.float32).reshape(32, 128)]
    ppermute x0 -> x26, waiting for transfers between devices: none -> 53.6 us  [the longest x20 41 us: ring(): lax.ppermute(value, axis_name, [(i, (i + shift) % size) for i in range(si...]
    ppermute x0 -> x26, starting transfers between devices: none -> 51.4 us  [the longest x20 33 us: ring(): lax.ppermute(value, axis_name, [(i, (i + shift) % size) for i in range(si...]
    gather x1 -> x0, local copies, waits for them, and re-layouts: 25.3 us -> none  [per_device(): picked = jnp.take(transformed, sample_rows, axis=0).astype(jnp.bfloat16)]
    pallas_call x0 -> x2, Pallas kernels: none -> 25.3 us  [the longest x1 21.3 us: sketch_pieces(): pl.pallas_call(sketch_kernel, grid_spec=pltpu.PrefetchScalarGridSpec(num_...]
  transfers between devices with their start and end apart: 3 -> 28, of which waited for: 2 -> 20; matrix products, arithmetic and copies ran while one was open for 1% -> 8% of each run, Pallas kernels for 0% -> 0%
where the time goes in v1:
time: 179 us; the launch traced here: 178 us
  waiting for transfers between devices  72.9 us (41%)
  starting transfers between devices  63.5 us (35%)
  Pallas kernels  25.3 us (14%)
  other arithmetic  6.46 us (4%)
  matrix products  5.68 us (3%)
  local copies, waits for them, and re-layouts  3.32 us (2%)
    ppermute x20, waiting for transfers between devices, ring(): lax.ppermute(value, axis_name, [(i, (i + shift) % size) for i in range(si...  41 us
    ppermute x20, starting transfers between devices, ring(): lax.ppermute(value, axis_name, [(i, (i + shift) % size) for i in range(si...  33 us
    pallas_call x1, Pallas kernels, sketch_pieces(): pl.pallas_call(sketch_kernel, grid_spec=pltpu.PrefetchScalarGridSpec(num_...  21.3 us
    all_to_all x1, waiting for transfers between devices, per_device(): parts = lax.all_to_all(tiles, ('zl', 'y'), 0, 0)  14.1 us
    ppermute x4, starting transfers between devices, swap_add(): lax.ppermute(value, axis_name, [(i, i ^ flip) for i in range(4)])  13.3 us
    ppermute x4, waiting for transfers between devices, swap_add(): lax.ppermute(value, axis_name, [(i, i ^ flip) for i in range(4)])  6.54 us
    all_to_all x1, starting transfers between devices, per_device(): lax.all_to_all(jnp.broadcast_to(partial_value, (16, 32, 128)), ('c', 'zl'...  6.29 us
    ppermute x2, waiting for transfers between devices, deliver(): return lax.ppermute(over_feat[i], ('x', 'y'), moves).astype(jnp.float32)  6.04 us
  transfers between devices with their start and end apart: 28, of which 20 were waited for; matrix products, arithmetic and copies ran while one was open for 8% of the time, Pallas kernels for 0%

profile of v1, /device:TPU:8, one launch (start us, length us, event | category | flops | bytes accessed | tf_op | source)
XLA Modules:
  0.0 178.3 jit_solution(13343688757312344321)
XLA Ops:
  0.7 0.8 pad_add_fusion
  2.8 5.7 %fusion.29 = f32[1,4096]{1,0:T(1,128)S(1)} fusion(bf16[4096,1024]{1,0:T(8,128)(2,1)} %own_ref.1, bf16[1024,1]{0,1:T(2,128)(2,1)S(1)} %reshape.271), kind=kOutput, calls=%fused_computation.100 | convolution fusion | flops 8388608 | bytes 8407040 | tf_op jit(solution)/shard_map/dot_general | solution.py:200
  8.5 0.7 broadcast_in_dim.13
  9.2 6.3 %all-to-all-start = ((f32[16,32,128]{2,1,0:T(8,128)}), f32[16,32,128]{2,1,0:T(8,128)S(1)}, u32[]{:S(2)}, u32[]{:S(2)}) async-start(f32[16,32,128]{2,1,0:T(8,128)} %broadcast_in_dim.13), calls=%async_computation | async-start | bytes 524288 | tf_op jit(solution)/shard_map/all_to_all | solution.py:201
  16.8 5.2 %all-to-all-done = f32[16,32,128]{2,1,0:T(8,128)S(1)} async-done(((f32[16,32,128]{2,1,0:T(8,128)}), f32[16,32,128]{2,1,0:T(8,128)S(1)}, u32[]{:S(2)}, u32[]{:S(2)}) %all-to-all-start) | async-done | bytes 262176 | tf_op jit(solution)/shard_map/all_to_all | solution.py:201
  22.8 21.3 %hadamard_pick.1 = (bf16[128,16,128]{2,1,0:T(8,128)(2,1)}, bf16[128,16,128]{2,1,0:T(8,128)(2,1)}, bf16[128,16,128]{2,1,0:T(8,128)(2,1)}, bf16[128,16,128]{2,1,0:...) custom-call(s32[4096]{0:T(1024)} %add.281.spots, ...), custom_call_target="tpu_custom_call" | custom-call | flops 4400000000 | bytes 22000000 | tf_op jit(solution)/shard_map/hadamard_pick/pallas_call | solution.py:115
  44.1 1.6 collective-permute-start.2
  45.6 1.7 collective-permute-start.3
  47.4 0.8 slice.208
  48.1 3.3 %collective-permute-start.4 = (f32[8,128]{1,0:T(8,128)S(1)}, f32[8,128]{1,0:T(8,128)S(1)}, u32[]{:S(2)}, u32[]{:S(2)}) collective-permute-start(f32[8,128]{1,0:T(8,128)S(1)} %bitcast.98), channel_id=1, source_target_pairs={{0,64},{64,0},{128,192},{192,128},{1,65},{65,1},{129,193},{193,129... | collective-permute-start | bytes 12296 | tf_op jit(solution)/shard_map/ppermute | solution.py:226
  51.7 3.0 %collective-permute-start.7 = (bf16[4,32,16,128]{3,2,1,0:T(8,128)(2,1)}, bf16[4,32,16,128]{3,2,1,0:T(8,128)(2,1)S(1)}, u32[]{:S(2)}, u32[]{:S(2)}) collective-permute-start(bf16[4,32,16,128]{3,2,1,0:T(8,128)(2,1)} %bitcast.100), channel_id=1, source_target_pairs={{0,48},{16,0},{32,16},{48,32},{1,49},{17,1},{33,17},{49,33},{2,50}... | collective-permute-start | bytes 1572872 | tf_op jit(solution)/shard_map/ppermute | solution.py:23
  54.7 5.7 %collective-permute-done.2 = bf16[4,32,16,128]{3,2,1,0:T(8,128)(2,1)S(1)} collective-permute-done((bf16[4,32,16,128]{3,2,1,0:T(8,128)(2,1)}, bf16[4,32,16,128]{3,2,1,0:T(8,128)(2,1)S(1)}, u32[]{:S(2)}, u32[]{:S(2)}) %collective-permute-start.2) | collective-permute-done | bytes 524320 | tf_op jit(solution)/shard_map/ppermute | solution.py:23
  60.6 1.2 fusion.1
  61.9 1.6 collective-permute-start.5
  63.4 1.2 fusion
  64.6 1.8 %collective-permute-start.9 = (bf16[4,32,16,128]{3,2,1,0:T(8,128)(2,1)S(1)}, bf16[4,32,16,128]{3,2,1,0:T(8,128)(2,1)S(1)}, u32[]{:S(2)}, u32[]{:S(2)}) collective-permute-start(bf16[4,32,16,128]{3,2,1,0:T(8,128)(2,1)S(1)} %fusion), channel_id=1, source_target_pairs={{0,48},{16,0},{32,16},{48,32},{1,49},{17,1},{33,17},{49,33},{2,50}... | collective-permute-start | bytes 1572872 | tf_op jit(solution)/shard_map/ppermute | solution.py:23
  66.5 6.3 %collective-permute-start.8 = (f32[8,128]{1,0:T(8,128)S(1)}, f32[8,128]{1,0:T(8,128)S(1)}, u32[]{:S(2)}, u32[]{:S(2)}) collective-permute-start(f32[8,128]{1,0:T(8,128)S(1)} %add.300), channel_id=1, source_target_pairs={{0,128},{64,192},{128,0},{192,64},{1,129},{65,193},{129,1},{193,65... | collective-permute-start | bytes 12296 | tf_op jit(solution)/shard_map/ppermute | solution.py:226
  72.7 1.6 collective-permute-done.8
  74.3 7.8 %collective-permute-done.5 = bf16[4,32,16,128]{3,2,1,0:T(8,128)(2,1)S(1)} collective-permute-done((bf16[4,32,16,128]{3,2,1,0:T(8,128)(2,1)S(1)}, bf16[4,32,16,128]{3,2,1,0:T(8,128)(2,1)S(1)}, u32[]{:S(2)}, u32[]{:S(2)}) %collective-permute-start.5) | collective-permute-done | bytes 524320 | tf_op jit(solution)/shard_map/ppermute | solution.py:23
  82.4 3.4 %collective-permute-start.10 = (bf16[2,32,16,128]{3,2,1,0:T(8,128)(2,1)S(1)}, bf16[2,32,16,128]{3,2,1,0:T(8,128)(2,1)S(1)}, u32[]{:S(2)}, u32[]{:S(2)}) collective-permute-start(bf16[2,32,16,128]{3,2,1,0:T(8,128)(2,1)S(1)} %pad_maximum_fusion.1), channel_id=1, source_target_pairs={{0,64},{64,128},{128,192},{192,0},{1,65},{65,129},{129,193},{193,1... | collective-permute-start | bytes 786440 | tf_op jit(solution)/shard_map/ppermute | solution.py:23
  85.8 2.2 %collective-permute-start.11 = (bf16[2,32,16,128]{3,2,1,0:T(8,128)(2,1)S(1)}, bf16[2,32,16,128]{3,2,1,0:T(8,128)(2,1)S(1)}, u32[]{:S(2)}, u32[]{:S(2)}) collective-permute-start(bf16[2,32,16,128]{3,2,1,0:T(8,128)(2,1)S(1)} %pad_maximum_fusion.2), channel_id=1, source_target_pairs={{0,192},{64,0},{128,64},{192,128},{1,193},{65,1},{129,65},{193,129... | collective-permute-start | bytes 786440 | tf_op jit(solution)/shard_map/ppermute | solution.py:23
  88.1 1.4 collective-permute-start.12
  89.4 2.2 %collective-permute-done.12 = f32[8,128]{1,0:T(8,128)S(1)} collective-permute-done((f32[8,128]{1,0:T(8,128)S(1)}, f32[8,128]{1,0:T(8,128)S(1)}, u32[]{:S(2)}, u32[]{:S(2)}) %collective-permute-start.12) | collective-permute-done | bytes 4128 | tf_op jit(solution)/shard_map/ppermute | solution.py:226
  91.7 7.6 %collective-permute-done.10 = bf16[2,32,16,128]{3,2,1,0:T(8,128)(2,1)S(1)} collective-permute-done((bf16[2,32,16,128]{3,2,1,0:T(8,128)(2,1)S(1)}, bf16[2,32,16,128]{3,2,1,0:T(8,128)(2,1)S(1)}, u32[]{:S(2)}, u32[]{:S(2)}) %collective-permute-start.10) | collective-permute-done | bytes 262176 | tf_op jit(solution)/shard_map/ppermute | solution.py:23
  99.2 1.1 collective-permute-done.11
  100.4 2.9 %collective-permute-start.14 = (bf16[32,16,128]{2,1,0:T(8,128)(2,1)S(1)}, bf16[32,16,128]{2,1,0:T(8,128)(2,1)S(1)}, u32[]{:S(2)}, u32[]{:S(2)}) collective-permute-start(bf16[32,16,128]{2,1,0:T(8,128)(2,1)S(1)} %fusion.5), channel_id=1, source_target_pairs={{0,192},{64,0},{128,64},{192,128},{1,193},{65,1},{129,65},{193,129... | collective-permute-start | bytes 393224 | tf_op jit(solution)/shard_map/ppermute | solution.py:23
  103.4 1.1 collective-permute-start.13
  104.5 2.4 %collective-permute-start.15 = (f32[8,128]{1,0:T(8,128)S(1)}, f32[8,128]{1,0:T(8,128)S(1)}, u32[]{:S(2)}, u32[]{:S(2)}) collective-permute-start(f32[8,128]{1,0:T(8,128)S(1)} %add.314), channel_id=1, source_target_pairs={{0,32},{16,48},{32,0},{48,16},{1,33},{17,49},{33,1},{49,17},{2,34}... | collective-permute-start | bytes 12296 | tf_op jit(solution)/shard_map/ppermute | solution.py:226
  106.9 2.7 %collective-permute-done.15 = f32[8,128]{1,0:T(8,128)S(1)} collective-permute-done((f32[8,128]{1,0:T(8,128)S(1)}, f32[8,128]{1,0:T(8,128)S(1)}, u32[]{:S(2)}, u32[]{:S(2)}) %collective-permute-start.15) | collective-permute-done | bytes 4128 | tf_op jit(solution)/shard_map/ppermute | solution.py:226
  109.6 1.2 collective-permute-done.13
  111.2 3.3 %collective-permute-start.20 = (bf16[128,1024]{1,0:T(8,128)(2,1)S(1)}, bf16[128,1024]{1,0:T(8,128)(2,1)S(1)}, u32[]{:S(2)}, u32[]{:S(2)}) collective-permute-start(bf16[128,1024]{1,0:T(8,128)(2,1)S(1)} %convert_element_type.358), channel_id=1, source_target_pairs={{0,32},{16,48},{32,0},{48,16},{1,33},{17,49},{33,1},{49,17},{2,34}... | collective-permute-start | bytes 786440 | tf_op jit(solution)/shard_map/ppermute | solution.py:23
  115.0 1.5 collective-permute-start.18
  116.5 1.7 collective-permute-start.17
  118.2 1.3 collective-permute-start.16
  119.4 2.6 %collective-permute-done.20 = bf16[128,1024]{1,0:T(8,128)(2,1)S(1)} collective-permute-done((bf16[128,1024]{1,0:T(8,128)(2,1)S(1)}, bf16[128,1024]{1,0:T(8,128)(2,1)S(1)}, u32[]{:S(2)}, u32[]{:S(2)}) %collective-permute-start.20) | collective-permute-done | bytes 262176 | tf_op jit(solution)/shard_map/ppermute | solution.py:23
  122.0 3.4 %collective-permute-done.19 = bf16[128,1024]{1,0:T(8,128)(2,1)S(1)} collective-permute-done((bf16[128,1024]{1,0:T(8,128)(2,1)S(1)}, bf16[128,1024]{1,0:T(8,128)(2,1)S(1)}, u32[]{:S(2)}, u32[]{:S(2)}) %collective-permute-start.19) | collective-permute-done | bytes 262176 | tf_op jit(solution)/shard_map/ppermute | solution.py:23
  125.6 1.5 collective-permute-done.17
  127.1 3.9 %collective-permute-done.16 = bf16[128,1024]{1,0:T(8,128)(2,1)S(1)} collective-permute-done((bf16[128,1024]{1,0:T(8,128)(2,1)S(1)}, bf16[128,1024]{1,0:T(8,128)(2,1)S(1)}, u32[]{:S(2)}, u32[]{:S(2)}) %collective-permute-start.16) | collective-permute-done | bytes 262176 | tf_op jit(solution)/shard_map/ppermute | solution.py:23
  131.1 4.4 %collective-permute-start.22 = (bf16[64,1024]{1,0:T(8,128)(2,1)S(1)}, bf16[64,1024]{1,0:T(8,128)(2,1)S(1)}, u32[]{:S(2)}, u32[]{:S(2)}) collective-permute-start(bf16[64,1024]{1,0:T(8,128)(2,1)S(1)} %slice.237), channel_id=1, source_target_pairs={{0,192},{64,0},{128,64},{192,128},{1,193},{65,1},{129,65},{193,129... | collective-permute-start | bytes 393224 | tf_op jit(solution)/shard_map/ppermute | solution.py:23
  135.6 3.3 %collective-permute-done.21 = bf16[64,1024]{1,0:T(8,128)(2,1)S(1)} collective-permute-done((bf16[64,1024]{1,0:T(8,128)(2,1)S(1)}, bf16[64,1024]{1,0:T(8,128)(2,1)S(1)}, u32[]{:S(2)}, u32[]{:S(2)}) %collective-permute-start.21) | collective-permute-done | bytes 131104 | tf_op jit(solution)/shard_map/ppermute | solution.py:23
  139.2 2.5 %collective-permute-done.23.other_ref = bf16[512,1024]{1,0:T(8,128)(2,1)S(1)} collective-permute-done((bf16[512,1024]{1,0:T(8,128)(2,1)S(1)}, bf16[512,1024]{1,0:T(8,128)(2,1)S(1)}, u32[]{:S(2)}, u32[]{:S(2)}) %collective-permute-start.23) | collective-permute-done | bytes 1048608 | tf_op jit(solution)/shard_map/ppermute | solution.py:23
  141.7 4.0 %gram_tile.1 = bf16[8,2,128,256]{3,2,1,0:T(8,128)(2,1)} custom-call(s32[3]{0:T(128)S(1)} %pad_add_fusion.2.place, bf16[512,1024]{1,0:T(8,128)(2,1)S(1)} %pad_maximum_fusion.left_ref, bf16[512,1024]{1,0:T(8,128)(2,1)S(1)} %constant_dynamic-update-slice_fusion.own_ref, bf16[512,1024]{1,0:T(8,128)(2,1)S(1)} %collective-permute-done.23.other_ref), custom_call_target="tpu_custom_call" | custom-call | flops 1100000000 | bytes 4000000 | tf_op jit(solution)/shard_map/gram_tile/pallas_call | solution.py:168
  145.7 5.8 %all-to-all-start.1 = ((bf16[8,2,128,256]{3,2,1,0:T(8,128)(2,1)}), bf16[8,2,128,256]{3,2,1,0:T(8,128)(2,1)S(1)}, u32[]{:S(2)}, u32[]{:S(2)}) async-start(bf16[8,2,128,256]{3,2,1,0:T(8,128)(2,1)} %gram_tile.1), calls=%async_computation.1 | async-start | bytes 2097152 | tf_op jit(solution)/shard_map/all_to_all | solution.py:262
  151.5 14.1 %all-to-all-done.1 = bf16[8,2,128,256]{3,2,1,0:T(8,128)(2,1)S(1)} async-done(((bf16[8,2,128,256]{3,2,1,0:T(8,128)(2,1)}), bf16[8,2,128,256]{3,2,1,0:T(8,128)(2,1)S(1)}, u32[]{:S(2)}, u32[]{:S(2)}) %all-to-all-start.1) | async-done | bytes 1048608 | tf_op jit(solution)/shard_map/all_to_all | solution.py:262
  165.7 3.2 %collective-permute-start.24 = (bf16[128,256]{1,0:T(8,128)(2,1)S(1)}, bf16[128,256]{1,0:T(8,128)(2,1)S(1)}, u32[]{:S(2)}, u32[]{:S(2)}) collective-permute-start(bf16[128,256]{1,0:T(8,128)(2,1)S(1)} %get-tuple-element.66), channel_id=1, source_target_pairs={{0,32},{1,48},{2,34},{3,50},{16,0},{17,16},{18,2},{19,18},{32,33},... | collective-permute-start | bytes 196616 | tf_op jit(solution)/shard_map/ppermute | solution.py:271
  169.0 1.9 %collective-permute-start.25 = (bf16[128,256]{1,0:T(8,128)(2,1)S(1)}, bf16[128,256]{1,0:T(8,128)(2,1)S(1)}, u32[]{:S(2)}, u32[]{:S(2)}) collective-permute-start(bf16[128,256]{1,0:T(8,128)(2,1)S(1)} %get-tuple-element.67), channel_id=1, source_target_pairs={{0,0},{1,16},{2,2},{3,18},{16,32},{17,48},{18,34},{19,50},{32,1},{... | collective-permute-start | bytes 196616 | tf_op jit(solution)/shard_map/ppermute | solution.py:271
  172.2 5.3 %collective-permute-done.25 = bf16[128,256]{1,0:T(8,128)(2,1)S(1)} collective-permute-done((bf16[128,256]{1,0:T(8,128)(2,1)S(1)}, bf16[128,256]{1,0:T(8,128)(2,1)S(1)}, u32[]{:S(2)}, u32[]{:S(2)}) %collective-permute-start.25) | collective-permute-done | bytes 65568 | tf_op jit(solution)/shard_map/ppermute | solution.py:271
  177.6 0.7 maximum_multiply_fusion.1
  (79 shorter events, 7.1 us)
Async XLA Ops:
  0.6 22.1 %collective-permute-start.1 = (bf16[4096,1024]{1,0:T(8,128)(2,1)}, bf16[4096,1024]{1,0:T(8,128)(2,1)}, u32[]{:S(2)}, u32[]{:S(2)}) collective-permute-start(bf16[4096,1024]{1,0:T(8,128)(2,1)} %own_ref.1), channel_id=1, source_target_pairs={{0,8},{8,0},{1,9},{9,1},{2,10},{10,2},{3,11},{11,3},{4,12},{12,4},... | collective-permute-start | bytes 25165832 | tf_op jit(solution)/shard_map/ppermute | solution.py:23
  1.5 14.1 %collective-permute-start = (s32[3,4096]{1,0:T(4,128)S(1)}, s32[3,4096]{1,0:T(4,128)S(1)}, u32[]{:S(2)}, u32[]{:S(2)}) collective-permute-start(s32[3,4096]{1,0:T(4,128)S(1)} %pad_add_fusion), channel_id=1, source_target_pairs={{0,8},{8,0},{1,9},{9,1},{2,10},{10,2},{3,11},{11,3},{4,12},{12,4},... | collective-permute-start | bytes 147464 | tf_op jit(solution)/shard_map/ppermute | solution.py:23
  2.8 12.7 %copy-start.3 = (s32[4096]{0:T(1024)S(1)}, s32[4096]{0:T(1024)}, u32[]{:S(2)}) copy-start(s32[4096]{0:T(1024)} %param.8) | copy-start | bytes 49156
  2.8 12.8 %copy-start.4 = (s32[4096]{0:T(1024)S(1)}, s32[4096]{0:T(1024)}, u32[]{:S(2)}) copy-start(s32[4096]{0:T(1024)} %param.7) | copy-start | bytes 49156
  2.8 12.9 %copy-start.5 = (s32[1,4096]{1,0:T(1,128)S(1)}, s32[1,4096]{1,0:T(1,128)}, u32[]{:S(2)}) copy-start(s32[1,4096]{1,0:T(1,128)} %param.9) | copy-start | bytes 49156
  9.2 12.8 %all-to-all-start = ((f32[16,32,128]{2,1,0:T(8,128)}), f32[16,32,128]{2,1,0:T(8,128)S(1)}, u32[]{:S(2)}, u32[]{:S(2)}) async-start(f32[16,32,128]{2,1,0:T(8,128)} %broadcast_in_dim.13), calls=%async_computation | async-start | bytes 524288 | tf_op jit(solution)/shard_map/all_to_all | solution.py:201
  44.1 38.1 %copy-start.1 = (bf16[128,16,128]{2,1,0:T(8,128)(2,1)S(1)}, bf16[128,16,128]{2,1,0:T(8,128)(2,1)}, u32[]{:S(2)}) copy-start(bf16[128,16,128]{2,1,0:T(8,128)(2,1)} %get-tuple-element.29) | copy-start | bytes 1572868
  44.1 16.2 %collective-permute-start.2 = (bf16[4,32,16,128]{3,2,1,0:T(8,128)(2,1)}, bf16[4,32,16,128]{3,2,1,0:T(8,128)(2,1)S(1)}, u32[]{:S(2)}, u32[]{:S(2)}) collective-permute-start(bf16[4,32,16,128]{3,2,1,0:T(8,128)(2,1)} %bitcast.103), channel_id=1, source_target_pairs={{0,16},{16,32},{32,48},{48,0},{1,17},{17,33},{33,49},{49,1},{2,18}... | collective-permute-start | bytes 1572872 | tf_op jit(solution)/shard_map/ppermute | solution.py:23
  45.6 15.0 %collective-permute-start.3 = (bf16[4,32,16,128]{3,2,1,0:T(8,128)(2,1)}, bf16[4,32,16,128]{3,2,1,0:T(8,128)(2,1)S(1)}, u32[]{:S(2)}, u32[]{:S(2)}) collective-permute-start(bf16[4,32,16,128]{3,2,1,0:T(8,128)(2,1)} %bitcast.102), channel_id=1, source_target_pairs={{0,48},{16,0},{32,16},{48,32},{1,49},{17,1},{33,17},{49,33},{2,50}... | collective-permute-start | bytes 1572872 | tf_op jit(solution)/shard_map/ppermute | solution.py:23
  48.1 6.5 %collective-permute-start.4 = (f32[8,128]{1,0:T(8,128)S(1)}, f32[8,128]{1,0:T(8,128)S(1)}, u32[]{:S(2)}, u32[]{:S(2)}) collective-permute-start(f32[8,128]{1,0:T(8,128)S(1)} %bitcast.98), channel_id=1, source_target_pairs={{0,64},{64,0},{128,192},{192,128},{1,65},{65,1},{129,193},{193,129... | collective-permute-start | bytes 12296 | tf_op jit(solution)/shard_map/ppermute | solution.py:226
  51.4 22.9 %collective-permute-start.6 = (bf16[4,32,16,128]{3,2,1,0:T(8,128)(2,1)}, bf16[4,32,16,128]{3,2,1,0:T(8,128)(2,1)S(1)}, u32[]{:S(2)}, u32[]{:S(2)}) collective-permute-start(bf16[4,32,16,128]{3,2,1,0:T(8,128)(2,1)} %bitcast.101), channel_id=1, source_target_pairs={{0,16},{16,32},{32,48},{48,0},{1,17},{17,33},{33,49},{49,1},{2,18}... | collective-permute-start | bytes 1572872 | tf_op jit(solution)/shard_map/ppermute | solution.py:23
  51.7 22.6 %collective-permute-start.7 = (bf16[4,32,16,128]{3,2,1,0:T(8,128)(2,1)}, bf16[4,32,16,128]{3,2,1,0:T(8,128)(2,1)S(1)}, u32[]{:S(2)}, u32[]{:S(2)}) collective-permute-start(bf16[4,32,16,128]{3,2,1,0:T(8,128)(2,1)} %bitcast.100), channel_id=1, source_target_pairs={{0,48},{16,0},{32,16},{48,32},{1,49},{17,1},{33,17},{49,33},{2,50}... | collective-permute-start | bytes 1572872 | tf_op jit(solution)/shard_map/ppermute | solution.py:23
  60.6 21.7 %copy-start.2 = (bf16[128,16,128]{2,1,0:T(8,128)(2,1)S(1)}, bf16[128,16,128]{2,1,0:T(8,128)(2,1)}, u32[]{:S(2)}) copy-start(bf16[128,16,128]{2,1,0:T(8,128)(2,1)} %get-tuple-element.39) | copy-start | bytes 1572868
  61.9 20.3 %collective-permute-start.5 = (bf16[4,32,16,128]{3,2,1,0:T(8,128)(2,1)S(1)}, bf16[4,32,16,128]{3,2,1,0:T(8,128)(2,1)S(1)}, u32[]{:S(2)}, u32[]{:S(2)}) collective-permute-start(bf16[4,32,16,128]{3,2,1,0:T(8,128)(2,1)S(1)} %fusion.1), channel_id=1, source_target_pairs={{0,16},{16,32},{32,48},{48,0},{1,17},{17,33},{33,49},{49,1},{2,18}... | collective-permute-start | bytes 1572872 | tf_op jit(solution)/shard_map/ppermute | solution.py:23
  64.6 17.6 %collective-permute-start.9 = (bf16[4,32,16,128]{3,2,1,0:T(8,128)(2,1)S(1)}, bf16[4,32,16,128]{3,2,1,0:T(8,128)(2,1)S(1)}, u32[]{:S(2)}, u32[]{:S(2)}) collective-permute-start(bf16[4,32,16,128]{3,2,1,0:T(8,128)(2,1)S(1)} %fusion), channel_id=1, source_target_pairs={{0,48},{16,0},{32,16},{48,32},{1,49},{17,1},{33,17},{49,33},{2,50}... | collective-permute-start | bytes 1572872 | tf_op jit(solution)/shard_map/ppermute | solution.py:23
  66.5 7.9 %collective-permute-start.8 = (f32[8,128]{1,0:T(8,128)S(1)}, f32[8,128]{1,0:T(8,128)S(1)}, u32[]{:S(2)}, u32[]{:S(2)}) collective-permute-start(f32[8,128]{1,0:T(8,128)S(1)} %add.300), channel_id=1, source_target_pairs={{0,128},{64,192},{128,0},{192,64},{1,129},{65,193},{129,1},{193,65... | collective-permute-start | bytes 12296 | tf_op jit(solution)/shard_map/ppermute | solution.py:226
  82.4 16.8 %collective-permute-start.10 = (bf16[2,32,16,128]{3,2,1,0:T(8,128)(2,1)S(1)}, bf16[2,32,16,128]{3,2,1,0:T(8,128)(2,1)S(1)}, u32[]{:S(2)}, u32[]{:S(2)}) collective-permute-start(bf16[2,32,16,128]{3,2,1,0:T(8,128)(2,1)S(1)} %pad_maximum_fusion.1), channel_id=1, source_target_pairs={{0,64},{64,128},{128,192},{192,0},{1,65},{65,129},{129,193},{193,1... | collective-permute-start | bytes 786440 | tf_op jit(solution)/shard_map/ppermute | solution.py:23
  85.8 14.5 %collective-permute-start.11 = (bf16[2,32,16,128]{3,2,1,0:T(8,128)(2,1)S(1)}, bf16[2,32,16,128]{3,2,1,0:T(8,128)(2,1)S(1)}, u32[]{:S(2)}, u32[]{:S(2)}) collective-permute-start(bf16[2,32,16,128]{3,2,1,0:T(8,128)(2,1)S(1)} %pad_maximum_fusion.2), channel_id=1, source_target_pairs={{0,192},{64,0},{128,64},{192,128},{1,193},{65,1},{129,65},{193,129... | collective-permute-start | bytes 786440 | tf_op jit(solution)/shard_map/ppermute | solution.py:23
  88.1 3.6 %collective-permute-start.12 = (f32[8,128]{1,0:T(8,128)S(1)}, f32[8,128]{1,0:T(8,128)S(1)}, u32[]{:S(2)}, u32[]{:S(2)}) collective-permute-start(f32[8,128]{1,0:T(8,128)S(1)} %add.303), channel_id=1, source_target_pairs={{0,16},{16,0},{32,48},{48,32},{1,17},{17,1},{33,49},{49,33},{2,18}... | collective-permute-start | bytes 12296 | tf_op jit(solution)/shard_map/ppermute | solution.py:226
  100.4 9.1 %collective-permute-start.14 = (bf16[32,16,128]{2,1,0:T(8,128)(2,1)S(1)}, bf16[32,16,128]{2,1,0:T(8,128)(2,1)S(1)}, u32[]{:S(2)}, u32[]{:S(2)}) collective-permute-start(bf16[32,16,128]{2,1,0:T(8,128)(2,1)S(1)} %fusion.5), channel_id=1, source_target_pairs={{0,192},{64,0},{128,64},{192,128},{1,193},{65,1},{129,65},{193,129... | collective-permute-start | bytes 393224 | tf_op jit(solution)/shard_map/ppermute | solution.py:23
  103.4 7.4 %collective-permute-start.13 = (bf16[32,16,128]{2,1,0:T(8,128)(2,1)S(1)}, bf16[32,16,128]{2,1,0:T(8,128)(2,1)S(1)}, u32[]{:S(2)}, u32[]{:S(2)}) collective-permute-start(bf16[32,16,128]{2,1,0:T(8,128)(2,1)S(1)} %fusion.7), channel_id=1, source_target_pairs={{0,64},{64,128},{128,192},{192,0},{1,65},{65,129},{129,193},{193,1... | collective-permute-start | bytes 393224 | tf_op jit(solution)/shard_map/ppermute | solution.py:23
  104.5 5.1 %collective-permute-start.15 = (f32[8,128]{1,0:T(8,128)S(1)}, f32[8,128]{1,0:T(8,128)S(1)}, u32[]{:S(2)}, u32[]{:S(2)}) collective-permute-start(f32[8,128]{1,0:T(8,128)S(1)} %add.314), channel_id=1, source_target_pairs={{0,32},{16,48},{32,0},{48,16},{1,33},{17,49},{33,1},{49,17},{2,34}... | collective-permute-start | bytes 12296 | tf_op jit(solution)/shard_map/ppermute | solution.py:226
  111.2 28.0 %copy-start = (bf16[128,1024]{1,0:T(8,128)(2,1)}, bf16[128,1024]{1,0:T(8,128)(2,1)S(1)}, u32[]{:S(2)}) copy-start(bf16[128,1024]{1,0:T(8,128)(2,1)S(1)} %convert_element_type.358) | copy-start | bytes 786436
  111.2 10.8 %collective-permute-start.20 = (bf16[128,1024]{1,0:T(8,128)(2,1)S(1)}, bf16[128,1024]{1,0:T(8,128)(2,1)S(1)}, u32[]{:S(2)}, u32[]{:S(2)}) collective-permute-start(bf16[128,1024]{1,0:T(8,128)(2,1)S(1)} %convert_element_type.358), channel_id=1, source_target_pairs={{0,32},{16,48},{32,0},{48,16},{1,33},{17,49},{33,1},{49,17},{2,34}... | collective-permute-start | bytes 786440 | tf_op jit(solution)/shard_map/ppermute | solution.py:23
  114.5 11.0 %collective-permute-start.19 = (bf16[128,1024]{1,0:T(8,128)(2,1)S(1)}, bf16[128,1024]{1,0:T(8,128)(2,1)S(1)}, u32[]{:S(2)}, u32[]{:S(2)}) collective-permute-start(bf16[128,1024]{1,0:T(8,128)(2,1)S(1)} %convert_element_type.358), channel_id=1, source_target_pairs={{0,48},{16,0},{32,16},{48,32},{1,49},{17,1},{33,17},{49,33},{2,50}... | collective-permute-start | bytes 786440 | tf_op jit(solution)/shard_map/ppermute | solution.py:23
  115.0 10.5 %collective-permute-start.18 = (bf16[128,1024]{1,0:T(8,128)(2,1)S(1)}, bf16[128,1024]{1,0:T(8,128)(2,1)S(1)}, u32[]{:S(2)}, u32[]{:S(2)}) collective-permute-start(bf16[128,1024]{1,0:T(8,128)(2,1)S(1)} %convert_element_type.358), channel_id=1, source_target_pairs={{0,16},{16,32},{32,48},{48,0},{1,17},{17,33},{33,49},{49,1},{2,18}... | collective-permute-start | bytes 786440 | tf_op jit(solution)/shard_map/ppermute | solution.py:23
  116.5 10.6 %collective-permute-start.17 = (bf16[128,1024]{1,0:T(8,128)(2,1)S(1)}, bf16[128,1024]{1,0:T(8,128)(2,1)S(1)}, u32[]{:S(2)}, u32[]{:S(2)}) collective-permute-start(bf16[128,1024]{1,0:T(8,128)(2,1)S(1)} %convert_element_type.358), channel_id=1, source_target_pairs={{0,192},{64,0},{128,64},{192,128},{1,193},{65,1},{129,65},{193,129... | collective-permute-start | bytes 786440 | tf_op jit(solution)/shard_map/ppermute | solution.py:23
  118.2 12.8 %collective-permute-start.16 = (bf16[128,1024]{1,0:T(8,128)(2,1)S(1)}, bf16[128,1024]{1,0:T(8,128)(2,1)S(1)}, u32[]{:S(2)}, u32[]{:S(2)}) collective-permute-start(bf16[128,1024]{1,0:T(8,128)(2,1)S(1)} %convert_element_type.358), channel_id=1, source_target_pairs={{0,64},{64,128},{128,192},{192,0},{1,65},{65,129},{129,193},{193,1... | collective-permute-start | bytes 786440 | tf_op jit(solution)/shard_map/ppermute | solution.py:23
  131.0 7.8 %collective-permute-start.21 = (bf16[64,1024]{1,0:T(8,128)(2,1)S(1)}, bf16[64,1024]{1,0:T(8,128)(2,1)S(1)}, u32[]{:S(2)}, u32[]{:S(2)}) collective-permute-start(bf16[64,1024]{1,0:T(8,128)(2,1)S(1)} %slice.236), channel_id=1, source_target_pairs={{0,64},{64,128},{128,192},{192,0},{1,65},{65,129},{129,193},{193,1... | collective-permute-start | bytes 393224 | tf_op jit(solution)/shard_map/ppermute | solution.py:23
  131.1 7.7 %collective-permute-start.22 = (bf16[64,1024]{1,0:T(8,128)(2,1)S(1)}, bf16[64,1024]{1,0:T(8,128)(2,1)S(1)}, u32[]{:S(2)}, u32[]{:S(2)}) collective-permute-start(bf16[64,1024]{1,0:T(8,128)(2,1)S(1)} %slice.237), channel_id=1, source_target_pairs={{0,192},{64,0},{128,64},{192,128},{1,193},{65,1},{129,65},{193,129... | collective-permute-start | bytes 393224 | tf_op jit(solution)/shard_map/ppermute | solution.py:23
  138.9 2.7 %collective-permute-start.23 = (bf16[512,1024]{1,0:T(8,128)(2,1)S(1)}, bf16[512,1024]{1,0:T(8,128)(2,1)S(1)}, u32[]{:S(2)}, u32[]{:S(2)}) collective-permute-start(bf16[512,1024]{1,0:T(8,128)(2,1)S(1)} %constant_dynamic-update-slice_fusion.own_ref), channel_id=1, source_target_pairs={{0,8},{8,0},{1,9},{9,1},{2,10},{10,2},{3,11},{11,3},{4,12},{12,4},... | collective-permute-start | bytes 3145736 | tf_op jit(solution)/shard_map/ppermute | solution.py:23
  145.7 19.9 %all-to-all-start.1 = ((bf16[8,2,128,256]{3,2,1,0:T(8,128)(2,1)}), bf16[8,2,128,256]{3,2,1,0:T(8,128)(2,1)S(1)}, u32[]{:S(2)}, u32[]{:S(2)}) async-start(bf16[8,2,128,256]{3,2,1,0:T(8,128)(2,1)} %gram_tile.1), calls=%async_computation.1 | async-start | bytes 2097152 | tf_op jit(solution)/shard_map/all_to_all | solution.py:262
  165.7 6.5 %collective-permute-start.24 = (bf16[128,256]{1,0:T(8,128)(2,1)S(1)}, bf16[128,256]{1,0:T(8,128)(2,1)S(1)}, u32[]{:S(2)}, u32[]{:S(2)}) collective-permute-start(bf16[128,256]{1,0:T(8,128)(2,1)S(1)} %get-tuple-element.66), channel_id=1, source_target_pairs={{0,32},{1,48},{2,34},{3,50},{16,0},{17,16},{18,2},{19,18},{32,33},... | collective-permute-start | bytes 196616 | tf_op jit(solution)/shard_map/ppermute | solution.py:271
  169.0 8.6 %collective-permute-start.25 = (bf16[128,256]{1,0:T(8,128)(2,1)S(1)}, bf16[128,256]{1,0:T(8,128)(2,1)S(1)}, u32[]{:S(2)}, u32[]{:S(2)}) collective-permute-start(bf16[128,256]{1,0:T(8,128)(2,1)S(1)} %get-tuple-element.67), channel_id=1, source_target_pairs={{0,0},{1,16},{2,2},{3,18},{16,32},{17,48},{18,34},{19,50},{32,1},{... | collective-permute-start | bytes 196616 | tf_op jit(solution)/shard_map/ppermute | solution.py:271

commit v2 on v1

--- a/solution.py
+++ b/solution.py
@@ -16,11 +16,39 @@
 HALF_PAIRS = 32
 UNROLL = 16
 EXTRA = 16
+MARGIN_ROWS = 1024
 
 
 def ring(axis_name, value, shift):
     size = lax.axis_size(axis_name)
     return lax.ppermute(value, axis_name, [(i, (i + shift) % size) for i in range(size)])
+
+
+def margin_kernel(rows_ref, coef_ref, out):
+    step = pl.program_id(0)
+    sums = lax.dot_general(
+        coef_ref[...], rows_ref[...], (((1,), (1,)), ((), ())), preferred_element_type=jnp.float32
+    )
+    for part in range(MARGIN_ROWS // 128):
+        out[:, pl.ds(step * (MARGIN_ROWS // 128) + part, 1), :] = sums[:, part * 128 : (part + 1) * 128].reshape(
+            16, 1, 128
+        )
+
+
+def margin_parts(features, coef):
+    return pl.pallas_call(
+        margin_kernel,
+        grid=(ROWS // MARGIN_ROWS,),
+        in_specs=[
+            pl.BlockSpec((MARGIN_ROWS, COLS), lambda i: (i, 0)),
+            pl.BlockSpec((16, COLS), lambda i: (0, 0)),
+        ],
+        out_specs=pl.BlockSpec((16, ROWS // 128, 128), lambda i: (0, 0, 0)),
+        out_shape=jax.ShapeDtypeStruct((16, ROWS // 128, 128), jnp.float32),
+        compiler_params=pltpu.CompilerParams(vmem_limit_bytes=60 * 1024 * 1024),
+        cost_estimate=pl.CostEstimate(flops=130_000_000, bytes_accessed=9_000_000, transcendentals=0),
+        name="margin_parts",
+    )(features, jnp.broadcast_to(coef, (16, COLS)))
 
 
 def sketch_kernel(spots, own_ref, other_ref, factor_ref, residual_ref, *refs):
@@ -140,41 +168,41 @@
     )(spots, own, other, factors, residuals)
 
 
-def gram_kernel(place, left_ref, own_ref, other_ref, out, tile):
+def gram_kernel(place, left_ref, right_ref, *refs):
+    earlier, out, tile = (refs[0], refs[1], refs[2]) if len(refs) == 3 else (None, *refs)
     my_zh, my_x, my_c = [place[i] for i in range(3)]
-    for which, source in enumerate((own_ref, other_ref)):
-        core = my_c if which == 0 else 1 - my_c
-        for shift in range(4):
-            product = lax.dot_general(
-                left_ref[...],
-                source[shift * 128 : (shift + 1) * 128, :],
-                (((1,), (1,)), ((), ())),
-                preferred_element_type=jnp.float32,
-            )
-            for row in range(4):
-                tile[lax.rem(my_zh + shift, 4) * 2 + core, lax.rem(my_x + row, 4)] = product[
-                    row * 128 : (row + 1) * 128
-                ].astype(jnp.bfloat16)
+    product = lax.dot_general(
+        left_ref[...], right_ref[...], (((1,), (1,)), ((), ())), preferred_element_type=jnp.float32
+    ).astype(jnp.bfloat16)
+    for shift in range(4):
+        for row in range(4):
+            tile[lax.rem(my_zh + shift, 4), lax.rem(my_x + row, 4)] = product[
+                row * 128 : (row + 1) * 128, shift * 128 : (shift + 1) * 128
+            ]
     for target in range(8):
         zh, x_low = target // 2, target % 2
         for i in range(2):
-            x_high = lax.rem(my_x + i, 2)
-            for core in range(2):
-                out[target, i, :, core * 128 : (core + 1) * 128] = tile[zh * 2 + core, x_high * 2 + x_low]
-
-
-def gram_pieces(place, left, right):
+            block = tile[zh, lax.rem(my_x + i, 2) * 2 + x_low]
+            if earlier is None:
+                out[target, i] = block
+            else:
+                first = earlier[target, i]
+                out[target, i, :, :128] = jnp.where(my_c == 0, first, block)
+                out[target, i, :, 128:] = jnp.where(my_c == 0, block, first)
+
+
+def gram_pieces(place, left, right, earlier=()):
     vmem = pl.BlockSpec(memory_space=pltpu.VMEM)
     return pl.pallas_call(
         gram_kernel,
-        in_specs=[pl.BlockSpec(memory_space=pltpu.SMEM)] + [vmem] * 3,
+        in_specs=[pl.BlockSpec(memory_space=pltpu.SMEM)] + [vmem] * (2 + len(earlier)),
         out_specs=vmem,
-        out_shape=jax.ShapeDtypeStruct((8, 2, 128, 256), jnp.bfloat16),
-        scratch_shapes=[pltpu.VMEM((8, 4, 128, 128), jnp.bfloat16)],
+        out_shape=jax.ShapeDtypeStruct((8, 2, 128, 128 * (1 + len(earlier))), jnp.bfloat16),
+        scratch_shapes=[pltpu.VMEM((4, 4, 128, 128), jnp.bfloat16)],
         compiler_params=pltpu.CompilerParams(vmem_limit_bytes=32 * 1024 * 1024),
-        cost_estimate=pl.CostEstimate(flops=1_100_000_000, bytes_accessed=4_000_000, transcendentals=0),
+        cost_estimate=pl.CostEstimate(flops=540_000_000, bytes_accessed=3_000_000, transcendentals=0),
         name="gram_tile",
-    )(place, *left, *right)
+    )(place, left, right, *earlier)
 
 
 def add_up(*terms):
@@ -197,8 +225,7 @@
     integers = jnp.concatenate([samples, sign_bits[None], labels[None]], axis=0)
     other_integers = ring("c", integers, 1)
 
-    partial_value = jnp.dot(features, coef, preferred_element_type=jnp.float32).reshape(32, 128)
-    everyone = lax.all_to_all(jnp.broadcast_to(partial_value, (16, 32, 128)), ("c", "zl", "y"), 0, 0).reshape(2, 8, 32, 128)
+    everyone = lax.all_to_all(margin_parts(features, coef), ("c", "zl", "y"), 0, 0).reshape(2, 8, 32, 128)
     by_core = [sum(everyone[core, k] for k in range(8)) for core in range(2)]
     margins = jnp.where(my_c == 0, by_core[0], by_core[1])
     other_margins = jnp.where(my_c == 0, by_core[1], by_core[0])
@@ -244,21 +271,24 @@
     from_last, from_next, gradient = lax.optimization_barrier((from_last, from_next, gradient))
     end_0 = ring("zh", narrow(short[1][0], from_last[0]), 1)
     end_1 = ring("zh", narrow(short[3][1], from_next[0]), -1)
-    gradient = swap_add("x", 2, gradient)
-    end_0, end_1, gradient = lax.optimization_barrier((end_0, end_1, gradient))
+    end_0, end_1 = lax.optimization_barrier((end_0, end_1))
     summed = [add_up(wide[0][0], from_next[1], end_0), add_up(wide[0][1], from_last[1], end_1)]
     summed = jnp.concatenate(summed, axis=0).reshape(128, COLS)
     sketch = (summed / root_total).astype(jnp.bfloat16)
 
     zh_last, zh_next = ring("zh", sketch, 1), ring("zh", sketch, -1)
-    x_next, x_far, x_last = (ring("x", sketch, shift) for shift in (-1, 2, 1))
+    _, gradient = lax.optimization_barrier((sketch, gradient))
+    gradient = swap_add("x", 2, gradient)
+    for_x, gradient = lax.optimization_barrier((sketch, gradient))
+    x_next, x_far, x_last = (ring("x", for_x, shift) for shift in (-1, 2, 1))
     zh_last, zh_next, x_last, x_next, x_far = lax.optimization_barrier((zh_last, zh_next, x_last, x_next, x_far))
     zh_far_0, zh_far_1 = ring("zh", zh_last[:64], 1), ring("zh", zh_next[64:], -1)
-    left = [jnp.concatenate([sketch, x_next, x_far, x_last], axis=0)]
+    left = jnp.concatenate([sketch, x_next, x_far, x_last], axis=0)
     own_rows = jnp.concatenate([sketch, zh_next, zh_far_0, zh_far_1, zh_last], axis=0)
-    right = [own_rows, ring("c", own_rows, 1)]
+    other_rows = ring("c", own_rows, 1)
     place = jnp.stack([my_zh, my_x, my_c]).astype(jnp.int32)
-    tiles = gram_pieces(place, left, right)
+    own_tile = gram_pieces(place, left, own_rows)
+    tiles = gram_pieces(place, left, other_rows, (own_tile,))
     parts = lax.all_to_all(tiles, ("zl", "y"), 0, 0)
     over_feat = add_up(*(parts[k] for k in range(8))).astype(jnp.bfloat16)
 

time: 179 us -> 180 us (level)
  Pallas kernels: 25.3 us -> 31.2 us
  matrix products: 5.68 us -> 0 us
  other arithmetic: 6.46 us -> 11.9 us
  starting transfers between devices: 63.5 us -> 60.2 us
    pallas_call x0 -> x1, Pallas kernels: none -> 6.1 us  [margin_parts(): pl.pallas_call(margin_kernel, grid=(ROWS // MARGIN_ROWS,), in_specs=[pl.B...]
    dot_general x1 -> x0, matrix products: 5.68 us -> none  [per_device(): jnp.dot(features, coef, preferred_element_type=jnp.float32).reshape(32, 128)]
    convert_element_type x2, other arithmetic: 0.22 us -> 2.15 us  [per_device(): short = [[half.astype(jnp.bfloat16) for half in pair] for pair in wide]]
    add x2, other arithmetic: 0.17 us -> 1.98 us  [add_up(): total = total + term.astype(jnp.float32)]
    pallas_call x1 -> x2, Pallas kernels: 4.04 us -> 3.81 us  [gram_pieces(): pl.pallas_call(gram_kernel, in_specs=[pl.BlockSpec(memory_space=pltpu.SME...]
  transfers between devices with their start and end apart: 28 -> 28, of which waited for: 20 -> 22; matrix products, arithmetic and copies ran while one was open for 8% -> 6% of each run, Pallas kernels for 0% -> 4%
where the time goes in v2:
time: 180 us; the launch traced here: 179 us
  waiting for transfers between devices  71.2 us (40%)
  starting transfers between devices  60.2 us (33%)
  Pallas kernels  31.2 us (17%)
  other arithmetic  11.9 us (7%)
  local copies, waits for them, and re-layouts  3.3 us (2%)
    ppermute x20, waiting for transfers between devices, ring(): lax.ppermute(value, axis_name, [(i, (i + shift) % size) for i in range(si...  41.9 us
    ppermute x20, starting transfers between devices, ring(): lax.ppermute(value, axis_name, [(i, (i + shift) % size) for i in range(si...  32 us
    pallas_call x1, Pallas kernels, sketch_pieces(): pl.pallas_call(sketch_kernel, grid_spec=pltpu.PrefetchScalarGridSpec(num_...  21.2 us
    all_to_all x1, waiting for transfers between devices, per_device(): parts = lax.all_to_all(tiles, ('zl', 'y'), 0, 0)  13.9 us
    ppermute x4, starting transfers between devices, swap_add(): lax.ppermute(value, axis_name, [(i, i ^ flip) for i in range(4)])  11.9 us
    all_to_all x1, starting transfers between devices, per_device(): lax.all_to_all(margin_parts(features, coef), ('c', 'zl', 'y'), 0, 0)  6.29 us
    pallas_call x1, Pallas kernels, margin_parts(): pl.pallas_call(margin_kernel, grid=(ROWS // MARGIN_ROWS,), in_specs=[pl.B...  6.1 us
    all_to_all x1, starting transfers between devices, per_device(): parts = lax.all_to_all(tiles, ('zl', 'y'), 0, 0)  5.49 us
  transfers between devices with their start and end apart: 28, of which 22 were waited for; matrix products, arithmetic and copies ran while one was open for 6% of the time, Pallas kernels for 4%

profile of v2, /device:TPU:8, one launch (start us, length us, event | category | flops | bytes accessed | tf_op | source)
XLA Modules:
  0.0 178.9 jit_solution(6974671151165347924)
XLA Ops:
  2.1 1.3 broadcast_in_dim.13.coef_ref
  3.4 6.1 %margin_parts.1 = f32[16,32,128]{2,1,0:T(8,128)} custom-call(bf16[4096,1024]{1,0:T(8,128)(2,1)} %own_ref.1, bf16[16,1024]{1,0:T(8,128)(2,1)} %broadcast_in_dim.13.coef_ref), custom_call_target="tpu_custom_call" | custom-call | flops 130000000 | bytes 9000000 | tf_op jit(solution)/shard_map/margin_parts/pallas_call | solution.py:39
  9.5 6.3 %all-to-all-start = ((f32[16,32,128]{2,1,0:T(8,128)}), f32[16,32,128]{2,1,0:T(8,128)S(1)}, u32[]{:S(2)}, u32[]{:S(2)}) async-start(f32[16,32,128]{2,1,0:T(8,128)} %margin_parts.1), calls=%async_computation | async-start | bytes 524288 | tf_op jit(solution)/shard_map/all_to_all | solution.py:228
  17.1 5.2 %all-to-all-done = f32[16,32,128]{2,1,0:T(8,128)S(1)} async-done(((f32[16,32,128]{2,1,0:T(8,128)}), f32[16,32,128]{2,1,0:T(8,128)S(1)}, u32[]{:S(2)}, u32[]{:S(2)}) %all-to-all-start) | async-done | bytes 262176 | tf_op jit(solution)/shard_map/all_to_all | solution.py:228
  23.1 21.2 %hadamard_pick.1 = (bf16[128,16,128]{2,1,0:T(8,128)(2,1)}, bf16[128,16,128]{2,1,0:T(8,128)(2,1)}, bf16[128,16,128]{2,1,0:T(8,128)(2,1)}, bf16[128,16,128]{2,1,0:...) custom-call(s32[4096]{0:T(1024)} %add.281.spots, ...), custom_call_target="tpu_custom_call" | custom-call | flops 4400000000 | bytes 22000000 | tf_op jit(solution)/shard_map/hadamard_pick/pallas_call | solution.py:143
  44.3 1.5 collective-permute-start.2
  45.9 1.7 collective-permute-start.3
  48.4 3.3 %collective-permute-start.4 = (f32[8,128]{1,0:T(8,128)S(1)}, f32[8,128]{1,0:T(8,128)S(1)}, u32[]{:S(2)}, u32[]{:S(2)}) collective-permute-start(f32[8,128]{1,0:T(8,128)S(1)} %bitcast.92), channel_id=1, source_target_pairs={{0,64},{64,0},{128,192},{192,128},{1,65},{65,1},{129,193},{193,129... | collective-permute-start | bytes 12296 | tf_op jit(solution)/shard_map/ppermute | solution.py:253
  51.9 3.0 %collective-permute-start.7 = (bf16[4,32,16,128]{3,2,1,0:T(8,128)(2,1)}, bf16[4,32,16,128]{3,2,1,0:T(8,128)(2,1)S(1)}, u32[]{:S(2)}, u32[]{:S(2)}) collective-permute-start(bf16[4,32,16,128]{3,2,1,0:T(8,128)(2,1)} %bitcast.94), channel_id=1, source_target_pairs={{0,48},{16,0},{32,16},{48,32},{1,49},{17,1},{33,17},{49,33},{2,50}... | collective-permute-start | bytes 1572872 | tf_op jit(solution)/shard_map/ppermute | solution.py:24
  54.9 5.7 %collective-permute-done.2 = bf16[4,32,16,128]{3,2,1,0:T(8,128)(2,1)S(1)} collective-permute-done((bf16[4,32,16,128]{3,2,1,0:T(8,128)(2,1)}, bf16[4,32,16,128]{3,2,1,0:T(8,128)(2,1)S(1)}, u32[]{:S(2)}, u32[]{:S(2)}) %collective-permute-start.2) | collective-permute-done | bytes 524320 | tf_op jit(solution)/shard_map/ppermute | solution.py:24
  60.9 1.2 fusion.1
  62.0 1.6 collective-permute-start.5
  63.6 1.2 fusion
  64.8 2.0 %collective-permute-start.9 = (bf16[4,32,16,128]{3,2,1,0:T(8,128)(2,1)S(1)}, bf16[4,32,16,128]{3,2,1,0:T(8,128)(2,1)S(1)}, u32[]{:S(2)}, u32[]{:S(2)}) collective-permute-start(bf16[4,32,16,128]{3,2,1,0:T(8,128)(2,1)S(1)} %fusion), channel_id=1, source_target_pairs={{0,48},{16,0},{32,16},{48,32},{1,49},{17,1},{33,17},{49,33},{2,50}... | collective-permute-start | bytes 1572872 | tf_op jit(solution)/shard_map/ppermute | solution.py:24
  66.8 6.3 %collective-permute-start.8 = (f32[8,128]{1,0:T(8,128)S(1)}, f32[8,128]{1,0:T(8,128)S(1)}, u32[]{:S(2)}, u32[]{:S(2)}) collective-permute-start(f32[8,128]{1,0:T(8,128)S(1)} %add.300), channel_id=1, source_target_pairs={{0,128},{64,192},{128,0},{192,64},{1,129},{65,193},{129,1},{193,65... | collective-permute-start | bytes 12296 | tf_op jit(solution)/shard_map/ppermute | solution.py:253
  73.1 1.6 collective-permute-done.8
  74.7 7.7 %collective-permute-done.5 = bf16[4,32,16,128]{3,2,1,0:T(8,128)(2,1)S(1)} collective-permute-done((bf16[4,32,16,128]{3,2,1,0:T(8,128)(2,1)S(1)}, bf16[4,32,16,128]{3,2,1,0:T(8,128)(2,1)S(1)}, u32[]{:S(2)}, u32[]{:S(2)}) %collective-permute-start.5) | collective-permute-done | bytes 524320 | tf_op jit(solution)/shard_map/ppermute | solution.py:24
  82.4 1.1 fusion.10
  83.5 1.1 fusion.12
  84.6 3.3 %collective-permute-start.10 = (bf16[2,32,16,128]{3,2,1,0:T(8,128)(2,1)S(1)}, bf16[2,32,16,128]{3,2,1,0:T(8,128)(2,1)S(1)}, u32[]{:S(2)}, u32[]{:S(2)}) collective-permute-start(bf16[2,32,16,128]{3,2,1,0:T(8,128)(2,1)S(1)} %pad_maximum_fusion), channel_id=1, source_target_pairs={{0,64},{64,128},{128,192},{192,0},{1,65},{65,129},{129,193},{193,1... | collective-permute-start | bytes 786440 | tf_op jit(solution)/shard_map/ppermute | solution.py:24
  88.0 2.2 %collective-permute-start.11 = (bf16[2,32,16,128]{3,2,1,0:T(8,128)(2,1)S(1)}, bf16[2,32,16,128]{3,2,1,0:T(8,128)(2,1)S(1)}, u32[]{:S(2)}, u32[]{:S(2)}) collective-permute-start(bf16[2,32,16,128]{3,2,1,0:T(8,128)(2,1)S(1)} %pad_maximum_fusion.1), channel_id=1, source_target_pairs={{0,192},{64,0},{128,64},{192,128},{1,193},{65,1},{129,65},{193,129... | collective-permute-start | bytes 786440 | tf_op jit(solution)/shard_map/ppermute | solution.py:24
  90.6 3.2 %collective-permute-done.12 = f32[8,128]{1,0:T(8,128)S(1)} collective-permute-done((f32[8,128]{1,0:T(8,128)S(1)}, f32[8,128]{1,0:T(8,128)S(1)}, u32[]{:S(2)}, u32[]{:S(2)}) %collective-permute-start.12) | collective-permute-done | bytes 4128 | tf_op jit(solution)/shard_map/ppermute | solution.py:253
  93.8 7.6 %collective-permute-done.10 = bf16[2,32,16,128]{3,2,1,0:T(8,128)(2,1)S(1)} collective-permute-done((bf16[2,32,16,128]{3,2,1,0:T(8,128)(2,1)S(1)}, bf16[2,32,16,128]{3,2,1,0:T(8,128)(2,1)S(1)}, u32[]{:S(2)}, u32[]{:S(2)}) %collective-permute-start.10) | collective-permute-done | bytes 262176 | tf_op jit(solution)/shard_map/ppermute | solution.py:24
  102.5 3.8 %collective-permute-start.13 = (bf16[32,16,128]{2,1,0:T(8,128)(2,1)S(1)}, bf16[32,16,128]{2,1,0:T(8,128)(2,1)S(1)}, u32[]{:S(2)}, u32[]{:S(2)}) collective-permute-start(bf16[32,16,128]{2,1,0:T(8,128)(2,1)S(1)} %fusion.6), channel_id=1, source_target_pairs={{0,64},{64,128},{128,192},{192,0},{1,65},{65,129},{129,193},{193,1... | collective-permute-start | bytes 393224 | tf_op jit(solution)/shard_map/ppermute | solution.py:24
  107.7 2.9 %collective-permute-done.13 = bf16[32,16,128]{2,1,0:T(8,128)(2,1)S(1)} collective-permute-done((bf16[32,16,128]{2,1,0:T(8,128)(2,1)S(1)}, bf16[32,16,128]{2,1,0:T(8,128)(2,1)S(1)}, u32[]{:S(2)}, u32[]{:S(2)}) %collective-permute-start.13) | collective-permute-done | bytes 131104 | tf_op jit(solution)/shard_map/ppermute | solution.py:24
  110.6 2.8 %collective-permute-done.14 = bf16[32,16,128]{2,1,0:T(8,128)(2,1)S(1)} collective-permute-done((bf16[32,16,128]{2,1,0:T(8,128)(2,1)S(1)}, bf16[32,16,128]{2,1,0:T(8,128)(2,1)S(1)}, u32[]{:S(2)}, u32[]{:S(2)}) %collective-permute-start.14) | collective-permute-done | bytes 131104 | tf_op jit(solution)/shard_map/ppermute | solution.py:24
  113.4 1.0 fusion.3
  114.4 1.0 fusion.8
  115.6 1.9 %collective-permute-start.15 = (f32[8,128]{1,0:T(8,128)S(1)}, f32[8,128]{1,0:T(8,128)S(1)}, u32[]{:S(2)}, u32[]{:S(2)}) collective-permute-start(f32[8,128]{1,0:T(8,128)S(1)} %add.314), channel_id=1, source_target_pairs={{0,32},{16,48},{32,0},{48,16},{1,33},{17,49},{33,1},{49,17},{2,34}... | collective-permute-start | bytes 12296 | tf_op jit(solution)/shard_map/ppermute | solution.py:253
  117.5 2.5 %collective-permute-start.17 = (bf16[128,1024]{1,0:T(8,128)(2,1)S(1)}, bf16[128,1024]{1,0:T(8,128)(2,1)S(1)}, u32[]{:S(2)}, u32[]{:S(2)}) collective-permute-start(bf16[128,1024]{1,0:T(8,128)(2,1)S(1)} %convert_element_type.358), channel_id=1, source_target_pairs={{0,192},{64,0},{128,64},{192,128},{1,193},{65,1},{129,65},{193,129... | collective-permute-start | bytes 786440 | tf_op jit(solution)/shard_map/ppermute | solution.py:24
  120.8 1.8 %collective-permute-start.20 = (bf16[128,1024]{1,0:T(8,128)(2,1)S(1)}, bf16[128,1024]{1,0:T(8,128)(2,1)S(1)}, u32[]{:S(2)}, u32[]{:S(2)}) collective-permute-start(bf16[128,1024]{1,0:T(8,128)(2,1)S(1)} %convert_element_type.358), channel_id=1, source_target_pairs={{0,32},{16,48},{32,0},{48,16},{1,33},{17,49},{33,1},{49,17},{2,34}... | collective-permute-start | bytes 786440 | tf_op jit(solution)/shard_map/ppermute | solution.py:24
  122.6 1.1 collective-permute-start.19
  125.1 3.5 %collective-permute-done.16 = bf16[128,1024]{1,0:T(8,128)(2,1)S(1)} collective-permute-done((bf16[128,1024]{1,0:T(8,128)(2,1)S(1)}, bf16[128,1024]{1,0:T(8,128)(2,1)S(1)}, u32[]{:S(2)}, u32[]{:S(2)}) %collective-permute-start.16) | collective-permute-done | bytes 262176 | tf_op jit(solution)/shard_map/ppermute | solution.py:24
  128.6 2.3 %collective-permute-done.20 = bf16[128,1024]{1,0:T(8,128)(2,1)S(1)} collective-permute-done((bf16[128,1024]{1,0:T(8,128)(2,1)S(1)}, bf16[128,1024]{1,0:T(8,128)(2,1)S(1)}, u32[]{:S(2)}, u32[]{:S(2)}) %collective-permute-start.20) | collective-permute-done | bytes 262176 | tf_op jit(solution)/shard_map/ppermute | solution.py:24
  131.0 1.1 collective-permute-done.19
  132.1 1.7 collective-permute-done.18
  133.7 2.9 %collective-permute-start.21 = (bf16[64,1024]{1,0:T(8,128)(2,1)S(1)}, bf16[64,1024]{1,0:T(8,128)(2,1)S(1)}, u32[]{:S(2)}, u32[]{:S(2)}) collective-permute-start(bf16[64,1024]{1,0:T(8,128)(2,1)S(1)} %slice.236), channel_id=1, source_target_pairs={{0,64},{64,128},{128,192},{192,0},{1,65},{65,129},{129,193},{193,1... | collective-permute-start | bytes 393224 | tf_op jit(solution)/shard_map/ppermute | solution.py:24
  136.8 1.4 collective-permute-start.22
  138.2 4.0 %collective-permute-done.21 = bf16[64,1024]{1,0:T(8,128)(2,1)S(1)} collective-permute-done((bf16[64,1024]{1,0:T(8,128)(2,1)S(1)}, bf16[64,1024]{1,0:T(8,128)(2,1)S(1)}, u32[]{:S(2)}, u32[]{:S(2)}) %collective-permute-start.21) | collective-permute-done | bytes 131104 | tf_op jit(solution)/shard_map/ppermute | solution.py:24
  143.3 1.3 gram_tile.2.refs_0_
  144.7 1.1 collective-permute-done.23.right_ref
  145.8 2.5 %gram_tile.3 = bf16[8,2,128,256]{3,2,1,0:T(8,128)(2,1)} custom-call(s32[3]{0:T(128)S(1)} %pad_add_fusion.2.place, bf16[512,1024]{1,0:T(8,128)(2,1)S(1)} %constant_dynamic-update-slice_fusion.left_ref, bf16[512,1024]{1,0:T(8,128)(2,1)S(1)} %collective-permute-done.23.right_ref, bf16[8,2,128,128]{3,2,1,0:T(8,128)(2,1)S(1)} %gram_tile.2.refs_0_), custom_call_target="tpu_custom_call" | custom-call | flops 540000000 | bytes 3000000 | tf_op jit(solution)/shard_map/gram_tile/pallas_call | solution.py:196
  148.3 5.5 %all-to-all-start.1 = ((bf16[8,2,128,256]{3,2,1,0:T(8,128)(2,1)}), bf16[8,2,128,256]{3,2,1,0:T(8,128)(2,1)S(1)}, u32[]{:S(2)}, u32[]{:S(2)}) async-start(bf16[8,2,128,256]{3,2,1,0:T(8,128)(2,1)} %gram_tile.3), calls=%async_computation.1 | async-start | bytes 2097152 | tf_op jit(solution)/shard_map/all_to_all | solution.py:292
  153.8 13.9 %all-to-all-done.1 = bf16[8,2,128,256]{3,2,1,0:T(8,128)(2,1)S(1)} async-done(((bf16[8,2,128,256]{3,2,1,0:T(8,128)(2,1)}), bf16[8,2,128,256]{3,2,1,0:T(8,128)(2,1)S(1)}, u32[]{:S(2)}, u32[]{:S(2)}) %all-to-all-start.1) | async-done | bytes 1048608 | tf_op jit(solution)/shard_map/all_to_all | solution.py:292
  167.9 1.7 collective-permute-start.24
  169.6 2.9 %collective-permute-start.25 = (bf16[128,256]{1,0:T(8,128)(2,1)S(1)}, bf16[128,256]{1,0:T(8,128)(2,1)S(1)}, u32[]{:S(2)}, u32[]{:S(2)}) collective-permute-start(bf16[128,256]{1,0:T(8,128)(2,1)S(1)} %get-tuple-element.71), channel_id=1, source_target_pairs={{0,0},{1,16},{2,2},{3,18},{16,32},{17,48},{18,34},{19,50},{32,1},{... | collective-permute-start | bytes 196616 | tf_op jit(solution)/shard_map/ppermute | solution.py:301
  173.1 1.2 collective-permute-done.24
  174.3 3.8 %collective-permute-done.25 = bf16[128,256]{1,0:T(8,128)(2,1)S(1)} collective-permute-done((bf16[128,256]{1,0:T(8,128)(2,1)S(1)}, bf16[128,256]{1,0:T(8,128)(2,1)S(1)}, u32[]{:S(2)}, u32[]{:S(2)}) %collective-permute-start.25) | collective-permute-done | bytes 65568 | tf_op jit(solution)/shard_map/ppermute | solution.py:301
  (78 shorter events, 12.9 us)
Async XLA Ops:
  0.6 15.4 %copy-start.3 = (s32[1,4096]{1,0:T(1,128)S(1)}, s32[1,4096]{1,0:T(1,128)}, u32[]{:S(2)}) copy-start(s32[1,4096]{1,0:T(1,128)} %param.9) | copy-start | bytes 49156
  0.6 15.3 %copy-start.2 = (s32[4096]{0:T(1024)S(1)}, s32[4096]{0:T(1024)}, u32[]{:S(2)}) copy-start(s32[4096]{0:T(1024)} %param.7) | copy-start | bytes 49156
  0.7 15.2 %copy-start.1 = (s32[4096]{0:T(1024)S(1)}, s32[4096]{0:T(1024)}, u32[]{:S(2)}) copy-start(s32[4096]{0:T(1024)} %param.8) | copy-start | bytes 49156
  0.7 22.4 %collective-permute-start.1 = (bf16[4096,1024]{1,0:T(8,128)(2,1)}, bf16[4096,1024]{1,0:T(8,128)(2,1)}, u32[]{:S(2)}, u32[]{:S(2)}) collective-permute-start(bf16[4096,1024]{1,0:T(8,128)(2,1)} %own_ref.1), channel_id=1, source_target_pairs={{0,8},{8,0},{1,9},{9,1},{2,10},{10,2},{3,11},{11,3},{4,12},{12,4},... | collective-permute-start | bytes 25165832 | tf_op jit(solution)/shard_map/ppermute | solution.py:24
  1.6 14.4 %collective-permute-start = (s32[3,4096]{1,0:T(4,128)S(1)}, s32[3,4096]{1,0:T(4,128)S(1)}, u32[]{:S(2)}, u32[]{:S(2)}) collective-permute-start(s32[3,4096]{1,0:T(4,128)S(1)} %pad_add_fusion), channel_id=1, source_target_pairs={{0,8},{8,0},{1,9},{9,1},{2,10},{10,2},{3,11},{11,3},{4,12},{12,4},... | collective-permute-start | bytes 147464 | tf_op jit(solution)/shard_map/ppermute | solution.py:24
  9.5 12.8 %all-to-all-start = ((f32[16,32,128]{2,1,0:T(8,128)}), f32[16,32,128]{2,1,0:T(8,128)S(1)}, u32[]{:S(2)}, u32[]{:S(2)}) async-start(f32[16,32,128]{2,1,0:T(8,128)} %margin_parts.1), calls=%async_computation | async-start | bytes 524288 | tf_op jit(solution)/shard_map/all_to_all | solution.py:228
  44.3 16.2 %collective-permute-start.2 = (bf16[4,32,16,128]{3,2,1,0:T(8,128)(2,1)}, bf16[4,32,16,128]{3,2,1,0:T(8,128)(2,1)S(1)}, u32[]{:S(2)}, u32[]{:S(2)}) collective-permute-start(bf16[4,32,16,128]{3,2,1,0:T(8,128)(2,1)} %bitcast.97), channel_id=1, source_target_pairs={{0,16},{16,32},{32,48},{48,0},{1,17},{17,33},{33,49},{49,1},{2,18}... | collective-permute-start | bytes 1572872 | tf_op jit(solution)/shard_map/ppermute | solution.py:24
  45.9 15.0 %collective-permute-start.3 = (bf16[4,32,16,128]{3,2,1,0:T(8,128)(2,1)}, bf16[4,32,16,128]{3,2,1,0:T(8,128)(2,1)S(1)}, u32[]{:S(2)}, u32[]{:S(2)}) collective-permute-start(bf16[4,32,16,128]{3,2,1,0:T(8,128)(2,1)} %bitcast.96), channel_id=1, source_target_pairs={{0,48},{16,0},{32,16},{48,32},{1,49},{17,1},{33,17},{49,33},{2,50}... | collective-permute-start | bytes 1572872 | tf_op jit(solution)/shard_map/ppermute | solution.py:24
  48.4 6.5 %collective-permute-start.4 = (f32[8,128]{1,0:T(8,128)S(1)}, f32[8,128]{1,0:T(8,128)S(1)}, u32[]{:S(2)}, u32[]{:S(2)}) collective-permute-start(f32[8,128]{1,0:T(8,128)S(1)} %bitcast.92), channel_id=1, source_target_pairs={{0,64},{64,0},{128,192},{192,128},{1,65},{65,1},{129,193},{193,129... | collective-permute-start | bytes 12296 | tf_op jit(solution)/shard_map/ppermute | solution.py:253
  51.6 23.0 %collective-permute-start.6 = (bf16[4,32,16,128]{3,2,1,0:T(8,128)(2,1)}, bf16[4,32,16,128]{3,2,1,0:T(8,128)(2,1)S(1)}, u32[]{:S(2)}, u32[]{:S(2)}) collective-permute-start(bf16[4,32,16,128]{3,2,1,0:T(8,128)(2,1)} %bitcast.95), channel_id=1, source_target_pairs={{0,16},{16,32},{32,48},{48,0},{1,17},{17,33},{33,49},{49,1},{2,18}... | collective-permute-start | bytes 1572872 | tf_op jit(solution)/shard_map/ppermute | solution.py:24
  51.9 22.8 %collective-permute-start.7 = (bf16[4,32,16,128]{3,2,1,0:T(8,128)(2,1)}, bf16[4,32,16,128]{3,2,1,0:T(8,128)(2,1)S(1)}, u32[]{:S(2)}, u32[]{:S(2)}) collective-permute-start(bf16[4,32,16,128]{3,2,1,0:T(8,128)(2,1)} %bitcast.94), channel_id=1, source_target_pairs={{0,48},{16,0},{32,16},{48,32},{1,49},{17,1},{33,17},{49,33},{2,50}... | collective-permute-start | bytes 1572872 | tf_op jit(solution)/shard_map/ppermute | solution.py:24
  62.0 20.4 %collective-permute-start.5 = (bf16[4,32,16,128]{3,2,1,0:T(8,128)(2,1)S(1)}, bf16[4,32,16,128]{3,2,1,0:T(8,128)(2,1)S(1)}, u32[]{:S(2)}, u32[]{:S(2)}) collective-permute-start(bf16[4,32,16,128]{3,2,1,0:T(8,128)(2,1)S(1)} %fusion.1), channel_id=1, source_target_pairs={{0,16},{16,32},{32,48},{48,0},{1,17},{17,33},{33,49},{49,1},{2,18}... | collective-permute-start | bytes 1572872 | tf_op jit(solution)/shard_map/ppermute | solution.py:24
  64.8 18.7 %collective-permute-start.9 = (bf16[4,32,16,128]{3,2,1,0:T(8,128)(2,1)S(1)}, bf16[4,32,16,128]{3,2,1,0:T(8,128)(2,1)S(1)}, u32[]{:S(2)}, u32[]{:S(2)}) collective-permute-start(bf16[4,32,16,128]{3,2,1,0:T(8,128)(2,1)S(1)} %fusion), channel_id=1, source_target_pairs={{0,48},{16,0},{32,16},{48,32},{1,49},{17,1},{33,17},{49,33},{2,50}... | collective-permute-start | bytes 1572872 | tf_op jit(solution)/shard_map/ppermute | solution.py:24
  66.8 7.9 %collective-permute-start.8 = (f32[8,128]{1,0:T(8,128)S(1)}, f32[8,128]{1,0:T(8,128)S(1)}, u32[]{:S(2)}, u32[]{:S(2)}) collective-permute-start(f32[8,128]{1,0:T(8,128)S(1)} %add.300), channel_id=1, source_target_pairs={{0,128},{64,192},{128,0},{192,64},{1,129},{65,193},{129,1},{193,65... | collective-permute-start | bytes 12296 | tf_op jit(solution)/shard_map/ppermute | solution.py:253
  84.6 16.8 %collective-permute-start.10 = (bf16[2,32,16,128]{3,2,1,0:T(8,128)(2,1)S(1)}, bf16[2,32,16,128]{3,2,1,0:T(8,128)(2,1)S(1)}, u32[]{:S(2)}, u32[]{:S(2)}) collective-permute-start(bf16[2,32,16,128]{3,2,1,0:T(8,128)(2,1)S(1)} %pad_maximum_fusion), channel_id=1, source_target_pairs={{0,64},{64,128},{128,192},{192,0},{1,65},{65,129},{129,193},{193,1... | collective-permute-start | bytes 786440 | tf_op jit(solution)/shard_map/ppermute | solution.py:24
  88.0 13.5 %collective-permute-start.11 = (bf16[2,32,16,128]{3,2,1,0:T(8,128)(2,1)S(1)}, bf16[2,32,16,128]{3,2,1,0:T(8,128)(2,1)S(1)}, u32[]{:S(2)}, u32[]{:S(2)}) collective-permute-start(bf16[2,32,16,128]{3,2,1,0:T(8,128)(2,1)S(1)} %pad_maximum_fusion.1), channel_id=1, source_target_pairs={{0,192},{64,0},{128,64},{192,128},{1,193},{65,1},{129,65},{193,129... | collective-permute-start | bytes 786440 | tf_op jit(solution)/shard_map/ppermute | solution.py:24
  90.2 3.6 %collective-permute-start.12 = (f32[8,128]{1,0:T(8,128)S(1)}, f32[8,128]{1,0:T(8,128)S(1)}, u32[]{:S(2)}, u32[]{:S(2)}) collective-permute-start(f32[8,128]{1,0:T(8,128)S(1)} %add.303), channel_id=1, source_target_pairs={{0,16},{16,0},{32,48},{48,32},{1,17},{17,1},{33,49},{49,33},{2,18}... | collective-permute-start | bytes 12296 | tf_op jit(solution)/shard_map/ppermute | solution.py:253
  102.5 8.1 %collective-permute-start.13 = (bf16[32,16,128]{2,1,0:T(8,128)(2,1)S(1)}, bf16[32,16,128]{2,1,0:T(8,128)(2,1)S(1)}, u32[]{:S(2)}, u32[]{:S(2)}) collective-permute-start(bf16[32,16,128]{2,1,0:T(8,128)(2,1)S(1)} %fusion.6), channel_id=1, source_target_pairs={{0,64},{64,128},{128,192},{192,0},{1,65},{65,129},{129,193},{193,1... | collective-permute-start | bytes 393224 | tf_op jit(solution)/shard_map/ppermute | solution.py:24
  107.2 6.2 %collective-permute-start.14 = (bf16[32,16,128]{2,1,0:T(8,128)(2,1)S(1)}, bf16[32,16,128]{2,1,0:T(8,128)(2,1)S(1)}, u32[]{:S(2)}, u32[]{:S(2)}) collective-permute-start(bf16[32,16,128]{2,1,0:T(8,128)(2,1)S(1)} %fusion.4), channel_id=1, source_target_pairs={{0,192},{64,0},{128,64},{192,128},{1,193},{65,1},{129,65},{193,129... | collective-permute-start | bytes 393224 | tf_op jit(solution)/shard_map/ppermute | solution.py:24
  115.6 63.3 %copy-start = (bf16[128,1024]{1,0:T(8,128)(2,1)}, bf16[128,1024]{1,0:T(8,128)(2,1)S(1)}, u32[]{:S(2)}) copy-start(bf16[128,1024]{1,0:T(8,128)(2,1)S(1)} %convert_element_type.358) | copy-start | bytes 786436
  115.6 5.2 %collective-permute-start.15 = (f32[8,128]{1,0:T(8,128)S(1)}, f32[8,128]{1,0:T(8,128)S(1)}, u32[]{:S(2)}, u32[]{:S(2)}) collective-permute-start(f32[8,128]{1,0:T(8,128)S(1)} %add.314), channel_id=1, source_target_pairs={{0,32},{16,48},{32,0},{48,16},{1,33},{17,49},{33,1},{49,17},{2,34}... | collective-permute-start | bytes 12296 | tf_op jit(solution)/shard_map/ppermute | solution.py:253
  117.5 7.7 %collective-permute-start.17 = (bf16[128,1024]{1,0:T(8,128)(2,1)S(1)}, bf16[128,1024]{1,0:T(8,128)(2,1)S(1)}, u32[]{:S(2)}, u32[]{:S(2)}) collective-permute-start(bf16[128,1024]{1,0:T(8,128)(2,1)S(1)} %convert_element_type.358), channel_id=1, source_target_pairs={{0,192},{64,0},{128,64},{192,128},{1,193},{65,1},{129,65},{193,129... | collective-permute-start | bytes 786440 | tf_op jit(solution)/shard_map/ppermute | solution.py:24
  120.0 8.6 %collective-permute-start.16 = (bf16[128,1024]{1,0:T(8,128)(2,1)S(1)}, bf16[128,1024]{1,0:T(8,128)(2,1)S(1)}, u32[]{:S(2)}, u32[]{:S(2)}) collective-permute-start(bf16[128,1024]{1,0:T(8,128)(2,1)S(1)} %convert_element_type.358), channel_id=1, source_target_pairs={{0,64},{64,128},{128,192},{192,0},{1,65},{65,129},{129,193},{193,1... | collective-permute-start | bytes 786440 | tf_op jit(solution)/shard_map/ppermute | solution.py:24
  120.8 10.2 %collective-permute-start.20 = (bf16[128,1024]{1,0:T(8,128)(2,1)S(1)}, bf16[128,1024]{1,0:T(8,128)(2,1)S(1)}, u32[]{:S(2)}, u32[]{:S(2)}) collective-permute-start(bf16[128,1024]{1,0:T(8,128)(2,1)S(1)} %convert_element_type.358), channel_id=1, source_target_pairs={{0,32},{16,48},{32,0},{48,16},{1,33},{17,49},{33,1},{49,17},{2,34}... | collective-permute-start | bytes 786440 | tf_op jit(solution)/shard_map/ppermute | solution.py:24
  122.6 9.5 %collective-permute-start.19 = (bf16[128,1024]{1,0:T(8,128)(2,1)S(1)}, bf16[128,1024]{1,0:T(8,128)(2,1)S(1)}, u32[]{:S(2)}, u32[]{:S(2)}) collective-permute-start(bf16[128,1024]{1,0:T(8,128)(2,1)S(1)} %convert_element_type.358), channel_id=1, source_target_pairs={{0,48},{16,0},{32,16},{48,32},{1,49},{17,1},{33,17},{49,33},{2,50}... | collective-permute-start | bytes 786440 | tf_op jit(solution)/shard_map/ppermute | solution.py:24
  123.7 10.0 %collective-permute-start.18 = (bf16[128,1024]{1,0:T(8,128)(2,1)S(1)}, bf16[128,1024]{1,0:T(8,128)(2,1)S(1)}, u32[]{:S(2)}, u32[]{:S(2)}) collective-permute-start(bf16[128,1024]{1,0:T(8,128)(2,1)S(1)} %convert_element_type.358), channel_id=1, source_target_pairs={{0,16},{16,32},{32,48},{48,0},{1,17},{17,33},{33,49},{49,1},{2,18}... | collective-permute-start | bytes 786440 | tf_op jit(solution)/shard_map/ppermute | solution.py:24
  133.7 8.4 %collective-permute-start.21 = (bf16[64,1024]{1,0:T(8,128)(2,1)S(1)}, bf16[64,1024]{1,0:T(8,128)(2,1)S(1)}, u32[]{:S(2)}, u32[]{:S(2)}) collective-permute-start(bf16[64,1024]{1,0:T(8,128)(2,1)S(1)} %slice.236), channel_id=1, source_target_pairs={{0,64},{64,128},{128,192},{192,0},{1,65},{65,129},{129,193},{193,1... | collective-permute-start | bytes 393224 | tf_op jit(solution)/shard_map/ppermute | solution.py:24
  136.8 6.0 %collective-permute-start.22 = (bf16[64,1024]{1,0:T(8,128)(2,1)S(1)}, bf16[64,1024]{1,0:T(8,128)(2,1)S(1)}, u32[]{:S(2)}, u32[]{:S(2)}) collective-permute-start(bf16[64,1024]{1,0:T(8,128)(2,1)S(1)} %slice.237), channel_id=1, source_target_pairs={{0,192},{64,0},{128,64},{192,128},{1,193},{65,1},{129,65},{193,129... | collective-permute-start | bytes 393224 | tf_op jit(solution)/shard_map/ppermute | solution.py:24
  142.9 3.0 %collective-permute-start.23 = (bf16[512,1024]{1,0:T(8,128)(2,1)S(1)}, bf16[512,1024]{1,0:T(8,128)(2,1)S(1)}, u32[]{:S(2)}, u32[]{:S(2)}) collective-permute-start(bf16[512,1024]{1,0:T(8,128)(2,1)S(1)} %constant_dynamic-update-slice_fusion.4.right_ref), channel_id=1, source_target_pairs={{0,8},{8,0},{1,9},{9,1},{2,10},{10,2},{3,11},{11,3},{4,12},{12,4},... | collective-permute-start | bytes 3145736 | tf_op jit(solution)/shard_map/ppermute | solution.py:24
  148.3 19.4 %all-to-all-start.1 = ((bf16[8,2,128,256]{3,2,1,0:T(8,128)(2,1)}), bf16[8,2,128,256]{3,2,1,0:T(8,128)(2,1)S(1)}, u32[]{:S(2)}, u32[]{:S(2)}) async-start(bf16[8,2,128,256]{3,2,1,0:T(8,128)(2,1)} %gram_tile.3), calls=%async_computation.1 | async-start | bytes 2097152 | tf_op jit(solution)/shard_map/all_to_all | solution.py:292
  167.9 6.5 %collective-permute-start.24 = (bf16[128,256]{1,0:T(8,128)(2,1)S(1)}, bf16[128,256]{1,0:T(8,128)(2,1)S(1)}, u32[]{:S(2)}, u32[]{:S(2)}) collective-permute-start(bf16[128,256]{1,0:T(8,128)(2,1)S(1)} %get-tuple-element.70), channel_id=1, source_target_pairs={{0,32},{1,48},{2,34},{3,50},{16,0},{17,16},{18,2},{19,18},{32,33},... | collective-permute-start | bytes 196616 | tf_op jit(solution)/shard_map/ppermute | solution.py:301
  169.6 8.6 %collective-permute-start.25 = (bf16[128,256]{1,0:T(8,128)(2,1)S(1)}, bf16[128,256]{1,0:T(8,128)(2,1)S(1)}, u32[]{:S(2)}, u32[]{:S(2)}) collective-permute-start(bf16[128,256]{1,0:T(8,128)(2,1)S(1)} %get-tuple-element.71), channel_id=1, source_target_pairs={{0,0},{1,16},{2,2},{3,18},{16,32},{17,48},{18,34},{19,50},{32,1},{... | collective-permute-start | bytes 196616 | tf_op jit(solution)/shard_map/ppermute | solution.py:301

commit v3 on v2

--- a/solution.py
+++ b/solution.py
@@ -14,9 +14,8 @@
 GROUP = 256
 LANE_TILES = COLS // 128
 HALF_PAIRS = 32
-UNROLL = 16
+SPLIT = 1
 EXTRA = 16
-MARGIN_ROWS = 1024
 
 
 def ring(axis_name, value, shift):
@@ -24,47 +23,23 @@
     return lax.ppermute(value, axis_name, [(i, (i + shift) % size) for i in range(size)])
 
 
-def margin_kernel(rows_ref, coef_ref, out):
-    step = pl.program_id(0)
-    sums = lax.dot_general(
-        coef_ref[...], rows_ref[...], (((1,), (1,)), ((), ())), preferred_element_type=jnp.float32
-    )
-    for part in range(MARGIN_ROWS // 128):
-        out[:, pl.ds(step * (MARGIN_ROWS // 128) + part, 1), :] = sums[:, part * 128 : (part + 1) * 128].reshape(
-            16, 1, 128
-        )
-
-
-def margin_parts(features, coef):
-    return pl.pallas_call(
-        margin_kernel,
-        grid=(ROWS // MARGIN_ROWS,),
-        in_specs=[
-            pl.BlockSpec((MARGIN_ROWS, COLS), lambda i: (i, 0)),
-            pl.BlockSpec((16, COLS), lambda i: (0, 0)),
-        ],
-        out_specs=pl.BlockSpec((16, ROWS // 128, 128), lambda i: (0, 0, 0)),
-        out_shape=jax.ShapeDtypeStruct((16, ROWS // 128, 128), jnp.float32),
-        compiler_params=pltpu.CompilerParams(vmem_limit_bytes=60 * 1024 * 1024),
-        cost_estimate=pl.CostEstimate(flops=130_000_000, bytes_accessed=9_000_000, transcendentals=0),
-        name="margin_parts",
-    )(features, jnp.broadcast_to(coef, (16, COLS)))
-
-
-def sketch_kernel(spots, own_ref, other_ref, factor_ref, residual_ref, *refs):
+def sketch_kernel(spots, *refs):
+    own_refs, other_refs, (factor_ref, residual_ref) = refs[:SPLIT], refs[SPLIT : 2 * SPLIT], refs[2 * SPLIT : 2 * SPLIT + 2]
+    refs = refs[2 * SPLIT + 2 :]
     outs, (gradient, table_rows, own_pass, other_pass, transformed) = refs[:8], refs[8:]
     step = pl.program_id(0)
     last = COLS // GROUP
 
     def multiply(block, high):
-        source, target = ((own_ref, own_pass), (other_ref, other_pass))[block]
+        sources, target = ((own_refs, own_pass), (other_refs, other_pass))[block]
+        share = HIGH // SPLIT
         product = jnp.dot(
             table_rows[block * HIGH + high],
-            source[pl.ds(pl.multiple_of(high * LOW, LOW), LOW), :],
+            sources[high // share][high % share * LOW : (high % share + 1) * LOW, :],
             preferred_element_type=jnp.float32,
         )
         target[high] = product[:LOW]
-        gradient[step] += product[LOW : LOW + 8]
+        return product[LOW : LOW + 8]
 
     def combine(block, group, tile_row):
         source = (own_pass, other_pass)[block]
@@ -83,15 +58,15 @@
                 transformed[block, pl.ds(pl.multiple_of(high * (LOW * 8) + place, 8), 8), :] = values[high]
 
     def run(multiplied, combined):
-        def body(high, carry):
+        extra = []
+        for high in range(HIGH):
             if multiplied is not None:
-                multiply(multiplied, high)
+                extra.append(multiply(multiplied, high))
             if combined is not None:
                 for tile in range(LOW // 8 // HIGH):
                     combine(*combined, high * (LOW // 8 // HIGH) + tile)
-            return carry
-
-        lax.fori_loop(0, HIGH, body, 0, unroll=UNROLL)
+        if extra:
+            gradient[step] += sum(extra[1:], extra[0])
 
     @pl.when(step == 0)
     def _():
@@ -133,7 +108,7 @@
                 out[pair] = jnp.concatenate(rows, axis=0).astype(jnp.bfloat16)
                 return carry
 
-            lax.fori_loop(0, pairs, pick, 0, unroll=16)
+            lax.fori_loop(0, pairs, pick, 0, unroll=32)
             start += 2 * pairs
 
 
@@ -146,8 +121,11 @@
             num_scalar_prefetch=1,
             grid=(last + 2,),
             in_specs=[
-                pl.BlockSpec((ROWS, GROUP), lambda i, s: (0, jnp.minimum(i, last))),
-                pl.BlockSpec((ROWS, GROUP), lambda i, s: (0, jnp.minimum(i, last))),
+                *[
+                    pl.BlockSpec((ROWS // SPLIT, GROUP), lambda i, s, part=part: (part, jnp.minimum(i, last)))
+                    for part in range(SPLIT)
+                ]
+                * 2,
                 pl.BlockSpec((2 * HIGH, LOW), lambda i, s: (0, 0)),
                 pl.BlockSpec((2 * HIGH, LOW), lambda i, s: (0, 0)),
             ],
@@ -165,7 +143,7 @@
         compiler_params=pltpu.CompilerParams(vmem_limit_bytes=62 * 1024 * 1024),
         cost_estimate=pl.CostEstimate(flops=4_400_000_000, bytes_accessed=22_000_000, transcendentals=0),
         name="hadamard_pick",
-    )(spots, own, other, factors, residuals)
+    )(spots, *[own] * SPLIT, *[other] * SPLIT, factors, residuals)
 
 
 def gram_kernel(place, left_ref, right_ref, *refs):
@@ -225,10 +203,17 @@
     integers = jnp.concatenate([samples, sign_bits[None], labels[None]], axis=0)
     other_integers = ring("c", integers, 1)
 
-    everyone = lax.all_to_all(margin_parts(features, coef), ("c", "zl", "y"), 0, 0).reshape(2, 8, 32, 128)
-    by_core = [sum(everyone[core, k] for k in range(8)) for core in range(2)]
-    margins = jnp.where(my_c == 0, by_core[0], by_core[1])
-    other_margins = jnp.where(my_c == 0, by_core[1], by_core[0])
+    partial_value = jnp.dot(features, coef, preferred_element_type=jnp.float32).reshape(32, 128)
+    partial_sum = partial_value
+    for shift in (1, 2, 3):
+        partial_sum = partial_sum + ring("y", partial_value, shift)
+    pairs = [(c * 2 + l, c, l) for c in range(2) for l in range(2)]
+
+    def swap(flip_c, flip_l):
+        return lax.ppermute(partial_sum, ("c", "zl"), [(i, (c ^ flip_c) * 2 + (l ^ flip_l)) for i, c, l in pairs])
+
+    margins = partial_sum + swap(0, 1)
+    other_margins = swap(1, 0) + swap(1, 1)
 
     def row_terms(value, bits, targets):
         probability = jax.nn.sigmoid(value)
@@ -265,14 +250,15 @@
         for a in range(4)
     ]
     short = [[half.astype(jnp.bfloat16) for half in pair] for pair in wide]
-    from_last = ring("zh", jnp.stack([short[2][0], short[1][1]]), 1)
-    from_next = ring("zh", jnp.stack([short[2][1], short[3][0]]), -1)
+    end_far_0, end_far_1 = ring("zh", short[2][0], 1), ring("zh", short[2][1], -1)
+    end_after_1, end_before_0 = ring("zh", short[1][1], 1), ring("zh", short[3][0], -1)
+    end_far_0, end_far_1 = lax.optimization_barrier((end_far_0, end_far_1))
+    end_after_0 = ring("zh", narrow(short[1][0], end_far_0), 1)
+    end_before_1 = ring("zh", narrow(short[3][1], end_far_1), -1)
     gradient = swap_add("x", 1, gradient)
-    from_last, from_next, gradient = lax.optimization_barrier((from_last, from_next, gradient))
-    end_0 = ring("zh", narrow(short[1][0], from_last[0]), 1)
-    end_1 = ring("zh", narrow(short[3][1], from_next[0]), -1)
-    end_0, end_1 = lax.optimization_barrier((end_0, end_1))
-    summed = [add_up(wide[0][0], from_next[1], end_0), add_up(wide[0][1], from_last[1], end_1)]
+    end_after_1, end_before_0, gradient = lax.optimization_barrier((end_after_1, end_before_0, gradient))
+    end_after_0, end_before_1 = lax.optimization_barrier((end_after_0, end_before_1))
+    summed = [add_up(wide[0][0], end_before_0, end_after_0), add_up(wide[0][1], end_after_1, end_before_1)]
     summed = jnp.concatenate(summed, axis=0).reshape(128, COLS)
     sketch = (summed / root_total).astype(jnp.bfloat16)
 
@@ -280,10 +266,12 @@
     _, gradient = lax.optimization_barrier((sketch, gradient))
     gradient = swap_add("x", 2, gradient)
     for_x, gradient = lax.optimization_barrier((sketch, gradient))
-    x_next, x_far, x_last = (ring("x", for_x, shift) for shift in (-1, 2, 1))
-    zh_last, zh_next, x_last, x_next, x_far = lax.optimization_barrier((zh_last, zh_next, x_last, x_next, x_far))
+    x_last, x_next = ring("x", for_x, 1), ring("x", for_x, -1)
+    zh_last, zh_next, x_last, x_next = lax.optimization_barrier((zh_last, zh_next, x_last, x_next))
     zh_far_0, zh_far_1 = ring("zh", zh_last[:64], 1), ring("zh", zh_next[64:], -1)
-    left = jnp.concatenate([sketch, x_next, x_far, x_last], axis=0)
+    x_far_0, x_far_1 = ring("x", x_last[:64], 1), ring("x", x_next[64:], -1)
+    zh_far_0, zh_far_1, x_far_0, x_far_1 = lax.optimization_barrier((zh_far_0, zh_far_1, x_far_0, x_far_1))
+    left = jnp.concatenate([sketch, x_next, x_far_0, x_far_1, x_last], axis=0)
     own_rows = jnp.concatenate([sketch, zh_next, zh_far_0, zh_far_1, zh_last], axis=0)
     other_rows = ring("c", own_rows, 1)
     place = jnp.stack([my_zh, my_x, my_c]).astype(jnp.int32)

time: 180 us -> 180 us (level)
  starting transfers between devices: 60.2 us -> 69.2 us
  Pallas kernels: 31.2 us -> 24.8 us
  waiting for transfers between devices: 71.2 us -> 65.1 us
  matrix products: 0 us -> 5.64 us
    ppermute x20 -> x26, starting transfers between devices: 32 us -> 41 us  [ring(): lax.ppermute(value, axis_name, [(i, (i + shift) % size) for i in range(si...]
    all_to_all x1 -> x0, starting transfers between devices: 6.29 us -> none  [per_device(): lax.all_to_all(margin_parts(features, coef), ('c', 'zl', 'y'), 0, 0)]
    pallas_call x1 -> x0, Pallas kernels: 6.1 us -> none  [margin_parts(): pl.pallas_call(margin_kernel, grid=(ROWS // MARGIN_ROWS,), in_specs=[pl.B...]
    dot_general x0 -> x1, matrix products: none -> 5.64 us  [per_device(): jnp.dot(features, coef, preferred_element_type=jnp.float32).reshape(32, 128)]
    all_to_all x1 -> x0, waiting for transfers between devices: 5.19 us -> none  [per_device(): lax.all_to_all(margin_parts(features, coef), ('c', 'zl', 'y'), 0, 0)]
    ppermute x20 -> x26, waiting for transfers between devices: 41.9 us -> 39.4 us  [ring(): lax.ppermute(value, axis_name, [(i, (i + shift) % size) for i in range(si...]
    ppermute x0 -> x3, starting transfers between devices: none -> 2.33 us  [swap(): lax.ppermute(partial_sum, ('c', 'zl'), [(i, (c ^ flip_c) * 2 + (l ^ flip_...]
    ppermute x4, starting transfers between devices: 11.9 us -> 14 us  [swap_add(): lax.ppermute(value, axis_name, [(i, i ^ flip) for i in range(4)])]
  transfers between devices with their start and end apart: 28 -> 36, of which waited for: 22 -> 21; matrix products, arithmetic and copies ran while one was open for 6% -> 9% of each run, Pallas kernels for 4% -> 1%
where the time goes in v3:
time: 180 us; the launch traced here: 179 us
  starting transfers between devices  69.2 us (38%)
  waiting for transfers between devices  65.1 us (36%)
  Pallas kernels  24.8 us (14%)
  other arithmetic  10.7 us (6%)
  matrix products  5.64 us (3%)
  local copies, waits for them, and re-layouts  2.69 us (1%)
    ppermute x26, starting transfers between devices, ring(): lax.ppermute(value, axis_name, [(i, (i + shift) % size) for i in range(si...  41 us
    ppermute x26, waiting for transfers between devices, ring(): lax.ppermute(value, axis_name, [(i, (i + shift) % size) for i in range(si...  39.4 us
    pallas_call x1, Pallas kernels, sketch_pieces(): pl.pallas_call(sketch_kernel, grid_spec=pltpu.PrefetchScalarGridSpec(num_...  21 us
    ppermute x4, starting transfers between devices, swap_add(): lax.ppermute(value, axis_name, [(i, i ^ flip) for i in range(4)])  14 us
    all_to_all x1, waiting for transfers between devices, per_device(): parts = lax.all_to_all(tiles, ('zl', 'y'), 0, 0)  13.9 us
    all_to_all x1, starting transfers between devices, per_device(): parts = lax.all_to_all(tiles, ('zl', 'y'), 0, 0)  6.24 us
    ppermute x2, waiting for transfers between devices, deliver(): return lax.ppermute(over_feat[i], ('x', 'y'), moves).astype(jnp.float32)  6.04 us
    ppermute x2, starting transfers between devices, deliver(): return lax.ppermute(over_feat[i], ('x', 'y'), moves).astype(jnp.float32)  5.67 us
  transfers between devices with their start and end apart: 36, of which 21 were waited for; matrix products, arithmetic and copies ran while one was open for 9% of the time, Pallas kernels for 1%

profile of v3, /device:TPU:8, one launch (start us, length us, event | category | flops | bytes accessed | tf_op | source)
XLA Modules:
  0.0 179.3 jit_solution(9656887361418241523)
XLA Ops:
  1.5 5.6 %fusion.22 = f32[1,4096]{1,0:T(1,128)S(1)} fusion(bf16[4096,1024]{1,0:T(8,128)(2,1)} %refs_0_.1, bf16[1024,1]{0,1:T(2,128)(2,1)S(1)} %reshape.177), kind=kOutput, calls=%fused_computation.88 | convolution fusion | flops 8388608 | bytes 8407040 | tf_op jit(solution)/shard_map/dot_general | solution.py:206
  7.1 2.2 %collective-permute-start.4 = (f32[32,128]{1,0:T(8,128)S(1)}, f32[32,128]{1,0:T(8,128)S(1)}, u32[]{:S(2)}, u32[]{:S(2)}) collective-permute-start(f32[32,128]{1,0:T(8,128)S(1)} %bitcast.103), channel_id=1, source_target_pairs={{0,3},{1,0},{2,1},{3,2},{4,7},{5,4},{6,5},{7,6},{8,11},{9,8},{10,9... | collective-permute-start | bytes 49160 | tf_op jit(solution)/shard_map/ppermute | solution.py:23
  10.1 1.9 %collective-permute-start.2 = (f32[32,128]{1,0:T(8,128)S(1)}, f32[32,128]{1,0:T(8,128)S(1)}, u32[]{:S(2)}, u32[]{:S(2)}) collective-permute-start(f32[32,128]{1,0:T(8,128)S(1)} %bitcast.105), channel_id=1, source_target_pairs={{0,1},{1,2},{2,3},{3,0},{4,5},{5,6},{6,7},{7,4},{8,9},{9,10},{10,1... | collective-permute-start | bytes 49160 | tf_op jit(solution)/shard_map/ppermute | solution.py:23
  12.0 2.5 %collective-permute-done.3 = f32[32,128]{1,0:T(8,128)S(1)} collective-permute-done((f32[32,128]{1,0:T(8,128)S(1)}, f32[32,128]{1,0:T(8,128)S(1)}, u32[]{:S(2)}, u32[]{:S(2)}) %collective-permute-start.3) | collective-permute-done | bytes 16416 | tf_op jit(solution)/shard_map/ppermute | solution.py:23
  14.6 1.3 collective-permute-start.5
  17.1 1.3 collective-permute-done.5
  21.6 21.0 %hadamard_pick.1 = (bf16[128,16,128]{2,1,0:T(8,128)(2,1)}, bf16[128,16,128]{2,1,0:T(8,128)(2,1)}, bf16[128,16,128]{2,1,0:T(8,128)(2,1)}, bf16[128,16,128]{2,1,0:...) custom-call(s32[4096]{0:T(1024)} %add.172.spots, ...), custom_call_target="tpu_custom_call" | custom-call | flops 4400000000 | bytes 22000000 | tf_op jit(solution)/shard_map/hadamard_pick/pallas_call | solution.py:118
  42.6 1.5 collective-permute-start.8
  44.1 1.7 collective-permute-start.9
  46.6 3.3 %collective-permute-start.10 = (f32[8,128]{1,0:T(8,128)S(1)}, f32[8,128]{1,0:T(8,128)S(1)}, u32[]{:S(2)}, u32[]{:S(2)}) collective-permute-start(f32[8,128]{1,0:T(8,128)S(1)} %bitcast.111), channel_id=1, source_target_pairs={{0,64},{64,0},{128,192},{192,128},{1,65},{65,1},{129,193},{193,129... | collective-permute-start | bytes 12296 | tf_op jit(solution)/shard_map/ppermute | solution.py:238
  50.1 3.0 %collective-permute-start.13 = (bf16[4,32,16,128]{3,2,1,0:T(8,128)(2,1)}, bf16[4,32,16,128]{3,2,1,0:T(8,128)(2,1)S(1)}, u32[]{:S(2)}, u32[]{:S(2)}) collective-permute-start(bf16[4,32,16,128]{3,2,1,0:T(8,128)(2,1)} %bitcast.113), channel_id=1, source_target_pairs={{0,48},{16,0},{32,16},{48,32},{1,49},{17,1},{33,17},{49,33},{2,50}... | collective-permute-start | bytes 1572872 | tf_op jit(solution)/shard_map/ppermute | solution.py:23
  53.1 5.6 %collective-permute-done.8 = bf16[4,32,16,128]{3,2,1,0:T(8,128)(2,1)S(1)} collective-permute-done((bf16[4,32,16,128]{3,2,1,0:T(8,128)(2,1)}, bf16[4,32,16,128]{3,2,1,0:T(8,128)(2,1)S(1)}, u32[]{:S(2)}, u32[]{:S(2)}) %collective-permute-start.8) | collective-permute-done | bytes 524320 | tf_op jit(solution)/shard_map/ppermute | solution.py:23
  59.1 1.2 fusion
  60.3 3.0 %collective-permute-start.15 = (bf16[4,32,16,128]{3,2,1,0:T(8,128)(2,1)S(1)}, bf16[4,32,16,128]{3,2,1,0:T(8,128)(2,1)S(1)}, u32[]{:S(2)}, u32[]{:S(2)}) collective-permute-start(bf16[4,32,16,128]{3,2,1,0:T(8,128)(2,1)S(1)} %fusion), channel_id=1, source_target_pairs={{0,48},{16,0},{32,16},{48,32},{1,49},{17,1},{33,17},{49,33},{2,50}... | collective-permute-start | bytes 1572872 | tf_op jit(solution)/shard_map/ppermute | solution.py:23
  63.3 1.2 fusion.1
  64.6 6.4 %collective-permute-start.14 = (f32[8,128]{1,0:T(8,128)S(1)}, f32[8,128]{1,0:T(8,128)S(1)}, u32[]{:S(2)}, u32[]{:S(2)}) collective-permute-start(f32[8,128]{1,0:T(8,128)S(1)} %add.180), channel_id=1, source_target_pairs={{0,128},{64,192},{128,0},{192,64},{1,129},{65,193},{129,1},{193,65... | collective-permute-start | bytes 12296 | tf_op jit(solution)/shard_map/ppermute | solution.py:238
  70.9 1.6 collective-permute-done.14
  72.5 8.1 %collective-permute-done.15 = bf16[4,32,16,128]{3,2,1,0:T(8,128)(2,1)S(1)} collective-permute-done((bf16[4,32,16,128]{3,2,1,0:T(8,128)(2,1)S(1)}, bf16[4,32,16,128]{3,2,1,0:T(8,128)(2,1)S(1)}, u32[]{:S(2)}, u32[]{:S(2)}) %collective-permute-start.15) | collective-permute-done | bytes 524320 | tf_op jit(solution)/shard_map/ppermute | solution.py:23
  81.6 5.7 %collective-permute-start.20 = (bf16[32,16,128]{2,1,0:T(8,128)(2,1)S(1)}, bf16[32,16,128]{2,1,0:T(8,128)(2,1)S(1)}, u32[]{:S(2)}, u32[]{:S(2)}) collective-permute-start(bf16[32,16,128]{2,1,0:T(8,128)(2,1)S(1)} %fusion.6), channel_id=1, source_target_pairs={{0,192},{64,0},{128,64},{192,128},{1,193},{65,1},{129,65},{193,129... | collective-permute-start | bytes 393224 | tf_op jit(solution)/shard_map/ppermute | solution.py:23
  87.3 1.1 fusion.9
  88.5 4.1 %collective-permute-start.17 = (bf16[32,16,128]{2,1,0:T(8,128)(2,1)S(1)}, bf16[32,16,128]{2,1,0:T(8,128)(2,1)S(1)}, u32[]{:S(2)}, u32[]{:S(2)}) collective-permute-start(bf16[32,16,128]{2,1,0:T(8,128)(2,1)S(1)} %get-tuple-element.69), channel_id=1, source_target_pairs={{0,192},{64,0},{128,64},{192,128},{1,193},{65,1},{129,65},{193,129... | collective-permute-start | bytes 393224 | tf_op jit(solution)/shard_map/ppermute | solution.py:23
  92.6 4.6 %collective-permute-done.19 = bf16[32,16,128]{2,1,0:T(8,128)(2,1)S(1)} collective-permute-done((bf16[32,16,128]{2,1,0:T(8,128)(2,1)S(1)}, bf16[32,16,128]{2,1,0:T(8,128)(2,1)S(1)}, u32[]{:S(2)}, u32[]{:S(2)}) %collective-permute-start.19) | collective-permute-done | bytes 131104 | tf_op jit(solution)/shard_map/ppermute | solution.py:23
  97.2 1.1 fusion.10
  98.4 1.0 add_convert_fusion.2
  99.4 1.3 collective-permute-start.21
  100.7 2.9 %collective-permute-start.22 = (bf16[32,16,128]{2,1,0:T(8,128)(2,1)S(1)}, bf16[32,16,128]{2,1,0:T(8,128)(2,1)S(1)}, u32[]{:S(2)}, u32[]{:S(2)}) collective-permute-start(bf16[32,16,128]{2,1,0:T(8,128)(2,1)S(1)} %get-tuple-element.72), channel_id=1, source_target_pairs={{0,192},{64,0},{128,64},{192,128},{1,193},{65,1},{129,65},{193,129... | collective-permute-start | bytes 393224 | tf_op jit(solution)/shard_map/ppermute | solution.py:23
  103.6 1.5 collective-permute-start.18
  105.1 2.1 %collective-permute-done.18 = f32[8,128]{1,0:T(8,128)S(1)} collective-permute-done((f32[8,128]{1,0:T(8,128)S(1)}, f32[8,128]{1,0:T(8,128)S(1)}, u32[]{:S(2)}, u32[]{:S(2)}) %collective-permute-start.18) | collective-permute-done | bytes 4128 | tf_op jit(solution)/shard_map/ppermute | solution.py:238
  107.3 2.1 %collective-permute-done.16 = bf16[32,16,128]{2,1,0:T(8,128)(2,1)S(1)} collective-permute-done((bf16[32,16,128]{2,1,0:T(8,128)(2,1)S(1)}, bf16[32,16,128]{2,1,0:T(8,128)(2,1)S(1)}, u32[]{:S(2)}, u32[]{:S(2)}) %collective-permute-start.16) | collective-permute-done | bytes 131104 | tf_op jit(solution)/shard_map/ppermute | solution.py:23
  109.3 3.2 %collective-permute-done.21 = bf16[32,16,128]{2,1,0:T(8,128)(2,1)S(1)} collective-permute-done((bf16[32,16,128]{2,1,0:T(8,128)(2,1)S(1)}, bf16[32,16,128]{2,1,0:T(8,128)(2,1)S(1)}, u32[]{:S(2)}, u32[]{:S(2)}) %collective-permute-start.21) | collective-permute-done | bytes 131104 | tf_op jit(solution)/shard_map/ppermute | solution.py:23
  112.6 1.1 fusion.4
  113.9 2.8 %collective-permute-start.23 = (f32[8,128]{1,0:T(8,128)S(1)}, f32[8,128]{1,0:T(8,128)S(1)}, u32[]{:S(2)}, u32[]{:S(2)}) collective-permute-start(f32[8,128]{1,0:T(8,128)S(1)} %add.190), channel_id=1, source_target_pairs={{0,32},{16,48},{32,0},{48,16},{1,33},{17,49},{33,1},{49,17},{2,34}... | collective-permute-start | bytes 12296 | tf_op jit(solution)/shard_map/ppermute | solution.py:238
  116.7 2.9 %collective-permute-start.24 = (bf16[128,1024]{1,0:T(8,128)(2,1)S(1)}, bf16[128,1024]{1,0:T(8,128)(2,1)S(1)}, u32[]{:S(2)}, u32[]{:S(2)}) collective-permute-start(bf16[128,1024]{1,0:T(8,128)(2,1)S(1)} %convert_element_type.338), channel_id=1, source_target_pairs={{0,64},{64,128},{128,192},{192,0},{1,65},{65,129},{129,193},{193,1... | collective-permute-start | bytes 786440 | tf_op jit(solution)/shard_map/ppermute | solution.py:23
  119.7 2.4 %collective-permute-start.27 = (bf16[128,1024]{1,0:T(8,128)(2,1)S(1)}, bf16[128,1024]{1,0:T(8,128)(2,1)S(1)}, u32[]{:S(2)}, u32[]{:S(2)}) collective-permute-start(bf16[128,1024]{1,0:T(8,128)(2,1)S(1)} %convert_element_type.338), channel_id=1, source_target_pairs={{0,48},{16,0},{32,16},{48,32},{1,49},{17,1},{33,17},{49,33},{2,50}... | collective-permute-start | bytes 786440 | tf_op jit(solution)/shard_map/ppermute | solution.py:23
  122.1 7.4 %collective-permute-done.25 = bf16[128,1024]{1,0:T(8,128)(2,1)S(1)} collective-permute-done((bf16[128,1024]{1,0:T(8,128)(2,1)S(1)}, bf16[128,1024]{1,0:T(8,128)(2,1)S(1)}, u32[]{:S(2)}, u32[]{:S(2)}) %collective-permute-start.25) | collective-permute-done | bytes 262176 | tf_op jit(solution)/shard_map/ppermute | solution.py:23
  129.5 1.5 collective-permute-done.24
  131.2 1.3 collective-permute-start.30
  133.0 2.4 %collective-permute-start.28 = (bf16[64,1024]{1,0:T(8,128)(2,1)S(1)}, bf16[64,1024]{1,0:T(8,128)(2,1)S(1)}, u32[]{:S(2)}, u32[]{:S(2)}) collective-permute-start(bf16[64,1024]{1,0:T(8,128)(2,1)S(1)} %slice.162), channel_id=1, source_target_pairs={{0,64},{64,128},{128,192},{192,0},{1,65},{65,129},{129,193},{193,1... | collective-permute-start | bytes 393224 | tf_op jit(solution)/shard_map/ppermute | solution.py:23
  135.4 2.0 %collective-permute-start.31 = (bf16[64,1024]{1,0:T(8,128)(2,1)S(1)}, bf16[64,1024]{1,0:T(8,128)(2,1)S(1)}, u32[]{:S(2)}, u32[]{:S(2)}) collective-permute-start(bf16[64,1024]{1,0:T(8,128)(2,1)S(1)} %slice.165), channel_id=1, source_target_pairs={{0,48},{16,0},{32,16},{48,32},{1,49},{17,1},{33,17},{49,33},{2,50}... | collective-permute-start | bytes 393224 | tf_op jit(solution)/shard_map/ppermute | solution.py:23
  138.3 1.8 collective-permute-done.28
  140.9 1.3 gram_tile.2.refs_0_
  142.3 1.1 collective-permute-done.32.right_ref
  143.4 2.5 %gram_tile.3 = bf16[8,2,128,256]{3,2,1,0:T(8,128)(2,1)} custom-call(s32[3]{0:T(128)S(1)} %pad_add_fusion.2.place, bf16[512,1024]{1,0:T(8,128)(2,1)S(1)} %constant_dynamic-update-slice_fusion.left_ref, bf16[512,1024]{1,0:T(8,128)(2,1)S(1)} %collective-permute-done.32.right_ref, bf16[8,2,128,128]{3,2,1,0:T(8,128)(2,1)S(1)} %gram_tile.2.refs_0_), custom_call_target="tpu_custom_call" | custom-call | flops 540000000 | bytes 3000000 | tf_op jit(solution)/shard_map/gram_tile/pallas_call | solution.py:174
  145.9 6.2 %all-to-all-start = ((bf16[8,2,128,256]{3,2,1,0:T(8,128)(2,1)}), bf16[8,2,128,256]{3,2,1,0:T(8,128)(2,1)S(1)}, u32[]{:S(2)}, u32[]{:S(2)}) async-start(bf16[8,2,128,256]{3,2,1,0:T(8,128)(2,1)} %gram_tile.3), calls=%async_computation | async-start | bytes 2097152 | tf_op jit(solution)/shard_map/all_to_all | solution.py:280
  152.1 13.9 %all-to-all-done = bf16[8,2,128,256]{3,2,1,0:T(8,128)(2,1)S(1)} async-done(((bf16[8,2,128,256]{3,2,1,0:T(8,128)(2,1)}), bf16[8,2,128,256]{3,2,1,0:T(8,128)(2,1)S(1)}, u32[]{:S(2)}, u32[]{:S(2)}) %all-to-all-start) | async-done | bytes 1048608 | tf_op jit(solution)/shard_map/all_to_all | solution.py:280
  166.2 3.8 %collective-permute-start.33 = (bf16[128,256]{1,0:T(8,128)(2,1)S(1)}, bf16[128,256]{1,0:T(8,128)(2,1)S(1)}, u32[]{:S(2)}, u32[]{:S(2)}) collective-permute-start(bf16[128,256]{1,0:T(8,128)(2,1)S(1)} %get-tuple-element.75), channel_id=1, source_target_pairs={{0,32},{1,48},{2,34},{3,50},{16,0},{17,16},{18,2},{19,18},{32,33},... | collective-permute-start | bytes 196616 | tf_op jit(solution)/shard_map/ppermute | solution.py:289
  170.0 1.9 %collective-permute-start.34 = (bf16[128,256]{1,0:T(8,128)(2,1)S(1)}, bf16[128,256]{1,0:T(8,128)(2,1)S(1)}, u32[]{:S(2)}, u32[]{:S(2)}) collective-permute-start(bf16[128,256]{1,0:T(8,128)(2,1)S(1)} %get-tuple-element.76), channel_id=1, source_target_pairs={{0,0},{1,16},{2,2},{3,18},{16,32},{17,48},{18,34},{19,50},{32,1},{... | collective-permute-start | bytes 196616 | tf_op jit(solution)/shard_map/ppermute | solution.py:289
  172.7 5.9 %collective-permute-done.34 = bf16[128,256]{1,0:T(8,128)(2,1)S(1)} collective-permute-done((bf16[128,256]{1,0:T(8,128)(2,1)S(1)}, bf16[128,256]{1,0:T(8,128)(2,1)S(1)}, u32[]{:S(2)}, u32[]{:S(2)}) %collective-permute-start.34) | collective-permute-done | bytes 65568 | tf_op jit(solution)/shard_map/ppermute | solution.py:289
  (90 shorter events, 12.7 us)
Async XLA Ops:
  0.6 15.2 %copy-start.3 = (s32[1,4096]{1,0:T(1,128)S(1)}, s32[1,4096]{1,0:T(1,128)}, u32[]{:S(2)}) copy-start(s32[1,4096]{1,0:T(1,128)} %param.9) | copy-start | bytes 49156
  0.6 15.2 %copy-start.1 = (s32[4096]{0:T(1024)S(1)}, s32[4096]{0:T(1024)}, u32[]{:S(2)}) copy-start(s32[4096]{0:T(1024)} %param.7) | copy-start | bytes 49156
  0.7 15.2 %copy-start.2 = (s32[4096]{0:T(1024)S(1)}, s32[4096]{0:T(1024)}, u32[]{:S(2)}) copy-start(s32[4096]{0:T(1024)} %param.8) | copy-start | bytes 49156
  0.7 20.9 %collective-permute-start.1 = (bf16[4096,1024]{1,0:T(8,128)(2,1)}, bf16[4096,1024]{1,0:T(8,128)(2,1)}, u32[]{:S(2)}, u32[]{:S(2)}) collective-permute-start(bf16[4096,1024]{1,0:T(8,128)(2,1)} %refs_0_.1), channel_id=1, source_target_pairs={{0,8},{8,0},{1,9},{9,1},{2,10},{10,2},{3,11},{11,3},{4,12},{12,4},... | collective-permute-start | bytes 25165832 | tf_op jit(solution)/shard_map/ppermute | solution.py:23
  7.1 4.9 %collective-permute-start.4 = (f32[32,128]{1,0:T(8,128)S(1)}, f32[32,128]{1,0:T(8,128)S(1)}, u32[]{:S(2)}, u32[]{:S(2)}) collective-permute-start(f32[32,128]{1,0:T(8,128)S(1)} %bitcast.103), channel_id=1, source_target_pairs={{0,3},{1,0},{2,1},{3,2},{4,7},{5,4},{6,5},{7,6},{8,11},{9,8},{10,9... | collective-permute-start | bytes 49160 | tf_op jit(solution)/shard_map/ppermute | solution.py:23
  9.3 5.2 %collective-permute-start.3 = (f32[32,128]{1,0:T(8,128)S(1)}, f32[32,128]{1,0:T(8,128)S(1)}, u32[]{:S(2)}, u32[]{:S(2)}) collective-permute-start(f32[32,128]{1,0:T(8,128)S(1)} %bitcast.104), channel_id=1, source_target_pairs={{0,2},{1,3},{2,0},{3,1},{4,6},{5,7},{6,4},{7,5},{8,10},{9,11},{10,... | collective-permute-start | bytes 49160 | tf_op jit(solution)/shard_map/ppermute | solution.py:23
  10.1 4.4 %collective-permute-start.2 = (f32[32,128]{1,0:T(8,128)S(1)}, f32[32,128]{1,0:T(8,128)S(1)}, u32[]{:S(2)}, u32[]{:S(2)}) collective-permute-start(f32[32,128]{1,0:T(8,128)S(1)} %bitcast.105), channel_id=1, source_target_pairs={{0,1},{1,2},{2,3},{3,0},{4,5},{5,6},{6,7},{7,4},{8,9},{9,10},{10,1... | collective-permute-start | bytes 49160 | tf_op jit(solution)/shard_map/ppermute | solution.py:23
  14.6 3.8 %collective-permute-start.5 = (f32[32,128]{1,0:T(8,128)S(1)}, f32[32,128]{1,0:T(8,128)S(1)}, u32[]{:S(2)}, u32[]{:S(2)}) collective-permute-start(f32[32,128]{1,0:T(8,128)S(1)} %add_add_fusion), channel_id=1, source_target_pairs={{0,4},{4,0},{8,12},{12,8},{1,5},{5,1},{9,13},{13,9},{2,6},{6,2},{1... | collective-permute-start | bytes 49160 | tf_op jit(solution)/shard_map/ppermute | solution.py:213
  15.9 2.6 %collective-permute-start = (s32[3,4096]{1,0:T(4,128)S(1)}, s32[3,4096]{1,0:T(4,128)S(1)}, u32[]{:S(2)}, u32[]{:S(2)}) collective-permute-start(s32[3,4096]{1,0:T(4,128)S(1)} %pad_add_fusion), channel_id=1, source_target_pairs={{0,8},{8,0},{1,9},{9,1},{2,10},{10,2},{3,11},{11,3},{4,12},{12,4},... | collective-permute-start | bytes 147464 | tf_op jit(solution)/shard_map/ppermute | solution.py:23
  16.0 3.3 %collective-permute-start.7 = (f32[32,128]{1,0:T(8,128)S(1)}, f32[32,128]{1,0:T(8,128)S(1)}, u32[]{:S(2)}, u32[]{:S(2)}) collective-permute-start(f32[32,128]{1,0:T(8,128)S(1)} %add_add_fusion), channel_id=1, source_target_pairs={{0,12},{4,8},{8,4},{12,0},{1,13},{5,9},{9,5},{13,1},{2,14},{6,10},... | collective-permute-start | bytes 49160 | tf_op jit(solution)/shard_map/ppermute | solution.py:213
  16.9 2.4 %collective-permute-start.6 = (f32[32,128]{1,0:T(8,128)S(1)}, f32[32,128]{1,0:T(8,128)S(1)}, u32[]{:S(2)}, u32[]{:S(2)}) collective-permute-start(f32[32,128]{1,0:T(8,128)S(1)} %add_add_fusion), channel_id=1, source_target_pairs={{0,8},{4,12},{8,0},{12,4},{1,9},{5,13},{9,1},{13,5},{2,10},{6,14},... | collective-permute-start | bytes 49160 | tf_op jit(solution)/shard_map/ppermute | solution.py:213
  42.6 16.2 %collective-permute-start.8 = (bf16[4,32,16,128]{3,2,1,0:T(8,128)(2,1)}, bf16[4,32,16,128]{3,2,1,0:T(8,128)(2,1)S(1)}, u32[]{:S(2)}, u32[]{:S(2)}) collective-permute-start(bf16[4,32,16,128]{3,2,1,0:T(8,128)(2,1)} %bitcast.116), channel_id=1, source_target_pairs={{0,16},{16,32},{32,48},{48,0},{1,17},{17,33},{33,49},{49,1},{2,18}... | collective-permute-start | bytes 1572872 | tf_op jit(solution)/shard_map/ppermute | solution.py:23
  44.1 15.0 %collective-permute-start.9 = (bf16[4,32,16,128]{3,2,1,0:T(8,128)(2,1)}, bf16[4,32,16,128]{3,2,1,0:T(8,128)(2,1)S(1)}, u32[]{:S(2)}, u32[]{:S(2)}) collective-permute-start(bf16[4,32,16,128]{3,2,1,0:T(8,128)(2,1)} %bitcast.115), channel_id=1, source_target_pairs={{0,48},{16,0},{32,16},{48,32},{1,49},{17,1},{33,17},{49,33},{2,50}... | collective-permute-start | bytes 1572872 | tf_op jit(solution)/shard_map/ppermute | solution.py:23
  46.6 6.5 %collective-permute-start.10 = (f32[8,128]{1,0:T(8,128)S(1)}, f32[8,128]{1,0:T(8,128)S(1)}, u32[]{:S(2)}, u32[]{:S(2)}) collective-permute-start(f32[8,128]{1,0:T(8,128)S(1)} %bitcast.111), channel_id=1, source_target_pairs={{0,64},{64,0},{128,192},{192,128},{1,65},{65,1},{129,193},{193,129... | collective-permute-start | bytes 12296 | tf_op jit(solution)/shard_map/ppermute | solution.py:238
  49.9 22.7 %collective-permute-start.12 = (bf16[4,32,16,128]{3,2,1,0:T(8,128)(2,1)}, bf16[4,32,16,128]{3,2,1,0:T(8,128)(2,1)S(1)}, u32[]{:S(2)}, u32[]{:S(2)}) collective-permute-start(bf16[4,32,16,128]{3,2,1,0:T(8,128)(2,1)} %bitcast.114), channel_id=1, source_target_pairs={{0,16},{16,32},{32,48},{48,0},{1,17},{17,33},{33,49},{49,1},{2,18}... | collective-permute-start | bytes 1572872 | tf_op jit(solution)/shard_map/ppermute | solution.py:23
  50.1 22.4 %collective-permute-start.13 = (bf16[4,32,16,128]{3,2,1,0:T(8,128)(2,1)}, bf16[4,32,16,128]{3,2,1,0:T(8,128)(2,1)S(1)}, u32[]{:S(2)}, u32[]{:S(2)}) collective-permute-start(bf16[4,32,16,128]{3,2,1,0:T(8,128)(2,1)} %bitcast.113), channel_id=1, source_target_pairs={{0,48},{16,0},{32,16},{48,32},{1,49},{17,1},{33,17},{49,33},{2,50}... | collective-permute-start | bytes 1572872 | tf_op jit(solution)/shard_map/ppermute | solution.py:23
  60.3 20.4 %collective-permute-start.15 = (bf16[4,32,16,128]{3,2,1,0:T(8,128)(2,1)S(1)}, bf16[4,32,16,128]{3,2,1,0:T(8,128)(2,1)S(1)}, u32[]{:S(2)}, u32[]{:S(2)}) collective-permute-start(bf16[4,32,16,128]{3,2,1,0:T(8,128)(2,1)S(1)} %fusion), channel_id=1, source_target_pairs={{0,48},{16,0},{32,16},{48,32},{1,49},{17,1},{33,17},{49,33},{2,50}... | collective-permute-start | bytes 1572872 | tf_op jit(solution)/shard_map/ppermute | solution.py:23
  64.5 22.8 %collective-permute-start.11 = (bf16[4,32,16,128]{3,2,1,0:T(8,128)(2,1)S(1)}, bf16[4,32,16,128]{3,2,1,0:T(8,128)(2,1)S(1)}, u32[]{:S(2)}, u32[]{:S(2)}) collective-permute-start(bf16[4,32,16,128]{3,2,1,0:T(8,128)(2,1)S(1)} %fusion.1), channel_id=1, source_target_pairs={{0,16},{16,32},{32,48},{48,0},{1,17},{17,33},{33,49},{49,1},{2,18}... | collective-permute-start | bytes 1572872 | tf_op jit(solution)/shard_map/ppermute | solution.py:23
  64.6 8.0 %collective-permute-start.14 = (f32[8,128]{1,0:T(8,128)S(1)}, f32[8,128]{1,0:T(8,128)S(1)}, u32[]{:S(2)}, u32[]{:S(2)}) collective-permute-start(f32[8,128]{1,0:T(8,128)S(1)} %add.180), channel_id=1, source_target_pairs={{0,128},{64,192},{128,0},{192,64},{1,129},{65,193},{129,1},{193,65... | collective-permute-start | bytes 12296 | tf_op jit(solution)/shard_map/ppermute | solution.py:238
  81.6 11.0 %collective-permute-start.20 = (bf16[32,16,128]{2,1,0:T(8,128)(2,1)S(1)}, bf16[32,16,128]{2,1,0:T(8,128)(2,1)S(1)}, u32[]{:S(2)}, u32[]{:S(2)}) collective-permute-start(bf16[32,16,128]{2,1,0:T(8,128)(2,1)S(1)} %fusion.6), channel_id=1, source_target_pairs={{0,192},{64,0},{128,64},{192,128},{1,193},{65,1},{129,65},{193,129... | collective-permute-start | bytes 393224 | tf_op jit(solution)/shard_map/ppermute | solution.py:23
  88.4 8.8 %collective-permute-start.19 = (bf16[32,16,128]{2,1,0:T(8,128)(2,1)S(1)}, bf16[32,16,128]{2,1,0:T(8,128)(2,1)S(1)}, u32[]{:S(2)}, u32[]{:S(2)}) collective-permute-start(bf16[32,16,128]{2,1,0:T(8,128)(2,1)S(1)} %get-tuple-element.70), channel_id=1, source_target_pairs={{0,64},{64,128},{128,192},{192,0},{1,65},{65,129},{129,193},{193,1... | collective-permute-start | bytes 393224 | tf_op jit(solution)/shard_map/ppermute | solution.py:23
  88.5 18.8 %collective-permute-start.17 = (bf16[32,16,128]{2,1,0:T(8,128)(2,1)S(1)}, bf16[32,16,128]{2,1,0:T(8,128)(2,1)S(1)}, u32[]{:S(2)}, u32[]{:S(2)}) collective-permute-start(bf16[32,16,128]{2,1,0:T(8,128)(2,1)S(1)} %get-tuple-element.69), channel_id=1, source_target_pairs={{0,192},{64,0},{128,64},{192,128},{1,193},{65,1},{129,65},{193,129... | collective-permute-start | bytes 393224 | tf_op jit(solution)/shard_map/ppermute | solution.py:23
  98.3 11.1 %collective-permute-start.16 = (bf16[32,16,128]{2,1,0:T(8,128)(2,1)S(1)}, bf16[32,16,128]{2,1,0:T(8,128)(2,1)S(1)}, u32[]{:S(2)}, u32[]{:S(2)}) collective-permute-start(bf16[32,16,128]{2,1,0:T(8,128)(2,1)S(1)} %get-tuple-element.71), channel_id=1, source_target_pairs={{0,64},{64,128},{128,192},{192,0},{1,65},{65,129},{129,193},{193,1... | collective-permute-start | bytes 393224 | tf_op jit(solution)/shard_map/ppermute | solution.py:23
  99.4 13.2 %collective-permute-start.21 = (bf16[32,16,128]{2,1,0:T(8,128)(2,1)S(1)}, bf16[32,16,128]{2,1,0:T(8,128)(2,1)S(1)}, u32[]{:S(2)}, u32[]{:S(2)}) collective-permute-start(bf16[32,16,128]{2,1,0:T(8,128)(2,1)S(1)} %add_convert_fusion.2), channel_id=1, source_target_pairs={{0,64},{64,128},{128,192},{192,0},{1,65},{65,129},{129,193},{193,1... | collective-permute-start | bytes 393224 | tf_op jit(solution)/shard_map/ppermute | solution.py:23
  100.7 11.9 %collective-permute-start.22 = (bf16[32,16,128]{2,1,0:T(8,128)(2,1)S(1)}, bf16[32,16,128]{2,1,0:T(8,128)(2,1)S(1)}, u32[]{:S(2)}, u32[]{:S(2)}) collective-permute-start(bf16[32,16,128]{2,1,0:T(8,128)(2,1)S(1)} %get-tuple-element.72), channel_id=1, source_target_pairs={{0,192},{64,0},{128,64},{192,128},{1,193},{65,1},{129,65},{193,129... | collective-permute-start | bytes 393224 | tf_op jit(solution)/shard_map/ppermute | solution.py:23
  103.6 3.6 %collective-permute-start.18 = (f32[8,128]{1,0:T(8,128)S(1)}, f32[8,128]{1,0:T(8,128)S(1)}, u32[]{:S(2)}, u32[]{:S(2)}) collective-permute-start(f32[8,128]{1,0:T(8,128)S(1)} %add.183), channel_id=1, source_target_pairs={{0,16},{16,0},{32,48},{48,32},{1,17},{17,1},{33,49},{49,33},{2,18}... | collective-permute-start | bytes 12296 | tf_op jit(solution)/shard_map/ppermute | solution.py:238
  113.9 64.7 %copy-start = (bf16[128,1024]{1,0:T(8,128)(2,1)}, bf16[128,1024]{1,0:T(8,128)(2,1)S(1)}, u32[]{:S(2)}) copy-start(bf16[128,1024]{1,0:T(8,128)(2,1)S(1)} %convert_element_type.338) | copy-start | bytes 786436
  113.9 5.8 %collective-permute-start.23 = (f32[8,128]{1,0:T(8,128)S(1)}, f32[8,128]{1,0:T(8,128)S(1)}, u32[]{:S(2)}, u32[]{:S(2)}) collective-permute-start(f32[8,128]{1,0:T(8,128)S(1)} %add.190), channel_id=1, source_target_pairs={{0,32},{16,48},{32,0},{48,16},{1,33},{17,49},{33,1},{49,17},{2,34}... | collective-permute-start | bytes 12296 | tf_op jit(solution)/shard_map/ppermute | solution.py:238
  116.7 12.8 %collective-permute-start.25 = (bf16[128,1024]{1,0:T(8,128)(2,1)S(1)}, bf16[128,1024]{1,0:T(8,128)(2,1)S(1)}, u32[]{:S(2)}, u32[]{:S(2)}) collective-permute-start(bf16[128,1024]{1,0:T(8,128)(2,1)S(1)} %convert_element_type.338), channel_id=1, source_target_pairs={{0,192},{64,0},{128,64},{192,128},{1,193},{65,1},{129,65},{193,129... | collective-permute-start | bytes 786440 | tf_op jit(solution)/shard_map/ppermute | solution.py:23
  116.7 14.3 %collective-permute-start.24 = (bf16[128,1024]{1,0:T(8,128)(2,1)S(1)}, bf16[128,1024]{1,0:T(8,128)(2,1)S(1)}, u32[]{:S(2)}, u32[]{:S(2)}) collective-permute-start(bf16[128,1024]{1,0:T(8,128)(2,1)S(1)} %convert_element_type.338), channel_id=1, source_target_pairs={{0,64},{64,128},{128,192},{192,0},{1,65},{65,129},{129,193},{193,1... | collective-permute-start | bytes 786440 | tf_op jit(solution)/shard_map/ppermute | solution.py:23
  119.7 11.4 %collective-permute-start.27 = (bf16[128,1024]{1,0:T(8,128)(2,1)S(1)}, bf16[128,1024]{1,0:T(8,128)(2,1)S(1)}, u32[]{:S(2)}, u32[]{:S(2)}) collective-permute-start(bf16[128,1024]{1,0:T(8,128)(2,1)S(1)} %convert_element_type.338), channel_id=1, source_target_pairs={{0,48},{16,0},{32,16},{48,32},{1,49},{17,1},{33,17},{49,33},{2,50}... | collective-permute-start | bytes 786440 | tf_op jit(solution)/shard_map/ppermute | solution.py:23
  122.1 9.0 %collective-permute-start.26 = (bf16[128,1024]{1,0:T(8,128)(2,1)S(1)}, bf16[128,1024]{1,0:T(8,128)(2,1)S(1)}, u32[]{:S(2)}, u32[]{:S(2)}) collective-permute-start(bf16[128,1024]{1,0:T(8,128)(2,1)S(1)} %convert_element_type.338), channel_id=1, source_target_pairs={{0,16},{16,32},{32,48},{48,0},{1,17},{17,33},{33,49},{49,1},{2,18}... | collective-permute-start | bytes 786440 | tf_op jit(solution)/shard_map/ppermute | solution.py:23
  131.2 6.4 %collective-permute-start.30 = (bf16[64,1024]{1,0:T(8,128)(2,1)S(1)}, bf16[64,1024]{1,0:T(8,128)(2,1)S(1)}, u32[]{:S(2)}, u32[]{:S(2)}) collective-permute-start(bf16[64,1024]{1,0:T(8,128)(2,1)S(1)} %slice.164), channel_id=1, source_target_pairs={{0,16},{16,32},{32,48},{48,0},{1,17},{17,33},{33,49},{49,1},{2,18}... | collective-permute-start | bytes 393224 | tf_op jit(solution)/shard_map/ppermute | solution.py:23
  132.4 5.9 %collective-permute-start.29 = (bf16[64,1024]{1,0:T(8,128)(2,1)S(1)}, bf16[64,1024]{1,0:T(8,128)(2,1)S(1)}, u32[]{:S(2)}, u32[]{:S(2)}) collective-permute-start(bf16[64,1024]{1,0:T(8,128)(2,1)S(1)} %slice.163), channel_id=1, source_target_pairs={{0,192},{64,0},{128,64},{192,128},{1,193},{65,1},{129,65},{193,129... | collective-permute-start | bytes 393224 | tf_op jit(solution)/shard_map/ppermute | solution.py:23
  133.0 7.1 %collective-permute-start.28 = (bf16[64,1024]{1,0:T(8,128)(2,1)S(1)}, bf16[64,1024]{1,0:T(8,128)(2,1)S(1)}, u32[]{:S(2)}, u32[]{:S(2)}) collective-permute-start(bf16[64,1024]{1,0:T(8,128)(2,1)S(1)} %slice.162), channel_id=1, source_target_pairs={{0,64},{64,128},{128,192},{192,0},{1,65},{65,129},{129,193},{193,1... | collective-permute-start | bytes 393224 | tf_op jit(solution)/shard_map/ppermute | solution.py:23
  135.4 5.0 %collective-permute-start.31 = (bf16[64,1024]{1,0:T(8,128)(2,1)S(1)}, bf16[64,1024]{1,0:T(8,128)(2,1)S(1)}, u32[]{:S(2)}, u32[]{:S(2)}) collective-permute-start(bf16[64,1024]{1,0:T(8,128)(2,1)S(1)} %slice.165), channel_id=1, source_target_pairs={{0,48},{16,0},{32,16},{48,32},{1,49},{17,1},{33,17},{49,33},{2,50}... | collective-permute-start | bytes 393224 | tf_op jit(solution)/shard_map/ppermute | solution.py:23
  140.4 3.0 %collective-permute-start.32 = (bf16[512,1024]{1,0:T(8,128)(2,1)S(1)}, bf16[512,1024]{1,0:T(8,128)(2,1)S(1)}, u32[]{:S(2)}, u32[]{:S(2)}) collective-permute-start(bf16[512,1024]{1,0:T(8,128)(2,1)S(1)} %constant_dynamic-update-slice_fusion.5.right_ref), channel_id=1, source_target_pairs={{0,8},{8,0},{1,9},{9,1},{2,10},{10,2},{3,11},{11,3},{4,12},{12,4},... | collective-permute-start | bytes 3145736 | tf_op jit(solution)/shard_map/ppermute | solution.py:23
  145.9 20.2 %all-to-all-start = ((bf16[8,2,128,256]{3,2,1,0:T(8,128)(2,1)}), bf16[8,2,128,256]{3,2,1,0:T(8,128)(2,1)S(1)}, u32[]{:S(2)}, u32[]{:S(2)}) async-start(bf16[8,2,128,256]{3,2,1,0:T(8,128)(2,1)} %gram_tile.3), calls=%async_computation | async-start | bytes 2097152 | tf_op jit(solution)/shard_map/all_to_all | solution.py:280
  166.2 6.5 %collective-permute-start.33 = (bf16[128,256]{1,0:T(8,128)(2,1)S(1)}, bf16[128,256]{1,0:T(8,128)(2,1)S(1)}, u32[]{:S(2)}, u32[]{:S(2)}) collective-permute-start(bf16[128,256]{1,0:T(8,128)(2,1)S(1)} %get-tuple-element.75), channel_id=1, source_target_pairs={{0,32},{1,48},{2,34},{3,50},{16,0},{17,16},{18,2},{19,18},{32,33},... | collective-permute-start | bytes 196616 | tf_op jit(solution)/shard_map/ppermute | solution.py:289
  170.0 8.6 %collective-permute-start.34 = (bf16[128,256]{1,0:T(8,128)(2,1)S(1)}, bf16[128,256]{1,0:T(8,128)(2,1)S(1)}, u32[]{:S(2)}, u32[]{:S(2)}) collective-permute-start(bf16[128,256]{1,0:T(8,128)(2,1)S(1)} %get-tuple-element.76), channel_id=1, source_target_pairs={{0,0},{1,16},{2,2},{3,18},{16,32},{17,48},{18,34},{19,50},{32,1},{... | collective-permute-start | bytes 196616 | tf_op jit(solution)/shard_map/ppermute | solution.py:289

commit v4 on v3

--- a/solution.py
+++ b/solution.py
@@ -231,7 +231,6 @@
     spots = (picks >> 3) * 64 + (picks & 7)
 
     *pieces, gradient = sketch_pieces(spots, features, other_features, factors, residuals)
-    gradient = gradient[:, 0, :].reshape(8, 128)
     piece = [[pieces[2 * b + h].reshape(4, HALF_PAIRS, 16, 128) for h in range(2)] for b in range(4)]
 
     def swap_add(axis_name, flip, value):
@@ -244,6 +243,7 @@
     after_0 = ring("x", narrow(piece[1][0], far_0), 1)
     before_1 = ring("x", narrow(piece[3][1], far_1), -1)
     gradient = swap_add("zh", 2, gradient)
+    gradient = swap_add("x", 1, gradient)
     after_1, before_0, gradient = lax.optimization_barrier((after_1, before_0, gradient))
     wide = [
         [add_up(piece[0][0][a], after_0[a], before_0[a]), add_up(piece[0][1][a], after_1[a], before_1[a])]
@@ -255,8 +255,6 @@
     end_far_0, end_far_1 = lax.optimization_barrier((end_far_0, end_far_1))
     end_after_0 = ring("zh", narrow(short[1][0], end_far_0), 1)
     end_before_1 = ring("zh", narrow(short[3][1], end_far_1), -1)
-    gradient = swap_add("x", 1, gradient)
-    end_after_1, end_before_0, gradient = lax.optimization_barrier((end_after_1, end_before_0, gradient))
     end_after_0, end_before_1 = lax.optimization_barrier((end_after_0, end_before_1))
     summed = [add_up(wide[0][0], end_before_0, end_after_0), add_up(wide[0][1], end_after_1, end_before_1)]
     summed = jnp.concatenate(summed, axis=0).reshape(128, COLS)
@@ -292,7 +290,7 @@
     upper = my_x >= 2
     gram = jnp.concatenate([jnp.where(upper, turned, same), jnp.where(upper, same, turned)], axis=1)
     gram = gram / jnp.float32(8 * COLS)
-    gradient = gradient.reshape(COLS)
+    gradient = gradient[:, 0, :].reshape(COLS)
     return (gradient / root_total, sketch, gram)
 
 

time: 180 us -> 182 us (1.011)
  waiting for transfers between devices: 65.1 us -> 68.7 us
    ppermute x4, waiting for transfers between devices: 3.7 us -> 9.96 us  [swap_add(): lax.ppermute(value, axis_name, [(i, i ^ flip) for i in range(4)])]
    ppermute x26, waiting for transfers between devices: 39.4 us -> 36.4 us  [ring(): lax.ppermute(value, axis_name, [(i, (i + shift) % size) for i in range(si...]
  transfers between devices with their start and end apart: 36 -> 36, of which waited for: 21 -> 19; matrix products, arithmetic and copies ran while one was open for 9% -> 9% of each run, Pallas kernels for 1% -> 1%
where the time goes in v4:
time: 182 us; the launch traced here: 181 us
  waiting for transfers between devices  68.7 us (38%)
  starting transfers between devices  67.5 us (37%)
  Pallas kernels  24.8 us (14%)
  other arithmetic  11.8 us (6%)
  matrix products  5.64 us (3%)
  local copies, waits for them, and re-layouts  1.93 us (1%)
    ppermute x26, starting transfers between devices, ring(): lax.ppermute(value, axis_name, [(i, (i + shift) % size) for i in range(si...  41.6 us
    ppermute x26, waiting for transfers between devices, ring(): lax.ppermute(value, axis_name, [(i, (i + shift) % size) for i in range(si...  36.4 us
    pallas_call x1, Pallas kernels, sketch_pieces(): pl.pallas_call(sketch_kernel, grid_spec=pltpu.PrefetchScalarGridSpec(num_...  21 us
    all_to_all x1, waiting for transfers between devices, per_device(): parts = lax.all_to_all(tiles, ('zl', 'y'), 0, 0)  14.2 us
    ppermute x4, starting transfers between devices, swap_add(): lax.ppermute(value, axis_name, [(i, i ^ flip) for i in range(4)])  12.9 us
    ppermute x4, waiting for transfers between devices, swap_add(): lax.ppermute(value, axis_name, [(i, i ^ flip) for i in range(4)])  9.96 us
    ppermute x2, waiting for transfers between devices, deliver(): return lax.ppermute(over_feat[i], ('x', 'y'), moves).astype(jnp.float32)  6.04 us
    dot_general x1, matrix products, per_device(): jnp.dot(features, coef, preferred_element_type=jnp.float32).reshape(32, 128)  5.64 us
  transfers between devices with their start and end apart: 36, of which 19 were waited for; matrix products, arithmetic and copies ran while one was open for 9% of the time, Pallas kernels for 1%

profile of v4, /device:TPU:8, one launch (start us, length us, event | category | flops | bytes accessed | tf_op | source)
XLA Modules:
  0.0 181.5 jit_solution(1779426538895799350)
XLA Ops:
  1.5 5.6 %fusion.22 = f32[1,4096]{1,0:T(1,128)S(1)} fusion(bf16[4096,1024]{1,0:T(8,128)(2,1)} %refs_0_.1, bf16[1024,1]{0,1:T(2,128)(2,1)S(1)} %reshape.176), kind=kOutput, calls=%fused_computation.88 | convolution fusion | flops 8388608 | bytes 8407040 | tf_op jit(solution)/shard_map/dot_general | solution.py:206
  7.1 2.2 %collective-permute-start.4 = (f32[32,128]{1,0:T(8,128)S(1)}, f32[32,128]{1,0:T(8,128)S(1)}, u32[]{:S(2)}, u32[]{:S(2)}) collective-permute-start(f32[32,128]{1,0:T(8,128)S(1)} %bitcast.101), channel_id=1, source_target_pairs={{0,3},{1,0},{2,1},{3,2},{4,7},{5,4},{6,5},{7,6},{8,11},{9,8},{10,9... | collective-permute-start | bytes 49160 | tf_op jit(solution)/shard_map/ppermute | solution.py:23
  10.1 1.9 %collective-permute-start.2 = (f32[32,128]{1,0:T(8,128)S(1)}, f32[32,128]{1,0:T(8,128)S(1)}, u32[]{:S(2)}, u32[]{:S(2)}) collective-permute-start(f32[32,128]{1,0:T(8,128)S(1)} %bitcast.103), channel_id=1, source_target_pairs={{0,1},{1,2},{2,3},{3,0},{4,5},{5,6},{6,7},{7,4},{8,9},{9,10},{10,1... | collective-permute-start | bytes 49160 | tf_op jit(solution)/shard_map/ppermute | solution.py:23
  12.0 2.5 %collective-permute-done.3 = f32[32,128]{1,0:T(8,128)S(1)} collective-permute-done((f32[32,128]{1,0:T(8,128)S(1)}, f32[32,128]{1,0:T(8,128)S(1)}, u32[]{:S(2)}, u32[]{:S(2)}) %collective-permute-start.3) | collective-permute-done | bytes 16416 | tf_op jit(solution)/shard_map/ppermute | solution.py:23
  14.6 1.3 collective-permute-start.5
  17.1 1.3 collective-permute-done.5
  21.0 21.0 %hadamard_pick.1 = (bf16[128,16,128]{2,1,0:T(8,128)(2,1)}, bf16[128,16,128]{2,1,0:T(8,128)(2,1)}, bf16[128,16,128]{2,1,0:T(8,128)(2,1)}, bf16[128,16,128]{2,1,0:...) custom-call(s32[4096]{0:T(1024)} %add.172.spots, ...), custom_call_target="tpu_custom_call" | custom-call | flops 4400000000 | bytes 22000000 | tf_op jit(solution)/shard_map/hadamard_pick/pallas_call | solution.py:118
  42.0 1.5 collective-permute-start.8
  43.5 1.7 collective-permute-start.9
  45.2 3.3 %collective-permute-start.10 = (f32[4,8,256]{2,1,0:T(8,128)}, f32[4,8,256]{2,1,0:T(8,128)S(1)}, u32[]{:S(2)}, u32[]{:S(2)}) collective-permute-start(f32[4,8,256]{2,1,0:T(8,128)} %get-tuple-element.37), channel_id=1, source_target_pairs={{0,64},{64,0},{128,192},{192,128},{1,65},{65,1},{129,193},{193,129... | collective-permute-start | bytes 98312 | tf_op jit(solution)/shard_map/ppermute | solution.py:237
  48.8 3.0 %collective-permute-start.13 = (bf16[4,32,16,128]{3,2,1,0:T(8,128)(2,1)}, bf16[4,32,16,128]{3,2,1,0:T(8,128)(2,1)S(1)}, u32[]{:S(2)}, u32[]{:S(2)}) collective-permute-start(bf16[4,32,16,128]{3,2,1,0:T(8,128)(2,1)} %bitcast.110), channel_id=1, source_target_pairs={{0,48},{16,0},{32,16},{48,32},{1,49},{17,1},{33,17},{49,33},{2,50}... | collective-permute-start | bytes 1572872 | tf_op jit(solution)/shard_map/ppermute | solution.py:23
  52.5 5.7 %collective-permute-done.8 = bf16[4,32,16,128]{3,2,1,0:T(8,128)(2,1)S(1)} collective-permute-done((bf16[4,32,16,128]{3,2,1,0:T(8,128)(2,1)}, bf16[4,32,16,128]{3,2,1,0:T(8,128)(2,1)S(1)}, u32[]{:S(2)}, u32[]{:S(2)}) %collective-permute-start.8) | collective-permute-done | bytes 524320 | tf_op jit(solution)/shard_map/ppermute | solution.py:23
  58.5 1.2 fusion
  59.7 3.0 %collective-permute-start.18 = (bf16[4,32,16,128]{3,2,1,0:T(8,128)(2,1)S(1)}, bf16[4,32,16,128]{3,2,1,0:T(8,128)(2,1)S(1)}, u32[]{:S(2)}, u32[]{:S(2)}) collective-permute-start(bf16[4,32,16,128]{3,2,1,0:T(8,128)(2,1)S(1)} %fusion), channel_id=1, source_target_pairs={{0,48},{16,0},{32,16},{48,32},{1,49},{17,1},{33,17},{49,33},{2,50}... | collective-permute-start | bytes 1572872 | tf_op jit(solution)/shard_map/ppermute | solution.py:23
  62.7 1.2 fusion.1
  64.0 6.4 %collective-permute-start.14 = (f32[4,8,256]{2,1,0:T(8,128)S(1)}, f32[4,8,256]{2,1,0:T(8,128)S(1)}, u32[]{:S(2)}, u32[]{:S(2)}) collective-permute-start(f32[4,8,256]{2,1,0:T(8,128)S(1)} %add.180), channel_id=1, source_target_pairs={{0,128},{64,192},{128,0},{192,64},{1,129},{65,193},{129,1},{193,65... | collective-permute-start | bytes 98312 | tf_op jit(solution)/shard_map/ppermute | solution.py:237
  70.3 1.9 %collective-permute-done.14 = f32[4,8,256]{2,1,0:T(8,128)S(1)} collective-permute-done((f32[4,8,256]{2,1,0:T(8,128)S(1)}, f32[4,8,256]{2,1,0:T(8,128)S(1)}, u32[]{:S(2)}, u32[]{:S(2)}) %collective-permute-start.14) | collective-permute-done | bytes 32800 | tf_op jit(solution)/shard_map/ppermute | solution.py:237
  72.7 8.1 %collective-permute-done.15 = f32[4,8,256]{2,1,0:T(8,128)S(1)} collective-permute-done((f32[4,8,256]{2,1,0:T(8,128)S(1)}, f32[4,8,256]{2,1,0:T(8,128)S(1)}, u32[]{:S(2)}, u32[]{:S(2)}) %collective-permute-start.15) | collective-permute-done | bytes 32800 | tf_op jit(solution)/shard_map/ppermute | solution.py:237
  80.8 1.0 fusion.7
  81.8 5.5 %collective-permute-start.19 = (bf16[32,16,128]{2,1,0:T(8,128)(2,1)S(1)}, bf16[32,16,128]{2,1,0:T(8,128)(2,1)S(1)}, u32[]{:S(2)}, u32[]{:S(2)}) collective-permute-start(bf16[32,16,128]{2,1,0:T(8,128)(2,1)S(1)} %fusion.7), channel_id=1, source_target_pairs={{0,192},{64,0},{128,64},{192,128},{1,193},{65,1},{129,65},{193,129... | collective-permute-start | bytes 393224 | tf_op jit(solution)/shard_map/ppermute | solution.py:23
  87.2 1.1 fusion.10
  88.4 4.1 %collective-permute-done.19 = bf16[32,16,128]{2,1,0:T(8,128)(2,1)S(1)} collective-permute-done((bf16[32,16,128]{2,1,0:T(8,128)(2,1)S(1)}, bf16[32,16,128]{2,1,0:T(8,128)(2,1)S(1)}, u32[]{:S(2)}, u32[]{:S(2)}) %collective-permute-start.19) | collective-permute-done | bytes 131104 | tf_op jit(solution)/shard_map/ppermute | solution.py:23
  92.5 4.7 %collective-permute-done.17 = bf16[32,16,128]{2,1,0:T(8,128)(2,1)S(1)} collective-permute-done((bf16[32,16,128]{2,1,0:T(8,128)(2,1)S(1)}, bf16[32,16,128]{2,1,0:T(8,128)(2,1)S(1)}, u32[]{:S(2)}, u32[]{:S(2)}) %collective-permute-start.17) | collective-permute-done | bytes 131104 | tf_op jit(solution)/shard_map/ppermute | solution.py:23
  97.1 1.0 add_convert_fusion.2
  98.2 1.1 fusion.3
  99.3 4.2 %collective-permute-start.21 = (bf16[32,16,128]{2,1,0:T(8,128)(2,1)S(1)}, bf16[32,16,128]{2,1,0:T(8,128)(2,1)S(1)}, u32[]{:S(2)}, u32[]{:S(2)}) collective-permute-start(bf16[32,16,128]{2,1,0:T(8,128)(2,1)S(1)} %get-tuple-element.66), channel_id=1, source_target_pairs={{0,192},{64,0},{128,64},{192,128},{1,193},{65,1},{129,65},{193,129... | collective-permute-start | bytes 393224 | tf_op jit(solution)/shard_map/ppermute | solution.py:23
  103.5 4.1 %collective-permute-start.16 = (bf16[32,16,128]{2,1,0:T(8,128)(2,1)S(1)}, bf16[32,16,128]{2,1,0:T(8,128)(2,1)S(1)}, u32[]{:S(2)}, u32[]{:S(2)}) collective-permute-start(bf16[32,16,128]{2,1,0:T(8,128)(2,1)S(1)} %get-tuple-element.63), channel_id=1, source_target_pairs={{0,192},{64,0},{128,64},{192,128},{1,193},{65,1},{129,65},{193,129... | collective-permute-start | bytes 393224 | tf_op jit(solution)/shard_map/ppermute | solution.py:23
  108.2 1.8 collective-permute-done.21
  110.0 2.2 %collective-permute-done.22 = bf16[32,16,128]{2,1,0:T(8,128)(2,1)S(1)} collective-permute-done((bf16[32,16,128]{2,1,0:T(8,128)(2,1)S(1)}, bf16[32,16,128]{2,1,0:T(8,128)(2,1)S(1)}, u32[]{:S(2)}, u32[]{:S(2)}) %collective-permute-start.22) | collective-permute-done | bytes 131104 | tf_op jit(solution)/shard_map/ppermute | solution.py:23
  112.2 1.0 fusion.5
  113.2 1.0 fusion.12
  114.4 2.8 %collective-permute-start.23 = (f32[4,8,256]{2,1,0:T(8,128)S(1)}, f32[4,8,256]{2,1,0:T(8,128)S(1)}, u32[]{:S(2)}, u32[]{:S(2)}) collective-permute-start(f32[4,8,256]{2,1,0:T(8,128)S(1)} %add.184), channel_id=1, source_target_pairs={{0,32},{16,48},{32,0},{48,16},{1,33},{17,49},{33,1},{49,17},{2,34}... | collective-permute-start | bytes 98312 | tf_op jit(solution)/shard_map/ppermute | solution.py:237
  117.2 4.2 %collective-permute-start.25 = (bf16[128,1024]{1,0:T(8,128)(2,1)S(1)}, bf16[128,1024]{1,0:T(8,128)(2,1)S(1)}, u32[]{:S(2)}, u32[]{:S(2)}) collective-permute-start(bf16[128,1024]{1,0:T(8,128)(2,1)S(1)} %convert_element_type.338), channel_id=1, source_target_pairs={{0,192},{64,0},{128,64},{192,128},{1,193},{65,1},{129,65},{193,129... | collective-permute-start | bytes 786440 | tf_op jit(solution)/shard_map/ppermute | solution.py:23
  122.2 1.2 collective-permute-start.26
  123.4 6.6 %collective-permute-done.25 = bf16[128,1024]{1,0:T(8,128)(2,1)S(1)} collective-permute-done((bf16[128,1024]{1,0:T(8,128)(2,1)S(1)}, bf16[128,1024]{1,0:T(8,128)(2,1)S(1)}, u32[]{:S(2)}, u32[]{:S(2)}) %collective-permute-start.25) | collective-permute-done | bytes 262176 | tf_op jit(solution)/shard_map/ppermute | solution.py:23
  130.0 3.2 %collective-permute-done.24 = bf16[128,1024]{1,0:T(8,128)(2,1)S(1)} collective-permute-done((bf16[128,1024]{1,0:T(8,128)(2,1)S(1)}, bf16[128,1024]{1,0:T(8,128)(2,1)S(1)}, u32[]{:S(2)}, u32[]{:S(2)}) %collective-permute-start.24) | collective-permute-done | bytes 262176 | tf_op jit(solution)/shard_map/ppermute | solution.py:23
  133.7 1.4 collective-permute-start.29
  135.1 1.5 collective-permute-start.28
  136.7 2.9 %collective-permute-start.31 = (bf16[64,1024]{1,0:T(8,128)(2,1)S(1)}, bf16[64,1024]{1,0:T(8,128)(2,1)S(1)}, u32[]{:S(2)}, u32[]{:S(2)}) collective-permute-start(bf16[64,1024]{1,0:T(8,128)(2,1)S(1)} %slice.165), channel_id=1, source_target_pairs={{0,48},{16,0},{32,16},{48,32},{1,49},{17,1},{33,17},{49,33},{2,50}... | collective-permute-start | bytes 393224 | tf_op jit(solution)/shard_map/ppermute | solution.py:23
  139.7 3.7 %collective-permute-done.28 = bf16[64,1024]{1,0:T(8,128)(2,1)S(1)} collective-permute-done((bf16[64,1024]{1,0:T(8,128)(2,1)S(1)}, bf16[64,1024]{1,0:T(8,128)(2,1)S(1)}, u32[]{:S(2)}, u32[]{:S(2)}) %collective-permute-start.28) | collective-permute-done | bytes 131104 | tf_op jit(solution)/shard_map/ppermute | solution.py:23
  144.0 1.3 gram_tile.2.refs_0_
  145.3 1.1 collective-permute-done.32.right_ref
  146.5 2.5 %gram_tile.3 = bf16[8,2,128,256]{3,2,1,0:T(8,128)(2,1)} custom-call(s32[3]{0:T(128)S(1)} %pad_add_fusion.2.place, bf16[512,1024]{1,0:T(8,128)(2,1)S(1)} %constant_dynamic-update-slice_fusion.left_ref, bf16[512,1024]{1,0:T(8,128)(2,1)S(1)} %collective-permute-done.32.right_ref, bf16[8,2,128,128]{3,2,1,0:T(8,128)(2,1)S(1)} %gram_tile.2.refs_0_), custom_call_target="tpu_custom_call" | custom-call | flops 540000000 | bytes 3000000 | tf_op jit(solution)/shard_map/gram_tile/pallas_call | solution.py:174
  149.0 5.3 %all-to-all-start = ((bf16[8,2,128,256]{3,2,1,0:T(8,128)(2,1)}), bf16[8,2,128,256]{3,2,1,0:T(8,128)(2,1)S(1)}, u32[]{:S(2)}, u32[]{:S(2)}) async-start(bf16[8,2,128,256]{3,2,1,0:T(8,128)(2,1)} %gram_tile.3), calls=%async_computation | async-start | bytes 2097152 | tf_op jit(solution)/shard_map/all_to_all | solution.py:278
  154.2 14.2 %all-to-all-done = bf16[8,2,128,256]{3,2,1,0:T(8,128)(2,1)S(1)} async-done(((bf16[8,2,128,256]{3,2,1,0:T(8,128)(2,1)}), bf16[8,2,128,256]{3,2,1,0:T(8,128)(2,1)S(1)}, u32[]{:S(2)}, u32[]{:S(2)}) %all-to-all-start) | async-done | bytes 1048608 | tf_op jit(solution)/shard_map/all_to_all | solution.py:278
  168.6 3.6 %collective-permute-start.33 = (bf16[128,256]{1,0:T(8,128)(2,1)S(1)}, bf16[128,256]{1,0:T(8,128)(2,1)S(1)}, u32[]{:S(2)}, u32[]{:S(2)}) collective-permute-start(bf16[128,256]{1,0:T(8,128)(2,1)S(1)} %get-tuple-element.69), channel_id=1, source_target_pairs={{0,32},{1,48},{2,34},{3,50},{16,0},{17,16},{18,2},{19,18},{32,33},... | collective-permute-start | bytes 196616 | tf_op jit(solution)/shard_map/ppermute | solution.py:287
  172.1 1.9 %collective-permute-start.34 = (bf16[128,256]{1,0:T(8,128)(2,1)S(1)}, bf16[128,256]{1,0:T(8,128)(2,1)S(1)}, u32[]{:S(2)}, u32[]{:S(2)}) collective-permute-start(bf16[128,256]{1,0:T(8,128)(2,1)S(1)} %get-tuple-element.70), channel_id=1, source_target_pairs={{0,0},{1,16},{2,2},{3,18},{16,32},{17,48},{18,34},{19,50},{32,1},{... | collective-permute-start | bytes 196616 | tf_op jit(solution)/shard_map/ppermute | solution.py:287
  175.0 5.7 %collective-permute-done.34 = bf16[128,256]{1,0:T(8,128)(2,1)S(1)} collective-permute-done((bf16[128,256]{1,0:T(8,128)(2,1)S(1)}, bf16[128,256]{1,0:T(8,128)(2,1)S(1)}, u32[]{:S(2)}, u32[]{:S(2)}) %collective-permute-start.34) | collective-permute-done | bytes 65568 | tf_op jit(solution)/shard_map/ppermute | solution.py:287
  (89 shorter events, 12.1 us)
Async XLA Ops:
  0.6 15.2 %copy-start.3 = (s32[1,4096]{1,0:T(1,128)S(1)}, s32[1,4096]{1,0:T(1,128)}, u32[]{:S(2)}) copy-start(s32[1,4096]{1,0:T(1,128)} %param.9) | copy-start | bytes 49156
  0.6 15.2 %copy-start.1 = (s32[4096]{0:T(1024)S(1)}, s32[4096]{0:T(1024)}, u32[]{:S(2)}) copy-start(s32[4096]{0:T(1024)} %param.7) | copy-start | bytes 49156
  0.7 15.2 %copy-start.2 = (s32[4096]{0:T(1024)S(1)}, s32[4096]{0:T(1024)}, u32[]{:S(2)}) copy-start(s32[4096]{0:T(1024)} %param.8) | copy-start | bytes 49156
  0.7 20.3 %collective-permute-start.1 = (bf16[4096,1024]{1,0:T(8,128)(2,1)}, bf16[4096,1024]{1,0:T(8,128)(2,1)}, u32[]{:S(2)}, u32[]{:S(2)}) collective-permute-start(bf16[4096,1024]{1,0:T(8,128)(2,1)} %refs_0_.1), channel_id=1, source_target_pairs={{0,8},{8,0},{1,9},{9,1},{2,10},{10,2},{3,11},{11,3},{4,12},{12,4},... | collective-permute-start | bytes 25165832 | tf_op jit(solution)/shard_map/ppermute | solution.py:23
  7.1 4.9 %collective-permute-start.4 = (f32[32,128]{1,0:T(8,128)S(1)}, f32[32,128]{1,0:T(8,128)S(1)}, u32[]{:S(2)}, u32[]{:S(2)}) collective-permute-start(f32[32,128]{1,0:T(8,128)S(1)} %bitcast.101), channel_id=1, source_target_pairs={{0,3},{1,0},{2,1},{3,2},{4,7},{5,4},{6,5},{7,6},{8,11},{9,8},{10,9... | collective-permute-start | bytes 49160 | tf_op jit(solution)/shard_map/ppermute | solution.py:23
  9.3 5.2 %collective-permute-start.3 = (f32[32,128]{1,0:T(8,128)S(1)}, f32[32,128]{1,0:T(8,128)S(1)}, u32[]{:S(2)}, u32[]{:S(2)}) collective-permute-start(f32[32,128]{1,0:T(8,128)S(1)} %bitcast.102), channel_id=1, source_target_pairs={{0,2},{1,3},{2,0},{3,1},{4,6},{5,7},{6,4},{7,5},{8,10},{9,11},{10,... | collective-permute-start | bytes 49160 | tf_op jit(solution)/shard_map/ppermute | solution.py:23
  10.1 4.4 %collective-permute-start.2 = (f32[32,128]{1,0:T(8,128)S(1)}, f32[32,128]{1,0:T(8,128)S(1)}, u32[]{:S(2)}, u32[]{:S(2)}) collective-permute-start(f32[32,128]{1,0:T(8,128)S(1)} %bitcast.103), channel_id=1, source_target_pairs={{0,1},{1,2},{2,3},{3,0},{4,5},{5,6},{6,7},{7,4},{8,9},{9,10},{10,1... | collective-permute-start | bytes 49160 | tf_op jit(solution)/shard_map/ppermute | solution.py:23
  14.6 3.8 %collective-permute-start.5 = (f32[32,128]{1,0:T(8,128)S(1)}, f32[32,128]{1,0:T(8,128)S(1)}, u32[]{:S(2)}, u32[]{:S(2)}) collective-permute-start(f32[32,128]{1,0:T(8,128)S(1)} %add_add_fusion), channel_id=1, source_target_pairs={{0,4},{4,0},{8,12},{12,8},{1,5},{5,1},{9,13},{13,9},{2,6},{6,2},{1... | collective-permute-start | bytes 49160 | tf_op jit(solution)/shard_map/ppermute | solution.py:213
  15.9 2.6 %collective-permute-start = (s32[3,4096]{1,0:T(4,128)S(1)}, s32[3,4096]{1,0:T(4,128)S(1)}, u32[]{:S(2)}, u32[]{:S(2)}) collective-permute-start(s32[3,4096]{1,0:T(4,128)S(1)} %pad_add_fusion), channel_id=1, source_target_pairs={{0,8},{8,0},{1,9},{9,1},{2,10},{10,2},{3,11},{11,3},{4,12},{12,4},... | collective-permute-start | bytes 147464 | tf_op jit(solution)/shard_map/ppermute | solution.py:23
  16.0 3.3 %collective-permute-start.7 = (f32[32,128]{1,0:T(8,128)S(1)}, f32[32,128]{1,0:T(8,128)S(1)}, u32[]{:S(2)}, u32[]{:S(2)}) collective-permute-start(f32[32,128]{1,0:T(8,128)S(1)} %add_add_fusion), channel_id=1, source_target_pairs={{0,12},{4,8},{8,4},{12,0},{1,13},{5,9},{9,5},{13,1},{2,14},{6,10},... | collective-permute-start | bytes 49160 | tf_op jit(solution)/shard_map/ppermute | solution.py:213
  16.9 2.4 %collective-permute-start.6 = (f32[32,128]{1,0:T(8,128)S(1)}, f32[32,128]{1,0:T(8,128)S(1)}, u32[]{:S(2)}, u32[]{:S(2)}) collective-permute-start(f32[32,128]{1,0:T(8,128)S(1)} %add_add_fusion), channel_id=1, source_target_pairs={{0,8},{4,12},{8,0},{12,4},{1,9},{5,13},{9,1},{13,5},{2,10},{6,14},... | collective-permute-start | bytes 49160 | tf_op jit(solution)/shard_map/ppermute | solution.py:213
  42.0 16.2 %collective-permute-start.8 = (bf16[4,32,16,128]{3,2,1,0:T(8,128)(2,1)}, bf16[4,32,16,128]{3,2,1,0:T(8,128)(2,1)S(1)}, u32[]{:S(2)}, u32[]{:S(2)}) collective-permute-start(bf16[4,32,16,128]{3,2,1,0:T(8,128)(2,1)} %bitcast.113), channel_id=1, source_target_pairs={{0,16},{16,32},{32,48},{48,0},{1,17},{17,33},{33,49},{49,1},{2,18}... | collective-permute-start | bytes 1572872 | tf_op jit(solution)/shard_map/ppermute | solution.py:23
  43.5 15.0 %collective-permute-start.9 = (bf16[4,32,16,128]{3,2,1,0:T(8,128)(2,1)}, bf16[4,32,16,128]{3,2,1,0:T(8,128)(2,1)S(1)}, u32[]{:S(2)}, u32[]{:S(2)}) collective-permute-start(bf16[4,32,16,128]{3,2,1,0:T(8,128)(2,1)} %bitcast.112), channel_id=1, source_target_pairs={{0,48},{16,0},{32,16},{48,32},{1,49},{17,1},{33,17},{49,33},{2,50}... | collective-permute-start | bytes 1572872 | tf_op jit(solution)/shard_map/ppermute | solution.py:23
  45.2 6.5 %collective-permute-start.10 = (f32[4,8,256]{2,1,0:T(8,128)}, f32[4,8,256]{2,1,0:T(8,128)S(1)}, u32[]{:S(2)}, u32[]{:S(2)}) collective-permute-start(f32[4,8,256]{2,1,0:T(8,128)} %get-tuple-element.37), channel_id=1, source_target_pairs={{0,64},{64,0},{128,192},{192,128},{1,65},{65,1},{129,193},{193,129... | collective-permute-start | bytes 98312 | tf_op jit(solution)/shard_map/ppermute | solution.py:237
  48.5 32.3 %collective-permute-start.12 = (bf16[4,32,16,128]{3,2,1,0:T(8,128)(2,1)}, bf16[4,32,16,128]{3,2,1,0:T(8,128)(2,1)S(1)}, u32[]{:S(2)}, u32[]{:S(2)}) collective-permute-start(bf16[4,32,16,128]{3,2,1,0:T(8,128)(2,1)} %bitcast.111), channel_id=1, source_target_pairs={{0,16},{16,32},{32,48},{48,0},{1,17},{17,33},{33,49},{49,1},{2,18}... | collective-permute-start | bytes 1572872 | tf_op jit(solution)/shard_map/ppermute | solution.py:23
  48.8 32.0 %collective-permute-start.13 = (bf16[4,32,16,128]{3,2,1,0:T(8,128)(2,1)}, bf16[4,32,16,128]{3,2,1,0:T(8,128)(2,1)S(1)}, u32[]{:S(2)}, u32[]{:S(2)}) collective-permute-start(bf16[4,32,16,128]{3,2,1,0:T(8,128)(2,1)} %bitcast.110), channel_id=1, source_target_pairs={{0,48},{16,0},{32,16},{48,32},{1,49},{17,1},{33,17},{49,33},{2,50}... | collective-permute-start | bytes 1572872 | tf_op jit(solution)/shard_map/ppermute | solution.py:23
  59.7 21.1 %collective-permute-start.18 = (bf16[4,32,16,128]{3,2,1,0:T(8,128)(2,1)S(1)}, bf16[4,32,16,128]{3,2,1,0:T(8,128)(2,1)S(1)}, u32[]{:S(2)}, u32[]{:S(2)}) collective-permute-start(bf16[4,32,16,128]{3,2,1,0:T(8,128)(2,1)S(1)} %fusion), channel_id=1, source_target_pairs={{0,48},{16,0},{32,16},{48,32},{1,49},{17,1},{33,17},{49,33},{2,50}... | collective-permute-start | bytes 1572872 | tf_op jit(solution)/shard_map/ppermute | solution.py:23
  63.9 23.4 %collective-permute-start.11 = (bf16[4,32,16,128]{3,2,1,0:T(8,128)(2,1)S(1)}, bf16[4,32,16,128]{3,2,1,0:T(8,128)(2,1)S(1)}, u32[]{:S(2)}, u32[]{:S(2)}) collective-permute-start(bf16[4,32,16,128]{3,2,1,0:T(8,128)(2,1)S(1)} %fusion.1), channel_id=1, source_target_pairs={{0,16},{16,32},{32,48},{48,0},{1,17},{17,33},{33,49},{49,1},{2,18}... | collective-permute-start | bytes 1572872 | tf_op jit(solution)/shard_map/ppermute | solution.py:23
  64.0 8.3 %collective-permute-start.14 = (f32[4,8,256]{2,1,0:T(8,128)S(1)}, f32[4,8,256]{2,1,0:T(8,128)S(1)}, u32[]{:S(2)}, u32[]{:S(2)}) collective-permute-start(f32[4,8,256]{2,1,0:T(8,128)S(1)} %add.180), channel_id=1, source_target_pairs={{0,128},{64,192},{128,0},{192,64},{1,129},{65,193},{129,1},{193,65... | collective-permute-start | bytes 98312 | tf_op jit(solution)/shard_map/ppermute | solution.py:237
  72.2 8.5 %collective-permute-start.15 = (f32[4,8,256]{2,1,0:T(8,128)S(1)}, f32[4,8,256]{2,1,0:T(8,128)S(1)}, u32[]{:S(2)}, u32[]{:S(2)}) collective-permute-start(f32[4,8,256]{2,1,0:T(8,128)S(1)} %add.183), channel_id=1, source_target_pairs={{0,16},{16,0},{32,48},{48,32},{1,17},{17,1},{33,49},{49,33},{2,18}... | collective-permute-start | bytes 98312 | tf_op jit(solution)/shard_map/ppermute | solution.py:237
  81.8 10.7 %collective-permute-start.19 = (bf16[32,16,128]{2,1,0:T(8,128)(2,1)S(1)}, bf16[32,16,128]{2,1,0:T(8,128)(2,1)S(1)}, u32[]{:S(2)}, u32[]{:S(2)}) collective-permute-start(bf16[32,16,128]{2,1,0:T(8,128)(2,1)S(1)} %fusion.7), channel_id=1, source_target_pairs={{0,192},{64,0},{128,64},{192,128},{1,193},{65,1},{129,65},{193,129... | collective-permute-start | bytes 393224 | tf_op jit(solution)/shard_map/ppermute | solution.py:23
  88.3 8.8 %collective-permute-start.17 = (bf16[32,16,128]{2,1,0:T(8,128)(2,1)S(1)}, bf16[32,16,128]{2,1,0:T(8,128)(2,1)S(1)}, u32[]{:S(2)}, u32[]{:S(2)}) collective-permute-start(bf16[32,16,128]{2,1,0:T(8,128)(2,1)S(1)} %get-tuple-element.64), channel_id=1, source_target_pairs={{0,64},{64,128},{128,192},{192,0},{1,65},{65,129},{129,193},{193,1... | collective-permute-start | bytes 393224 | tf_op jit(solution)/shard_map/ppermute | solution.py:23
  98.1 10.1 %collective-permute-start.20 = (bf16[32,16,128]{2,1,0:T(8,128)(2,1)S(1)}, bf16[32,16,128]{2,1,0:T(8,128)(2,1)S(1)}, u32[]{:S(2)}, u32[]{:S(2)}) collective-permute-start(bf16[32,16,128]{2,1,0:T(8,128)(2,1)S(1)} %add_convert_fusion.2), channel_id=1, source_target_pairs={{0,64},{64,128},{128,192},{192,0},{1,65},{65,129},{129,193},{193,1... | collective-permute-start | bytes 393224 | tf_op jit(solution)/shard_map/ppermute | solution.py:23
  99.3 10.7 %collective-permute-start.21 = (bf16[32,16,128]{2,1,0:T(8,128)(2,1)S(1)}, bf16[32,16,128]{2,1,0:T(8,128)(2,1)S(1)}, u32[]{:S(2)}, u32[]{:S(2)}) collective-permute-start(bf16[32,16,128]{2,1,0:T(8,128)(2,1)S(1)} %get-tuple-element.66), channel_id=1, source_target_pairs={{0,192},{64,0},{128,64},{192,128},{1,193},{65,1},{129,65},{193,129... | collective-permute-start | bytes 393224 | tf_op jit(solution)/shard_map/ppermute | solution.py:23
  103.5 8.7 %collective-permute-start.22 = (bf16[32,16,128]{2,1,0:T(8,128)(2,1)S(1)}, bf16[32,16,128]{2,1,0:T(8,128)(2,1)S(1)}, u32[]{:S(2)}, u32[]{:S(2)}) collective-permute-start(bf16[32,16,128]{2,1,0:T(8,128)(2,1)S(1)} %get-tuple-element.65), channel_id=1, source_target_pairs={{0,64},{64,128},{128,192},{192,0},{1,65},{65,129},{129,193},{193,1... | collective-permute-start | bytes 393224 | tf_op jit(solution)/shard_map/ppermute | solution.py:23
  103.5 9.7 %collective-permute-start.16 = (bf16[32,16,128]{2,1,0:T(8,128)(2,1)S(1)}, bf16[32,16,128]{2,1,0:T(8,128)(2,1)S(1)}, u32[]{:S(2)}, u32[]{:S(2)}) collective-permute-start(bf16[32,16,128]{2,1,0:T(8,128)(2,1)S(1)} %get-tuple-element.63), channel_id=1, source_target_pairs={{0,192},{64,0},{128,64},{192,128},{1,193},{65,1},{129,65},{193,129... | collective-permute-start | bytes 393224 | tf_op jit(solution)/shard_map/ppermute | solution.py:23
  114.4 66.3 %copy-start = (bf16[128,1024]{1,0:T(8,128)(2,1)}, bf16[128,1024]{1,0:T(8,128)(2,1)S(1)}, u32[]{:S(2)}) copy-start(bf16[128,1024]{1,0:T(8,128)(2,1)S(1)} %convert_element_type.338) | copy-start | bytes 786436
  114.4 6.9 %collective-permute-start.23 = (f32[4,8,256]{2,1,0:T(8,128)S(1)}, f32[4,8,256]{2,1,0:T(8,128)S(1)}, u32[]{:S(2)}, u32[]{:S(2)}) collective-permute-start(f32[4,8,256]{2,1,0:T(8,128)S(1)} %add.184), channel_id=1, source_target_pairs={{0,32},{16,48},{32,0},{48,16},{1,33},{17,49},{33,1},{49,17},{2,34}... | collective-permute-start | bytes 98312 | tf_op jit(solution)/shard_map/ppermute | solution.py:237
  117.2 12.9 %collective-permute-start.25 = (bf16[128,1024]{1,0:T(8,128)(2,1)S(1)}, bf16[128,1024]{1,0:T(8,128)(2,1)S(1)}, u32[]{:S(2)}, u32[]{:S(2)}) collective-permute-start(bf16[128,1024]{1,0:T(8,128)(2,1)S(1)} %convert_element_type.338), channel_id=1, source_target_pairs={{0,192},{64,0},{128,64},{192,128},{1,193},{65,1},{129,65},{193,129... | collective-permute-start | bytes 786440 | tf_op jit(solution)/shard_map/ppermute | solution.py:23
  121.3 11.9 %collective-permute-start.24 = (bf16[128,1024]{1,0:T(8,128)(2,1)S(1)}, bf16[128,1024]{1,0:T(8,128)(2,1)S(1)}, u32[]{:S(2)}, u32[]{:S(2)}) collective-permute-start(bf16[128,1024]{1,0:T(8,128)(2,1)S(1)} %convert_element_type.338), channel_id=1, source_target_pairs={{0,64},{64,128},{128,192},{192,0},{1,65},{65,129},{129,193},{193,1... | collective-permute-start | bytes 786440 | tf_op jit(solution)/shard_map/ppermute | solution.py:23
  121.3 11.9 %collective-permute-start.27 = (bf16[128,1024]{1,0:T(8,128)(2,1)S(1)}, bf16[128,1024]{1,0:T(8,128)(2,1)S(1)}, u32[]{:S(2)}, u32[]{:S(2)}) collective-permute-start(bf16[128,1024]{1,0:T(8,128)(2,1)S(1)} %convert_element_type.338), channel_id=1, source_target_pairs={{0,48},{16,0},{32,16},{48,32},{1,49},{17,1},{33,17},{49,33},{2,50}... | collective-permute-start | bytes 786440 | tf_op jit(solution)/shard_map/ppermute | solution.py:23
  122.2 11.0 %collective-permute-start.26 = (bf16[128,1024]{1,0:T(8,128)(2,1)S(1)}, bf16[128,1024]{1,0:T(8,128)(2,1)S(1)}, u32[]{:S(2)}, u32[]{:S(2)}) collective-permute-start(bf16[128,1024]{1,0:T(8,128)(2,1)S(1)} %convert_element_type.338), channel_id=1, source_target_pairs={{0,16},{16,32},{32,48},{48,0},{1,17},{17,33},{33,49},{49,1},{2,18}... | collective-permute-start | bytes 786440 | tf_op jit(solution)/shard_map/ppermute | solution.py:23
  133.3 6.4 %collective-permute-start.30 = (bf16[64,1024]{1,0:T(8,128)(2,1)S(1)}, bf16[64,1024]{1,0:T(8,128)(2,1)S(1)}, u32[]{:S(2)}, u32[]{:S(2)}) collective-permute-start(bf16[64,1024]{1,0:T(8,128)(2,1)S(1)} %slice.164), channel_id=1, source_target_pairs={{0,16},{16,32},{32,48},{48,0},{1,17},{17,33},{33,49},{49,1},{2,18}... | collective-permute-start | bytes 393224 | tf_op jit(solution)/shard_map/ppermute | solution.py:23
  133.7 6.0 %collective-permute-start.29 = (bf16[64,1024]{1,0:T(8,128)(2,1)S(1)}, bf16[64,1024]{1,0:T(8,128)(2,1)S(1)}, u32[]{:S(2)}, u32[]{:S(2)}) collective-permute-start(bf16[64,1024]{1,0:T(8,128)(2,1)S(1)} %slice.163), channel_id=1, source_target_pairs={{0,192},{64,0},{128,64},{192,128},{1,193},{65,1},{129,65},{193,129... | collective-permute-start | bytes 393224 | tf_op jit(solution)/shard_map/ppermute | solution.py:23
  135.1 8.3 %collective-permute-start.28 = (bf16[64,1024]{1,0:T(8,128)(2,1)S(1)}, bf16[64,1024]{1,0:T(8,128)(2,1)S(1)}, u32[]{:S(2)}, u32[]{:S(2)}) collective-permute-start(bf16[64,1024]{1,0:T(8,128)(2,1)S(1)} %slice.162), channel_id=1, source_target_pairs={{0,64},{64,128},{128,192},{192,0},{1,65},{65,129},{129,193},{193,1... | collective-permute-start | bytes 393224 | tf_op jit(solution)/shard_map/ppermute | solution.py:23
  136.7 6.7 %collective-permute-start.31 = (bf16[64,1024]{1,0:T(8,128)(2,1)S(1)}, bf16[64,1024]{1,0:T(8,128)(2,1)S(1)}, u32[]{:S(2)}, u32[]{:S(2)}) collective-permute-start(bf16[64,1024]{1,0:T(8,128)(2,1)S(1)} %slice.165), channel_id=1, source_target_pairs={{0,48},{16,0},{32,16},{48,32},{1,49},{17,1},{33,17},{49,33},{2,50}... | collective-permute-start | bytes 393224 | tf_op jit(solution)/shard_map/ppermute | solution.py:23
  143.5 3.0 %collective-permute-start.32 = (bf16[512,1024]{1,0:T(8,128)(2,1)S(1)}, bf16[512,1024]{1,0:T(8,128)(2,1)S(1)}, u32[]{:S(2)}, u32[]{:S(2)}) collective-permute-start(bf16[512,1024]{1,0:T(8,128)(2,1)S(1)} %constant_dynamic-update-slice_fusion.5.right_ref), channel_id=1, source_target_pairs={{0,8},{8,0},{1,9},{9,1},{2,10},{10,2},{3,11},{11,3},{4,12},{12,4},... | collective-permute-start | bytes 3145736 | tf_op jit(solution)/shard_map/ppermute | solution.py:23
  149.0 19.5 %all-to-all-start = ((bf16[8,2,128,256]{3,2,1,0:T(8,128)(2,1)}), bf16[8,2,128,256]{3,2,1,0:T(8,128)(2,1)S(1)}, u32[]{:S(2)}, u32[]{:S(2)}) async-start(bf16[8,2,128,256]{3,2,1,0:T(8,128)(2,1)} %gram_tile.3), calls=%async_computation | async-start | bytes 2097152 | tf_op jit(solution)/shard_map/all_to_all | solution.py:278
  168.6 6.5 %collective-permute-start.33 = (bf16[128,256]{1,0:T(8,128)(2,1)S(1)}, bf16[128,256]{1,0:T(8,128)(2,1)S(1)}, u32[]{:S(2)}, u32[]{:S(2)}) collective-permute-start(bf16[128,256]{1,0:T(8,128)(2,1)S(1)} %get-tuple-element.69), channel_id=1, source_target_pairs={{0,32},{1,48},{2,34},{3,50},{16,0},{17,16},{18,2},{19,18},{32,33},... | collective-permute-start | bytes 196616 | tf_op jit(solution)/shard_map/ppermute | solution.py:287
  172.1 8.6 %collective-permute-start.34 = (bf16[128,256]{1,0:T(8,128)(2,1)S(1)}, bf16[128,256]{1,0:T(8,128)(2,1)S(1)}, u32[]{:S(2)}, u32[]{:S(2)}) collective-permute-start(bf16[128,256]{1,0:T(8,128)(2,1)S(1)} %get-tuple-element.70), channel_id=1, source_target_pairs={{0,0},{1,16},{2,2},{3,18},{16,32},{17,48},{18,34},{19,50},{32,1},{... | collective-permute-start | bytes 196616 | tf_op jit(solution)/shard_map/ppermute | solution.py:287
